TPU v7x, 32 devices: a whole 2x2x4 slice. The times are simulated.
32 devices in a mesh: seq: 8 (over y, x, core), head: 4 (over z).
Axes of the slice: x: 2, y: 2, z: 4, core: 2. Of those that a mesh axis runs over, the one named last changes fastest.
Arguments:
- tokens: bfloat16 [4096, 2048], P(('seq', 'head')), may hold values from -6 to 6
- cotangent: bfloat16 [4096, 2048], P(('seq', 'head')), may hold values from -6 to 6
- doc_lengths: int32 [3], replicated, may hold values from 1 to 3840, as said below
- q_weight: bfloat16 [2048, 2048], P('seq', 'head'), may hold values from -0.125 to 0.125
- k_weight: bfloat16 [2048, 2048], P('seq', 'head'), may hold values from -0.125 to 0.125
- v_weight: bfloat16 [2048, 2048], P('seq', 'head'), may hold values from -0.125 to 0.125
- o_weight: bfloat16 [2048, 2048], P('head', 'seq'), may hold values from -0.125 to 0.125
- gate_weight: bfloat16 [2048, 8192], P('seq', 'head'), may hold values from -0.125 to 0.125
- up_weight: bfloat16 [2048, 8192], P('seq', 'head'), may hold values from -0.125 to 0.125
- down_weight: bfloat16 [8192, 2048], P('head', 'seq'), may hold values from -0.0625 to 0.0625
- q_gain: float32 [2048], replicated, may hold values from 0.25 to 1.75
- k_gain: float32 [2048], replicated, may hold values from 0.25 to 1.75
- attn_gain: float32 [2048], replicated, may hold values from 0.25 to 1.75
- mlp_gain: float32 [2048], replicated, may hold values from 0.25 to 1.75
Outputs:
- output: bfloat16 [4096, 2048], P(('seq', 'head'))
- input_grad: float32 [4096, 2048], P(('seq', 'head'))
- q_weight_grad: float32 [2048, 2048], P('seq', 'head')
- k_weight_grad: float32 [2048, 2048], P('seq', 'head')
- v_weight_grad: float32 [2048, 2048], P('seq', 'head')
- o_weight_grad: float32 [2048, 2048], P('head', 'seq')
- gate_weight_grad: float32 [2048, 8192], P('seq', 'head')
- up_weight_grad: float32 [2048, 8192], P('seq', 'head')
- down_weight_grad: float32 [8192, 2048], P('head', 'seq')
- q_gain_grad: float32 [2048], P('seq')
- k_gain_grad: float32 [2048], P('seq')
- attn_gain_grad: float32 [2048], P('seq')
- mlp_gain_grad: float32 [2048], P('seq')
Inputs may be any that keep to these rules, and one draw needn't show every extreme that they name: `doc_lengths`: three documents packed in order fill the row; the longest has exactly 3840 tokens.
All inputs are finite; a program needn't handle non-finite values.
Results may differ from a plain program's by a relative error of at most 0.025.
Values may be sent and summed in bfloat16 or wider, within the bound.
A program may use at most 192 MiB of HBM per device.

v0:
```python
import jax
import jax.numpy as jnp
from jax import lax
from jax.sharding import PartitionSpec as P

D = 2048
HEAD_DIM = 128
KEY_BLOCK = 1024


epsilon = 1e-06
rope_base = 500000.0


def rms_norm(vector):
    return vector * lax.rsqrt(jnp.mean(vector * vector, axis=-1, keepdims=True) + epsilon)


def norm_grad(normed_rows, raw_rows, upstream, gain):
    row_scale = lax.rsqrt(jnp.mean(raw_rows * raw_rows, axis=-1, keepdims=True) + epsilon)
    grad_normed = upstream * gain
    inner_sum = jnp.mean(grad_normed * normed_rows, axis=-1, keepdims=True)
    return (
        row_scale * (grad_normed - normed_rows * inner_sum),
        jnp.sum(upstream * normed_rows, axis=0),
    )


def rope_tables(positions):
    frequency = jnp.power(
        rope_base, -jnp.arange(HEAD_DIM // 2, dtype=jnp.float32) * (2.0 / HEAD_DIM)
    )
    angles = positions.astype(jnp.float32)[:, None] * frequency[None, :]
    return (jnp.cos(angles), jnp.sin(angles))


def rotate(head_rows, cosine_table, sine_table):
    half_dim = HEAD_DIM // 2
    first_half = head_rows[..., :half_dim]
    second_half = head_rows[..., half_dim:]
    cosine_rows = cosine_table[:, None, :]
    sine_rows = sine_table[:, None, :]
    return jnp.concatenate(
        [
            first_half * cosine_rows - second_half * sine_rows,
            second_half * cosine_rows + first_half * sine_rows,
        ],
        axis=-1,
    )


def unrotate(head_rows, cosine_table, sine_table):
    half_dim = HEAD_DIM // 2
    first_half = head_rows[..., :half_dim]
    second_half = head_rows[..., half_dim:]
    cosine_rows = cosine_table[:, None, :]
    sine_rows = sine_table[:, None, :]
    return jnp.concatenate(
        [
            first_half * cosine_rows + second_half * sine_rows,
            second_half * cosine_rows - first_half * sine_rows,
        ],
        axis=-1,
    )


def segments_of(doc_lengths, token_index):
    doc_ends = jnp.cumsum(doc_lengths)
    return jnp.sum((token_index[:, None] >= doc_ends[None, :]).astype(jnp.int32), axis=1)


def doc_layout(doc_lengths, first_row, row_count):
    token_index = first_row + jnp.arange(row_count, dtype=jnp.int32)
    doc_ends = jnp.cumsum(doc_lengths)
    doc_starts = doc_ends - doc_lengths
    segment = segments_of(doc_lengths, token_index)
    inside = (token_index[:, None] >= doc_starts[None, :]) & (
        token_index[:, None] < doc_ends[None, :]
    )
    positions = token_index - jnp.sum(jnp.where(inside, doc_starts[None, :], 0), axis=1)
    return (token_index, segment, positions)


def collect(w_query, w_key, w_value, w_out, w_gate, w_up, w_down):
    return (
        lax.all_gather(w_query, "seq", axis=0, tiled=True),
        lax.all_gather(w_key, "seq", axis=0, tiled=True),
        lax.all_gather(w_value, "seq", axis=0, tiled=True),
        lax.all_gather(w_out, "seq", axis=1, tiled=True),
        lax.all_gather(w_gate, "seq", axis=0, tiled=True),
        lax.all_gather(w_up, "seq", axis=0, tiled=True),
        lax.all_gather(w_down, "seq", axis=1, tiled=True),
    )


def place_gain(vector, head_index, total_width):
    return lax.dynamic_update_slice_in_dim(
        jnp.zeros((total_width,), jnp.float32), vector, head_index * vector.shape[0], 0
    )


def on_device(
    tokens,
    cotangent,
    doc_lengths,
    q_weight,
    k_weight,
    v_weight,
    o_weight,
    gate_weight,
    up_weight,
    down_weight,
    q_gain,
    k_gain,
    attn_gain,
    mlp_gain,
):
    local_width = q_weight.shape[1]
    local_heads = local_width // HEAD_DIM
    seq_index = lax.axis_index("seq")
    head_index = lax.axis_index("head")
    f32 = jnp.float32
    bf16 = jnp.bfloat16
    gathered = lax.all_gather(tokens, "head", axis=0, tiled=True)
    tok_local = gathered.shape[0]
    total_tokens = tok_local * lax.axis_size("seq")
    token_index, segment, positions = doc_layout(doc_lengths, seq_index * tok_local, tok_local)
    cosine_table, sine_table = rope_tables(positions)
    gain_query = lax.dynamic_slice_in_dim(q_gain, head_index * local_width, local_width)
    gain_key = lax.dynamic_slice_in_dim(k_gain, head_index * local_width, local_width)
    w_query, w_key, w_value, w_out, w_gate, w_up, w_down = collect(
        q_weight, k_weight, v_weight, o_weight, gate_weight, up_weight, down_weight
    )
    queries = jnp.dot(gathered, w_query, preferred_element_type=f32)
    key_pre = jnp.dot(gathered, w_key, preferred_element_type=f32)
    value_pre = jnp.dot(gathered, w_value, preferred_element_type=f32)
    q_total, k_total = lax.psum(
        (jnp.sum(queries * queries, axis=1), jnp.sum(key_pre * key_pre, axis=1)), "head"
    )
    q_scale = lax.rsqrt(q_total / D + epsilon)
    k_scale = lax.rsqrt(k_total / D + epsilon)
    q_hat = queries * q_scale[:, None]
    k_hat = key_pre * k_scale[:, None]
    q_rot = rotate(
        (q_hat * gain_query).reshape(tok_local, local_heads, HEAD_DIM), cosine_table, sine_table
    ).astype(bf16)
    k_rot = rotate(
        (k_hat * gain_key).reshape(tok_local, local_heads, HEAD_DIM), cosine_table, sine_table
    ).astype(bf16)
    key_all, value_all = (
        lax.all_gather(k_rot.reshape(tok_local, local_width), "seq", axis=0, tiled=True),
        lax.all_gather(value_pre.astype(bf16), "seq", axis=0, tiled=True),
    )
    score_scale = HEAD_DIM ** (-0.5)
    block_count = ((seq_index + 1) * tok_local + KEY_BLOCK - 1) // KEY_BLOCK

    def block_scores(block_id):
        begin_row = block_id * KEY_BLOCK
        key_slab = lax.dynamic_slice_in_dim(key_all, begin_row, KEY_BLOCK, 0).reshape(
            KEY_BLOCK, local_heads, HEAD_DIM
        )
        value_slab = lax.dynamic_slice_in_dim(value_all, begin_row, KEY_BLOCK, 0).reshape(
            KEY_BLOCK, local_heads, HEAD_DIM
        )
        scores = (
            jnp.einsum("qhd,khd->hqk", q_rot, key_slab, preferred_element_type=f32) * score_scale
        )
        key_index = begin_row + jnp.arange(KEY_BLOCK, dtype=jnp.int32)
        key_segment = segments_of(doc_lengths, key_index)
        allowed_mask = (key_index[None, :] <= token_index[:, None]) & (
            key_segment[None, :] == segment[:, None]
        )
        return (scores, allowed_mask, key_slab, value_slab)

    def stats_step(block_id, carry):
        row_top, row_total = carry
        scores, allowed_mask, key_slab, value_slab = block_scores(block_id)
        masked = jnp.where(allowed_mask[None], scores, -1e30)
        new_top = jnp.maximum(row_top, jnp.max(masked, axis=-1))
        terms = jnp.where(allowed_mask[None], jnp.exp(masked - new_top[:, :, None]), 0.0)
        return (new_top, row_total * jnp.exp(row_top - new_top) + jnp.sum(terms, axis=-1))

    row_top, row_total = lax.fori_loop(
        0,
        block_count,
        stats_step,
        (jnp.full((local_heads, tok_local), -1e30, f32), jnp.zeros((local_heads, tok_local), f32)),
    )
    log_total = row_top + jnp.log(row_total)

    def apply_step(block_id, summed):
        scores, allowed_mask, key_slab, value_slab = block_scores(block_id)
        attn_weights = jnp.where(
            allowed_mask[None], jnp.exp(scores - log_total[:, :, None]), 0.0
        ).astype(bf16)
        return summed + jnp.einsum(
            "hqk,khd->qhd", attn_weights, value_slab, preferred_element_type=f32
        )

    summed = lax.fori_loop(
        0, block_count, apply_step, jnp.zeros((tok_local, local_heads, HEAD_DIM), f32)
    )
    attended = summed.reshape(tok_local, local_width).astype(bf16)
    branch = lax.psum_scatter(
        jnp.dot(attended, w_out, preferred_element_type=f32).astype(jnp.bfloat16),
        "head",
        scatter_dimension=0,
        tiled=True,
    ).astype(jnp.float32)
    attn_normed = rms_norm(branch)
    hidden_in = tokens.astype(f32) + attn_normed * attn_gain
    mlp_gathered = lax.all_gather(hidden_in.astype(bf16), "head", axis=0, tiled=True)
    gate_pre = jnp.dot(mlp_gathered, w_gate, preferred_element_type=f32)
    up_pre = jnp.dot(mlp_gathered, w_up, preferred_element_type=f32)
    hidden = (jax.nn.silu(gate_pre) * up_pre).astype(bf16)
    second = lax.psum_scatter(
        jnp.dot(hidden, w_down, preferred_element_type=f32).astype(jnp.bfloat16),
        "head",
        scatter_dimension=0,
        tiled=True,
    ).astype(jnp.float32)
    mlp_normed = rms_norm(second)
    output = (hidden_in + mlp_normed * mlp_gain).astype(bf16)
    w_query, w_key, w_value, w_out, w_gate, w_up, w_down = collect(
        q_weight, k_weight, v_weight, o_weight, gate_weight, up_weight, down_weight
    )
    upstream = cotangent.astype(f32)
    d_second, mlp_gain_part = norm_grad(mlp_normed, second, upstream, mlp_gain)
    second_grads = lax.all_gather(d_second.astype(bf16), "head", axis=0, tiled=True)
    grad_down = jnp.einsum("tf,td->fd", hidden, second_grads, preferred_element_type=f32)
    d_hidden = jnp.einsum("td,fd->tf", second_grads, w_down, preferred_element_type=f32)
    sigmoid_gate = jax.nn.sigmoid(gate_pre)
    d_up = (d_hidden * gate_pre * sigmoid_gate).astype(bf16)
    d_gate = (d_hidden * up_pre * sigmoid_gate * (1.0 + gate_pre * (1.0 - sigmoid_gate))).astype(
        bf16
    )
    grad_gate = jnp.einsum("td,tf->df", mlp_gathered, d_gate, preferred_element_type=f32)
    grad_up = jnp.einsum("td,tf->df", mlp_gathered, d_up, preferred_element_type=f32)
    d_middle = upstream + lax.psum_scatter(
        (
            jnp.einsum("tf,df->td", d_gate, w_gate, preferred_element_type=f32)
            + jnp.einsum("tf,df->td", d_up, w_up, preferred_element_type=f32)
        ).astype(jnp.bfloat16),
        "head",
        scatter_dimension=0,
        tiled=True,
    ).astype(jnp.float32)
    d_branch, attn_gain_part = norm_grad(attn_normed, branch, d_middle, attn_gain)
    branch_grads = lax.all_gather(d_branch.astype(bf16), "head", axis=0, tiled=True)
    grad_out = jnp.einsum("tc,td->cd", attended, branch_grads, preferred_element_type=f32)
    d_attended = jnp.einsum("td,cd->tc", branch_grads, w_out, preferred_element_type=f32).astype(
        bf16
    )
    d_heads = d_attended.reshape(tok_local, local_heads, HEAD_DIM)
    delta_rows = jnp.transpose(jnp.sum(d_heads.astype(f32) * summed, axis=-1))

    def grad_step(block_id, carry):
        d_query, d_keys, d_values = carry
        scores, allowed_mask, key_slab, value_slab = block_scores(block_id)
        attn_weights = jnp.where(allowed_mask[None], jnp.exp(scores - log_total[:, :, None]), 0.0)
        weights_low = attn_weights.astype(bf16)
        d_weights = jnp.einsum("qhd,khd->hqk", d_heads, value_slab, preferred_element_type=f32)
        d_scores = (attn_weights * (d_weights - delta_rows[:, :, None])).astype(bf16)
        d_query = (
            d_query
            + jnp.einsum("hqk,khd->qhd", d_scores, key_slab, preferred_element_type=f32)
            * score_scale
        )
        key_part = (
            jnp.einsum("hqk,qhd->khd", d_scores, q_rot, preferred_element_type=f32) * score_scale
        ).reshape(KEY_BLOCK, local_width)
        value_part = jnp.einsum(
            "hqk,qhd->khd", weights_low, d_heads, preferred_element_type=f32
        ).reshape(KEY_BLOCK, local_width)
        begin_row = block_id * KEY_BLOCK
        d_keys = lax.dynamic_update_slice_in_dim(d_keys, key_part, begin_row, 0)
        d_values = lax.dynamic_update_slice_in_dim(d_values, value_part, begin_row, 0)
        return (d_query, d_keys, d_values)

    d_query, d_keys, d_values = lax.fori_loop(
        0,
        block_count,
        grad_step,
        (
            jnp.zeros((tok_local, local_heads, HEAD_DIM), f32),
            jnp.zeros((total_tokens, local_width), f32),
            jnp.zeros((total_tokens, local_width), f32),
        ),
    )
    key_grads, value_grads = (
        lax.psum_scatter(
            d_keys.astype(jnp.bfloat16), "seq", scatter_dimension=0, tiled=True
        ).astype(jnp.float32),
        lax.psum_scatter(
            d_values.astype(jnp.bfloat16), "seq", scatter_dimension=0, tiled=True
        ).astype(jnp.float32),
    )
    d_qnorm = unrotate(d_query, cosine_table, sine_table).reshape(tok_local, local_width)
    d_knorm = unrotate(
        key_grads.reshape(tok_local, local_heads, HEAD_DIM), cosine_table, sine_table
    ).reshape(tok_local, local_width)
    q_gain_part = jnp.sum(d_qnorm * q_hat, axis=0)
    k_gain_part = jnp.sum(d_knorm * k_hat, axis=0)
    d_qhat = d_qnorm * gain_query
    d_khat = d_knorm * gain_key
    q_inner, k_inner, q_gain_full, k_gain_full, attn_gain_full, mlp_gain_full = (
        lax.psum(jnp.sum(d_qhat * q_hat, axis=1).astype(jnp.bfloat16), "head").astype(jnp.float32),
        lax.psum(jnp.sum(d_khat * k_hat, axis=1).astype(jnp.bfloat16), "head").astype(jnp.float32),
        lax.psum(place_gain(q_gain_part, head_index, D).astype(jnp.bfloat16), "head").astype(
            jnp.float32
        ),
        lax.psum(place_gain(k_gain_part, head_index, D).astype(jnp.bfloat16), "head").astype(
            jnp.float32
        ),
        lax.psum(attn_gain_part.astype(jnp.bfloat16), "head").astype(jnp.float32),
        lax.psum(mlp_gain_part.astype(jnp.bfloat16), "head").astype(jnp.float32),
    )
    d_q = (q_scale[:, None] * (d_qhat - q_hat * (q_inner / D)[:, None])).astype(bf16)
    d_k = (k_scale[:, None] * (d_khat - k_hat * (k_inner / D)[:, None])).astype(bf16)
    d_v = value_grads.astype(bf16)
    grad_query = jnp.einsum("td,tc->dc", gathered, d_q, preferred_element_type=f32)
    grad_key = jnp.einsum("td,tc->dc", gathered, d_k, preferred_element_type=f32)
    grad_value = jnp.einsum("td,tc->dc", gathered, d_v, preferred_element_type=f32)
    input_grad = d_middle + lax.psum_scatter(
        (
            jnp.einsum("tc,dc->td", d_q, w_query, preferred_element_type=f32)
            + jnp.einsum("tc,dc->td", d_k, w_key, preferred_element_type=f32)
            + jnp.einsum("tc,dc->td", d_v, w_value, preferred_element_type=f32)
        ).astype(jnp.bfloat16),
        "head",
        scatter_dimension=0,
        tiled=True,
    ).astype(jnp.float32)
    reduced = (
        lax.psum_scatter(
            grad_query.astype(jnp.bfloat16), "seq", scatter_dimension=0, tiled=True
        ).astype(jnp.float32),
        lax.psum_scatter(
            grad_key.astype(jnp.bfloat16), "seq", scatter_dimension=0, tiled=True
        ).astype(jnp.float32),
        lax.psum_scatter(
            grad_value.astype(jnp.bfloat16), "seq", scatter_dimension=0, tiled=True
        ).astype(jnp.float32),
        lax.psum_scatter(
            grad_out.astype(jnp.bfloat16), "seq", scatter_dimension=1, tiled=True
        ).astype(jnp.float32),
        lax.psum_scatter(
            grad_gate.astype(jnp.bfloat16), "seq", scatter_dimension=0, tiled=True
        ).astype(jnp.float32),
        lax.psum_scatter(
            grad_up.astype(jnp.bfloat16), "seq", scatter_dimension=0, tiled=True
        ).astype(jnp.float32),
        lax.psum_scatter(
            grad_down.astype(jnp.bfloat16), "seq", scatter_dimension=1, tiled=True
        ).astype(jnp.float32),
        lax.psum_scatter(
            q_gain_full.astype(jnp.bfloat16), "seq", scatter_dimension=0, tiled=True
        ).astype(jnp.float32),
        lax.psum_scatter(
            k_gain_full.astype(jnp.bfloat16), "seq", scatter_dimension=0, tiled=True
        ).astype(jnp.float32),
        lax.psum_scatter(
            attn_gain_full.astype(jnp.bfloat16), "seq", scatter_dimension=0, tiled=True
        ).astype(jnp.float32),
        lax.psum_scatter(
            mlp_gain_full.astype(jnp.bfloat16), "seq", scatter_dimension=0, tiled=True
        ).astype(jnp.float32),
    )
    return (
        output,
        input_grad,
        reduced[0],
        reduced[1],
        reduced[2],
        reduced[3],
        reduced[4],
        reduced[5],
        reduced[6],
        reduced[7],
        reduced[8],
        reduced[9],
        reduced[10],
    )


def solution(mesh):
    in_specs = (
        P(("seq", "head"), None),
        P(("seq", "head"), None),
        P(),
        P("seq", "head"),
        P("seq", "head"),
        P("seq", "head"),
        P("head", "seq"),
        P("seq", "head"),
        P("seq", "head"),
        P("head", "seq"),
        P(),
        P(),
        P(),
        P(),
    )
    out_specs = (
        P(("seq", "head"), None),
        P(("seq", "head"), None),
        P("seq", "head"),
        P("seq", "head"),
        P("seq", "head"),
        P("head", "seq"),
        P("seq", "head"),
        P("seq", "head"),
        P("head", "seq"),
        P("seq"),
        P("seq"),
        P("seq"),
        P("seq"),
    )
    return jax.shard_map(
        on_device, mesh=mesh, in_specs=in_specs, out_specs=out_specs, check_vma=False
    )
```

profile of v0, /device:TPU:8, one launch (start us, length us, event | category | flops | bytes accessed | tf_op | source)
XLA Modules:
  0.0 1386.6 jit_solution(17100924299550583849)
XLA Ops:
  13.7 41.4 %all-gather.14.cloned.1.call-done = bf16[512,2048]{1,0:T(8,128)(2,1)} async-done(((bf16[128,2048]{1,0:T(8,128)(2,1)}), bf16[512,2048]{1,0:T(8,128)(2,1)}) %all-gather.14.cloned.1.call-update) | async-done | bytes 2097168 | tf_op jit(solution)/shard_map/all_gather | solution.py:124
  55.1 30.1 %all-gather.20.cloned.1.call-done = bf16[2048,512]{1,0:T(8,128)(2,1)} async-done(((bf16[256,512]{1,0:T(8,128)(2,1)}), bf16[2048,512]{1,0:T(8,128)(2,1)}) %all-gather.20.cloned.1.call-update) | async-done | bytes 2097168 | tf_op jit(solution)/shard_map/all_gather | solution.py:87
  88.8 26.3 %all-gather.24.cloned.1.call-done = bf16[2048,512]{1,0:T(8,128)(2,1)} async-done(((bf16[256,512]{1,0:T(8,128)(2,1)}), bf16[2048,512]{1,0:T(8,128)(2,1)}) %all-gather.24.cloned.1.call-update) | async-done | bytes 2097168 | tf_op jit(solution)/shard_map/all_gather | solution.py:86
  118.6 8.9 all-reduce.4
  129.2 15.5 %all-gather.16.cloned.1.call-done = bf16[2048,512]{1,0:T(8,128)(2,1)} async-done(((bf16[256,512]{1,0:T(8,128)(2,1)}), bf16[2048,512]{1,0:T(8,128)(2,1)}) %all-gather.16.cloned.1.call-update) | async-done | bytes 2097168 | tf_op jit(solution)/shard_map/all_gather | solution.py:88
  144.7 4.3 convolution_convert_fusion.10
  150.3 34.2 %all-gather.22.cloned.1.call-done = bf16[4096,512]{0,1:T(8,128)(2,1)} async-done(((bf16[512,512]{0,1:T(8,128)(2,1)}), bf16[4096,512]{0,1:T(8,128)(2,1)}) %all-gather.22.cloned.1.call-update) | async-done | bytes 4194320 | tf_op jit(solution)/shard_map/all_gather | solution.py:151
  184.5 6.2 while.45
  190.7 32.8 %all-gather.18.cloned.1.call-done = bf16[4096,512]{1,0:T(8,128)(2,1)} async-done(((bf16[512,512]{1,0:T(8,128)(2,1)}), bf16[4096,512]{1,0:T(8,128)(2,1)}) %all-gather.18.cloned.1.call-update) | async-done | bytes 4194320 | tf_op jit(solution)/shard_map/all_gather | solution.py:152
  223.6 6.4 copy.101
  231.1 8.6 while.46
  234.7 5.0 fusion.151
  241.0 12.7 all-gather.26.cloned.1.call-done
  253.7 4.2 convolution_convert_fusion.8
  258.8 53.3 %reduce-scatter.14.cloned.1.call-done = bf16[128,2048]{1,0:T(8,128)(2,1)} async-done(((bf16[512,2048]{1,0:T(8,128)(2,1)}), bf16[128,2048]{1,0:T(8,128)(2,1)}) %reduce-scatter.14.cloned.1.call-update) | async-done | bytes 524304 | tf_op jit(solution)/shard_map/reduce_scatter | solution.py:204
  316.8 53.3 %all-gather.30.cloned.1.call-done = bf16[2048,2048]{1,0:T(8,128)(2,1)} async-done(((bf16[256,2048]{1,0:T(8,128)(2,1)}), bf16[2048,2048]{1,0:T(8,128)(2,1)}) %all-gather.30.cloned.1.call-update) | async-done | bytes 8388624 | tf_op jit(solution)/shard_map/all_gather | solution.py:90
  370.1 46.4 %all-gather.28.cloned.1.call-done = bf16[512,2048]{1,0:T(8,128)(2,1)} async-done(((bf16[128,2048]{1,0:T(8,128)(2,1)}), bf16[512,2048]{1,0:T(8,128)(2,1)}) %all-gather.28.cloned.1.call-update) | async-done | bytes 2097168 | tf_op jit(solution)/shard_map/all_gather | solution.py:212
  416.5 10.6 fusion.62
  427.1 46.2 %all-gather.32.cloned.1.call-done = bf16[2048,2048]{1,0:T(8,128)(2,1)} async-done(((bf16[256,2048]{1,0:T(8,128)(2,1)}), bf16[2048,2048]{1,0:T(8,128)(2,1)}) %all-gather.32.cloned.1.call-update) | async-done | bytes 8388624 | tf_op jit(solution)/shard_map/all_gather | solution.py:91
  473.3 12.5 multiply_convert_fusion.2
  485.8 45.4 %all-gather.34.cloned.1.call-done = bf16[2048,2048]{1,0:T(8,128)(2,1)} async-done(((bf16[2048,256]{1,0:T(8,128)(2,1)}), bf16[2048,2048]{1,0:T(8,128)(2,1)}) %all-gather.34.cloned.1.call-update) | async-done | bytes 8388624 | tf_op jit(solution)/shard_map/all_gather | solution.py:92
  531.2 9.9 convolution_convert_fusion.7
  541.2 41.7 %reduce-scatter.16.cloned.1.call-done = bf16[128,2048]{1,0:T(8,128)(2,1)} async-done(((bf16[512,2048]{1,0:T(8,128)(2,1)}), bf16[128,2048]{1,0:T(8,128)(2,1)}) %reduce-scatter.16.cloned.1.call-update) | async-done | bytes 524304 | tf_op jit(solution)/shard_map/reduce_scatter | solution.py:216
  588.9 45.6 %all-gather.36.cloned.1.call-done = bf16[512,2048]{1,0:T(8,128)(2,1)} async-done(((bf16[128,2048]{1,0:T(8,128)(2,1)}), bf16[512,2048]{1,0:T(8,128)(2,1)}) %all-gather.36.cloned.1.call-update) | async-done | bytes 2097168 | tf_op jit(solution)/shard_map/all_gather | solution.py:229
  634.5 11.9 multiply_convert_fusion
  646.4 8.5 fusion.63
  654.9 9.3 add_convert_fusion.1
  664.3 42.0 %reduce-scatter.18.cloned.1.call-done = bf16[128,2048]{1,0:T(8,128)(2,1)} async-done(((bf16[512,2048]{1,0:T(8,128)(2,1)}), bf16[128,2048]{1,0:T(8,128)(2,1)}) %reduce-scatter.18.cloned.1.call-update) | async-done | bytes 524304 | tf_op jit(solution)/shard_map/reduce_scatter | solution.py:239
  710.7 45.9 %all-gather.38.cloned.1.call-done = bf16[512,2048]{1,0:T(8,128)(2,1)} async-done(((bf16[128,2048]{1,0:T(8,128)(2,1)}), bf16[512,2048]{1,0:T(8,128)(2,1)}) %all-gather.38.cloned.1.call-update) | async-done | bytes 2097168 | tf_op jit(solution)/shard_map/all_gather | solution.py:249
  765.6 14.4 %while.47 = (s32[]{:T(128)}, f32[512,4,128]{0,2,1:T(8,128)S(1)}, bf16[4096,512]{0,1:T(8,128)(2,1)}, bf16[4096,512]{0,1:T(8,128)(2,1)}, s32[]{:T(128)}, /*index=5...) while((s32[]{:T(128)}, f32[512,4,128]{0,2,1:T(8,128)S(1)}, ...), condition=%wide.region_26.27_spmd.clone, body=%wide.region_24.26_spmd.clone.sunk | while | flops 2708481536 | bytes 57198836 | solution.py:280
  785.5 10.1 convolution_convert_fusion
  795.6 10.0 convolution_convert_fusion.2
  805.9 10.1 convolution_convert_fusion.1
  817.9 56.9 %reduce-scatter.20.cloned.1.call-done = bf16[512,512]{0,1:T(8,128)(2,1)} async-done(((bf16[4096,512]{0,1:T(8,128)(2,1)}), bf16[512,512]{0,1:T(8,128)(2,1)}) %reduce-scatter.20.cloned.1.call-update) | async-done | bytes 524304 | tf_op jit(solution)/shard_map/reduce_scatter | solution.py:291
  880.3 23.2 %all-reduce.5 = (bf16[2048]{0:T(1024)(128)(2,1)S(1)}, bf16[2048]{0:T(1024)(128)(2,1)S(1)}, bf16[2048]{0:T(1024)(128)(2,1)S(1)}, bf16[2048]{0:T(1024)(128)(2,1)S(1)}) all-reduce(bf16[2048]{0:T(1024)(128)(2,1)S(1)} %dynamic_update_slice.16, ...), channel_id=15, replica_groups=mesh['seq'=8,'head'=4] {'seq'}, use_global_device_ids=true, to_apply=%region_43.44.clone | all-reduce | flops 8192 | bytes 32768
  903.8 8.9 all-reduce.6
  914.2 4.4 fusion.34
  918.9 4.2 fusion.33
  923.2 6.1 reduce-scatter.22.cloned.1.call-done
  929.3 4.3 fusion.35
  939.9 34.9 %reduce-scatter.32.cloned.1.call-done = bf16[512,256]{1,0:T(8,128)(2,1)} async-done(((bf16[512,2048]{1,0:T(8,128)(2,1)}), bf16[512,256]{1,0:T(8,128)(2,1)}) %reduce-scatter.32.cloned.1.call-update) | async-done | bytes 262160 | tf_op jit(solution)/shard_map/reduce_scatter | solution.py:344
  976.6 72.8 %reduce-scatter.38.cloned.1.call-done = bf16[2048,256]{1,0:T(8,128)(2,1)} async-done(((bf16[2048,2048]{1,0:T(8,128)(2,1)}), bf16[2048,256]{1,0:T(8,128)(2,1)}) %reduce-scatter.38.cloned.1.call-update) | async-done | bytes 1048592 | tf_op jit(solution)/shard_map/reduce_scatter | solution.py:353
  1052.1 72.5 %reduce-scatter.34.cloned.1.call-done = bf16[256,2048]{1,0:T(8,128)(2,1)} async-done(((bf16[2048,2048]{1,0:T(8,128)(2,1)}), bf16[256,2048]{1,0:T(8,128)(2,1)}) %reduce-scatter.34.cloned.1.call-update) | async-done | bytes 1048592 | tf_op jit(solution)/shard_map/reduce_scatter | solution.py:347
  1127.4 72.0 %reduce-scatter.36.cloned.1.call-done = bf16[256,2048]{1,0:T(8,128)(2,1)} async-done(((bf16[2048,2048]{1,0:T(8,128)(2,1)}), bf16[256,2048]{1,0:T(8,128)(2,1)}) %reduce-scatter.36.cloned.1.call-update) | async-done | bytes 1048592 | tf_op jit(solution)/shard_map/reduce_scatter | solution.py:350
  1204.4 39.8 %reduce-scatter.28.cloned.1.call-done = bf16[256,512]{0,1:T(8,128)(2,1)} async-done(((bf16[2048,512]{0,1:T(8,128)(2,1)}), bf16[256,512]{0,1:T(8,128)(2,1)}) %reduce-scatter.28.cloned.1.call-update) | async-done | bytes 262160 | tf_op jit(solution)/shard_map/reduce_scatter | solution.py:338
  1246.1 42.5 %reduce-scatter.26.cloned.1.call-done = bf16[256,512]{0,1:T(8,128)(2,1)} async-done(((bf16[2048,512]{0,1:T(8,128)(2,1)}), bf16[256,512]{0,1:T(8,128)(2,1)}) %reduce-scatter.26.cloned.1.call-update) | async-done | bytes 262160 | tf_op jit(solution)/shard_map/reduce_scatter | solution.py:335
  1290.5 43.0 %reduce-scatter.30.cloned.1.call-done = bf16[256,512]{0,1:T(8,128)(2,1)} async-done(((bf16[2048,512]{0,1:T(8,128)(2,1)}), bf16[256,512]{0,1:T(8,128)(2,1)}) %reduce-scatter.30.cloned.1.call-update) | async-done | bytes 262160 | tf_op jit(solution)/shard_map/reduce_scatter | solution.py:341
  1335.4 41.9 %reduce-scatter.24.cloned.1.call-done = bf16[128,2048]{1,0:T(8,128)(2,1)} async-done(((bf16[512,2048]{1,0:T(8,128)(2,1)}), bf16[128,2048]{1,0:T(8,128)(2,1)}) %reduce-scatter.24.cloned.1.call-update) | async-done | bytes 524304 | tf_op jit(solution)/shard_map/reduce_scatter | solution.py:324
  (231 shorter events, 108.6 us)
Async XLA Ops:
  7.2 47.9 %all-gather.14.cloned.1.call-start = ((), (), s32[]{:S(2)}) async-start(), calls=%async_computation.13 | async-start | bytes 2621440 | tf_op jit(solution)/shard_map/all_gather | solution.py:124
  7.9 77.3 %all-gather.20.cloned.1.call-start = ((), (), s32[]{:S(2)}) async-start(), calls=%async_computation.16 | async-start | bytes 2359296 | tf_op jit(solution)/shard_map/all_gather | solution.py:87
  8.7 106.4 %all-gather.24.cloned.1.call-start = ((), (), s32[]{:S(2)}) async-start(), calls=%async_computation.18 | async-start | bytes 2359296 | tf_op jit(solution)/shard_map/all_gather | solution.py:86
  9.4 135.3 %all-gather.16.cloned.1.call-start = ((), (), s32[]{:S(2)}) async-start(), calls=%async_computation.14 | async-start | bytes 2359296 | tf_op jit(solution)/shard_map/all_gather | solution.py:88
  10.0 174.5 %all-gather.22.cloned.1.call-start = ((), (), s32[]{:S(2)}) async-start(), calls=%async_computation.17 | async-start | bytes 4718592 | tf_op jit(solution)/shard_map/all_gather | solution.py:151
  10.8 116.8 %copy-start.28 = (f32[512]{0:T(512)}, f32[512]{0:T(512)S(1)}, u32[]{:S(2)}) copy-start(f32[512]{0:T(512)S(1)} %dynamic_slice.31) | copy-start | bytes 6148
  11.6 116.2 %copy-start.26 = (f32[512]{0:T(512)}, f32[512]{0:T(512)S(1)}, u32[]{:S(2)}) copy-start(f32[512]{0:T(512)S(1)} %dynamic_slice.32) | copy-start | bytes 6148
  13.7 114.2 %copy-start.17 = (f32[512,64]{0,1:T(8,128)}, f32[512,64]{0,1:T(8,128)S(1)}, u32[]{:S(2)}) copy-start(f32[512,64]{0,1:T(8,128)S(1)} %get-tuple-element.816) | copy-start | bytes 393220
  13.7 114.2 %copy-start.19 = (f32[512,64]{0,1:T(8,128)}, f32[512,64]{0,1:T(8,128)S(1)}, u32[]{:S(2)}) copy-start(f32[512,64]{0,1:T(8,128)S(1)} %get-tuple-element.817) | copy-start | bytes 393220
  88.8 38.8 %copy-start.4 = (f32[512,512]{0,1:T(8,128)}, f32[512,512]{0,1:T(8,128)S(1)}, u32[]{:S(2)}) copy-start(f32[512,512]{0,1:T(8,128)S(1)} %get-tuple-element.819) | copy-start | bytes 3145732
  118.6 10.5 copy-start.2
  129.1 20.7 %copy-start.35 = (s32[3]{0:T(128)S(1)}, s32[3]{0:T(128)}, u32[]{:S(2)}) copy-start(s32[3]{0:T(128)} %param.22) | copy-start | bytes 40
  129.1 94.4 %all-gather.18.cloned.1.call-start = ((), (), s32[]{:S(2)}) async-start(), calls=%async_computation.15 | async-start | bytes 4718592 | tf_op jit(solution)/shard_map/all_gather | solution.py:152
  149.0 104.7 %all-gather.26.cloned.1.call-start = ((), (), s32[]{:S(2)}) async-start(), calls=%async_computation.19 | async-start | bytes 2359296 | tf_op jit(solution)/shard_map/all_gather | solution.py:89
  149.8 162.2 %reduce-scatter.14.cloned.1.call-start = ((), (), s32[]{:S(2)}) async-start(), calls=%async_computation.20 | async-start | bytes 2621440 | tf_op jit(solution)/shard_map/reduce_scatter | solution.py:204
  241.0 17.8 %copy-start.21 = (bf16[512,4,128]{0,2,1:T(8,128)(2,1)}, bf16[512,4,128]{0,2,1:T(8,128)(2,1)S(1)}, u32[]{:S(2)}) copy-start(bf16[512,4,128]{0,2,1:T(8,128)(2,1)S(1)} %convert_element_type.227) | copy-start | bytes 1572868
  253.7 59.6 %copy-start.11 = (bf16[128,2048]{1,0:T(8,128)(2,1)S(1)}, bf16[128,2048]{1,0:T(8,128)(2,1)}, u32[]{:S(2)}) copy-start(bf16[128,2048]{1,0:T(8,128)(2,1)} %param.20) | copy-start | bytes 1572868
  253.7 59.6 %copy-start.24 = (f32[2048]{0:T(1024)S(1)}, f32[2048]{0:T(1024)}, u32[]{:S(2)}) copy-start(f32[2048]{0:T(1024)} %param.32) | copy-start | bytes 24580
  258.0 112.1 %all-gather.30.cloned.1.call-start = ((), (), s32[]{:S(2)}) async-start(), calls=%async_computation.22 | async-start | bytes 9437184 | tf_op jit(solution)/shard_map/all_gather | solution.py:90
  258.7 157.8 %all-gather.28.cloned.1.call-start = ((), (), s32[]{:S(2)}) async-start(), calls=%async_computation.21 | async-start | bytes 2621440 | tf_op jit(solution)/shard_map/all_gather | solution.py:212
  315.4 157.9 %all-gather.32.cloned.1.call-start = ((), (), s32[]{:S(2)}) async-start(), calls=%async_computation.23 | async-start | bytes 9437184 | tf_op jit(solution)/shard_map/all_gather | solution.py:91
  316.1 215.1 %all-gather.34.cloned.1.call-start = ((), (), s32[]{:S(2)}) async-start(), calls=%async_computation.24 | async-start | bytes 9437184 | tf_op jit(solution)/shard_map/all_gather | solution.py:92
  316.7 266.2 %reduce-scatter.16.cloned.1.call-start = ((), (), s32[]{:S(2)}) async-start(), calls=%async_computation.25 | async-start | bytes 2621440 | tf_op jit(solution)/shard_map/reduce_scatter | solution.py:216
  531.2 52.9 %copy-start = (bf16[128,2048]{1,0:T(8,128)(2,1)S(1)}, bf16[128,2048]{1,0:T(8,128)(2,1)}, u32[]{:S(2)}) copy-start(bf16[128,2048]{1,0:T(8,128)(2,1)} %param.21) | copy-start | bytes 1572868
  531.2 52.9 %copy-start.25 = (f32[2048]{0:T(1024)S(1)}, f32[2048]{0:T(1024)}, u32[]{:S(2)}) copy-start(f32[2048]{0:T(1024)} %param.33) | copy-start | bytes 24580
  541.1 93.4 %all-gather.36.cloned.1.call-start = ((), (), s32[]{:S(2)}) async-start(), calls=%async_computation.26 | async-start | bytes 2621440 | tf_op jit(solution)/shard_map/all_gather | solution.py:229
  588.4 117.9 %reduce-scatter.18.cloned.1.call-start = ((), (), s32[]{:S(2)}) async-start(), calls=%async_computation.27 | async-start | bytes 2621440 | tf_op jit(solution)/shard_map/reduce_scatter | solution.py:239
  654.9 51.4 %copy-start.9 = (bf16[128,2048]{1,0:T(8,128)(2,1)S(1)}, bf16[128,2048]{1,0:T(8,128)(2,1)}, u32[]{:S(2)}) copy-start(bf16[128,2048]{1,0:T(8,128)(2,1)} %reduce-scatter.14.cloned.1.call-done) | copy-start | bytes 1572868
  654.9 52.9 %copy-start.10 = (bf16[128,2048]{1,0:T(8,128)(2,1)S(1)}, bf16[128,2048]{1,0:T(8,128)(2,1)}, u32[]{:S(2)}) copy-start(bf16[128,2048]{1,0:T(8,128)(2,1)} %reduce-scatter.16.cloned.1.call-done) | copy-start | bytes 1572868
  664.2 92.4 %all-gather.38.cloned.1.call-start = ((), (), s32[]{:S(2)}) async-start(), calls=%async_computation.28 | async-start | bytes 2621440 | tf_op jit(solution)/shard_map/all_gather | solution.py:249
  710.5 164.3 %reduce-scatter.20.cloned.1.call-start = ((), (), s32[]{:S(2)}) async-start(), calls=%async_computation.29 | async-start | bytes 4718592 | tf_op jit(solution)/shard_map/reduce_scatter | solution.py:291
  780.0 149.3 %reduce-scatter.22.cloned.1.call-start = ((), (), s32[]{:S(2)}) async-start(), calls=%async_computation.30 | async-start | bytes 4718592 | tf_op jit(solution)/shard_map/reduce_scatter | solution.py:294
  780.6 194.2 %reduce-scatter.32.cloned.1.call-start = ((), (), s32[]{:S(2)}) async-start(), calls=%async_computation.35 | async-start | bytes 2359296 | tf_op jit(solution)/shard_map/reduce_scatter | solution.py:344
  785.2 264.2 %reduce-scatter.38.cloned.1.call-start = ((), (), s32[]{:S(2)}) async-start(), calls=%async_computation.38 | async-start | bytes 9437184 | tf_op jit(solution)/shard_map/reduce_scatter | solution.py:353
  795.5 329.0 %reduce-scatter.34.cloned.1.call-start = ((), (), s32[]{:S(2)}) async-start(), calls=%async_computation.36 | async-start | bytes 9437184 | tf_op jit(solution)/shard_map/reduce_scatter | solution.py:347
  805.6 393.7 %reduce-scatter.36.cloned.1.call-start = ((), (), s32[]{:S(2)}) async-start(), calls=%async_computation.37 | async-start | bytes 9437184 | tf_op jit(solution)/shard_map/reduce_scatter | solution.py:350
  816.0 59.9 %copy-start.18 = (f32[512,64]{0,1:T(8,128)S(1)}, f32[512,64]{0,1:T(8,128)}, u32[]{:S(2)}) copy-start(f32[512,64]{0,1:T(8,128)} %copy-done.17) | copy-start | bytes 393220
  816.0 60.0 %copy-start.20 = (f32[512,64]{0,1:T(8,128)S(1)}, f32[512,64]{0,1:T(8,128)}, u32[]{:S(2)}) copy-start(f32[512,64]{0,1:T(8,128)} %copy-done.19) | copy-start | bytes 393220
  816.0 62.1 %copy-start.5 = (f32[512,512]{0,1:T(8,128)S(1)}, f32[512,512]{0,1:T(8,128)}, u32[]{:S(2)}) copy-start(f32[512,512]{0,1:T(8,128)} %copy-done.4) | copy-start | bytes 3145732
  816.0 62.1 %copy-start.29 = (f32[512]{0:T(512)S(1)}, f32[512]{0:T(512)}, u32[]{:S(2)}) copy-start(f32[512]{0:T(512)} %copy-done.28) | copy-start | bytes 6148
  816.0 62.1 %copy-start.33 = (f32[512]{0:T(512)S(1)}, f32[512]{0:T(512)}, u32[]{:S(2)}) copy-start(f32[512]{0:T(512)} %copy-done.32) | copy-start | bytes 6148
  816.0 428.2 %reduce-scatter.28.cloned.1.call-start = ((), (), s32[]{:S(2)}) async-start(), calls=%async_computation.33 | async-start | bytes 2359296 | tf_op jit(solution)/shard_map/reduce_scatter | solution.py:338
  918.6 370.1 %reduce-scatter.26.cloned.1.call-start = ((), (), s32[]{:S(2)}) async-start(), calls=%async_computation.32 | async-start | bytes 2359296 | tf_op jit(solution)/shard_map/reduce_scatter | solution.py:335
  923.1 10.9 copy-start.15
  923.1 410.4 %reduce-scatter.30.cloned.1.call-start = ((), (), s32[]{:S(2)}) async-start(), calls=%async_computation.34 | async-start | bytes 2359296 | tf_op jit(solution)/shard_map/reduce_scatter | solution.py:341
  933.7 443.6 %reduce-scatter.24.cloned.1.call-start = ((), (), s32[]{:S(2)}) async-start(), calls=%async_computation.31 | async-start | bytes 2621440 | tf_op jit(solution)/shard_map/reduce_scatter | solution.py:324
  1052.1 325.2 %copy-start.1 = (bf16[128,2048]{1,0:T(8,128)(2,1)S(1)}, bf16[128,2048]{1,0:T(8,128)(2,1)}, u32[]{:S(2)}) copy-start(bf16[128,2048]{1,0:T(8,128)(2,1)} %param.21) | copy-start | bytes 1572868
  1052.1 325.2 %copy-start.12 = (bf16[128,2048]{1,0:T(8,128)(2,1)S(1)}, bf16[128,2048]{1,0:T(8,128)(2,1)}, u32[]{:S(2)}) copy-start(bf16[128,2048]{1,0:T(8,128)(2,1)} %reduce-scatter.18.cloned.1.call-done) | copy-start | bytes 1572868
  (17 other events, 46.3 us)
Sparse Core Ops, SparseCore 0:
  9.6 45.4 all-gather.13
  57.0 28.2 all-gather.19
  87.1 27.8 all-gather.23
  116.8 27.8 all-gather.15
  147.0 37.4 all-gather.21
  186.8 36.7 all-gather.17
  225.4 28.2 all-gather.25
  258.1 53.8 reduce-scatter.13
  314.1 55.9 all-gather.29
  372.2 44.3 all-gather.27
  418.6 54.6 all-gather.31
  475.2 55.9 all-gather.33
  541.2 41.5 reduce-scatter.15
  588.5 45.9 all-gather.35
  664.3 41.9 reduce-scatter.17
  710.6 45.9 all-gather.37
  780.1 94.6 reduce-scatter.19
  878.0 51.2 reduce-scatter.21
  933.5 41.2 reduce-scatter.31
  978.1 71.2 reduce-scatter.37
  1053.3 71.2 reduce-scatter.33
  1128.0 71.2 reduce-scatter.35
  1203.0 41.1 reduce-scatter.27
  1247.4 41.2 reduce-scatter.25
  1292.2 41.2 reduce-scatter.29
  1335.7 41.6 reduce-scatter.23
where the time goes:
time: 1400 us; the launch traced here: 1390 us
  waiting for transfers between devices  1100 us (79%)
  matrix products  150 us (11%)
  other arithmetic  43 us (3%)
  blocking collectives  41 us (3%)
  local copies, waits for them, and re-layouts  32.4 us (2%)
  between operations  15.8 us (1%)
    reduce_scatter x1, waiting for transfers between devices, on_device(): lax.psum_scatter(grad_down.astype(jnp.bfloat16), 'seq', scatter_dimension...  72.8 us
    reduce_scatter x1, waiting for transfers between devices, on_device(): lax.psum_scatter(grad_gate.astype(jnp.bfloat16), 'seq', scatter_dimension...  72.5 us
    reduce_scatter x1, waiting for transfers between devices, on_device(): lax.psum_scatter(grad_up.astype(jnp.bfloat16), 'seq', scatter_dimension=0...  72 us
    reduce_scatter x1, waiting for transfers between devices, on_device(): lax.psum_scatter(d_keys.astype(jnp.bfloat16), 'seq', scatter_dimension=0,...  56.9 us
    all_gather x1, waiting for transfers between devices, collect(): lax.all_gather(w_gate, 'seq', axis=0, tiled=True)  53.3 us
    reduce_scatter x1, waiting for transfers between devices, on_device(): lax.psum_scatter(jnp.dot(attended, w_out, preferred_element_type=f32).ast...  53.3 us
    all_gather x1, waiting for transfers between devices, on_device(): lax.all_gather(hidden_in.astype(bf16), 'head', axis=0, tiled=True)  46.4 us
    all_gather x1, waiting for transfers between devices, collect(): lax.all_gather(w_up, 'seq', axis=0, tiled=True)  46.2 us
  transfers between devices with their start and end apart: 26, of which 26 were waited for; matrix products, arithmetic and copies ran while one was open for 10% of the time, Pallas kernels for 0%

commit v1 on v0

--- a/solution.py
+++ b/solution.py
@@ -1,6 +1,10 @@
+import functools
+
 import jax
 import jax.numpy as jnp
 from jax import lax
+from jax.experimental import pallas as pl
+from jax.experimental.pallas import tpu as pltpu
 from jax.sharding import PartitionSpec as P
 
 D = 2048
@@ -81,16 +85,400 @@
     return (token_index, segment, positions)
 
 
-def collect(w_query, w_key, w_value, w_out, w_gate, w_up, w_down):
-    return (
-        lax.all_gather(w_query, "seq", axis=0, tiled=True),
-        lax.all_gather(w_key, "seq", axis=0, tiled=True),
-        lax.all_gather(w_value, "seq", axis=0, tiled=True),
-        lax.all_gather(w_out, "seq", axis=1, tiled=True),
-        lax.all_gather(w_gate, "seq", axis=0, tiled=True),
-        lax.all_gather(w_up, "seq", axis=0, tiled=True),
-        lax.all_gather(w_down, "seq", axis=1, tiled=True),
-    )
+MESH = pl.DeviceIdType.MESH
+F32 = jnp.float32
+BF16 = jnp.bfloat16
+STEPS = 4
+AG_CHUNKS = 2
+VMEM_BYTES = 60 * 1024 * 1024
+ANY = pl.BlockSpec(memory_space=pl.ANY)
+VMEM = pl.BlockSpec(memory_space=pltpu.VMEM)
+NN = (((1,), (0,)), ((), ()))
+NT = (((1,), (1,)), ((), ()))
+TN = (((0,), (0,)), ((), ()))
+
+
+def mm(left, right, dims=NN):
+    return lax.dot_general(left, right, dims, preferred_element_type=F32)
+
+
+def rows_at(index, count):
+    return pl.ds(pl.multiple_of(index * count, count), count)
+
+
+def line_barrier(z, n):
+    bar = pltpu.get_barrier_semaphore()
+    for other, there in ((z - 1, z > 0), (z + 1, z < n - 1)):
+
+        @pl.when(there)
+        def _():
+            pl.semaphore_signal(bar, inc=1, device_id={"head": other}, device_id_type=MESH)
+
+    pl.semaphore_wait(bar, (z > 0).astype(jnp.int32) + (z < n - 1).astype(jnp.int32))
+
+
+def line_gather(z, n, buf, rows, send_sem, recv_sem, use):
+    part = rows // AG_CHUNKS
+
+    def copy(src, c, up):
+        at = pl.ds(pl.multiple_of(src * rows + c * part, part), part)
+        return pltpu.make_async_remote_copy(
+            src_ref=buf.at[at],
+            dst_ref=buf.at[at],
+            send_sem=send_sem.at[up, src, c],
+            recv_sem=recv_sem.at[src, c],
+            device_id={"head": z + 1 if up else z - 1},
+            device_id_type=MESH,
+        )
+
+    more = (z > 0, z < n - 1)
+    for c in range(AG_CHUNKS):
+        for up in (0, 1):
+
+            @pl.when(more[up])
+            def _():
+                copy(z, c, up).start()
+
+    use(z)
+
+    @pl.loop(1, n)
+    def _(k):
+        sides = ((z + k, z + k < n, 0), (z - k, z - k >= 0, 1))
+        for c in range(AG_CHUNKS):
+            for src, there, up in sides:
+
+                @pl.when(there)
+                def _():
+                    copy(src, c, up).wait_recv()
+
+                    @pl.when(more[up])
+                    def _():
+                        copy(src, c, up).start()
+
+        for src, there, up in sides:
+
+            @pl.when(there)
+            def _():
+                use(src)
+
+    @pl.loop(0, n)
+    def _(src):
+        for c in range(AG_CHUNKS):
+
+            @pl.when((src >= z) & (z > 0))
+            def _():
+                copy(src, c, 0).wait_send()
+
+            @pl.when((src <= z) & (z < n - 1))
+            def _():
+                copy(src, c, 1).wait_send()
+
+
+def line_scatter(z, n, partial, land, send_sem, recv_sem, total):
+    width = total.shape[1] // STEPS
+
+    def copy(d, c, up):
+        return pltpu.make_async_remote_copy(
+            src_ref=land.at[up, d, c],
+            dst_ref=land.at[up, d, c],
+            send_sem=send_sem.at[up, d, c],
+            recv_sem=recv_sem.at[up, d, c],
+            device_id={"head": z + 1 if up else z - 1},
+            device_id_type=MESH,
+        )
+
+    @pl.loop(0, (n - 1) * STEPS)
+    def _(t):
+        j, c = t // STEPS, t % STEPS
+        for d, there, first, up in ((n - 1 - j, n - 1 - j > z, z == 0, 1), (j, j < z, z == n - 1, 0)):
+
+            @pl.when(there)
+            def _():
+                mine = partial(d, c)
+
+                @pl.when(first)
+                def _():
+                    land[up, d, c] = mine.astype(land.dtype)
+
+                @pl.when(jnp.logical_not(first))
+                def _():
+                    copy(d, c, up).wait_recv()
+                    land[up, d, c] = (land[up, d, c].astype(F32) + mine).astype(land.dtype)
+
+                copy(d, c, up).start()
+
+    @pl.loop(0, STEPS)
+    def _(c):
+        at = rows_at(c, width)
+        total[:, at] = partial(z, c)
+        for there, up in ((z > 0, 1), (z < n - 1, 0)):
+
+            @pl.when(there)
+            def _():
+                copy(z, c, up).wait_recv()
+                total[:, at] += land[up, z, c].astype(F32)
+
+    @pl.loop(0, n * STEPS)
+    def _(t):
+        d, c = t // STEPS, t % STEPS
+        for there, up in ((d > z, 1), (d < z, 0)):
+
+            @pl.when(there)
+            def _():
+                copy(d, c, up).wait_send()
+
+
+def line_sems(n):
+    dma = pltpu.SemaphoreType.DMA
+    return {
+        "gather": [dma((2, n, AG_CHUNKS)), dma((n, AG_CHUNKS))],
+        "scatter": [dma((2, n, STEPS)), dma((2, n, STEPS))],
+    }
+
+
+BLOCK = 16
+
+
+def row_scale(block):
+    return lax.rsqrt(jnp.mean(block * block, axis=-1, keepdims=True) + epsilon)
+
+
+def norm_back(e, normed, scale, gain):
+    g = e * gain
+    return scale * (g - normed * jnp.mean(g * normed, axis=-1, keepdims=True))
+
+
+def sigmoid(x):
+    return 1.0 / (1.0 + jnp.exp(-x))
+
+
+def forward_kernel(
+    n, ns,
+    att, tok, cot, wod, wgu, attn_gain, mlp_gain,
+    out, h1r, branch_out, hidden, dy2, dg, du, gain_part,
+    wo, wd, wg, wu, land, branch, h1, second, g_pre, u_pre,
+    wsem, osem, g1s, g1r, s1s, s1r, g2s, g2r, s2s, s2r,
+):
+    z = lax.axis_index("head")
+    rows, depth = tok.shape
+    lw, ff = att.shape[1], hidden.shape[1]
+    col = depth // ns
+    width = depth // STEPS
+    line_barrier(z, n)
+    loads = []
+    for s in range(ns):
+        loads.append(pltpu.make_async_copy(wod.at[s, pl.ds(0, lw)], wo.at[:, pl.ds(s * col, col)], wsem.at[0]))
+    l_g = pltpu.make_async_copy(wgu.at[:, pl.ds(0, ff)], wg, wsem.at[1])
+    l_u = pltpu.make_async_copy(wgu.at[:, pl.ds(ff, ff)], wu, wsem.at[2])
+    d_loads = [
+        pltpu.make_async_copy(wod.at[s, pl.ds(lw, ff)], wd.at[:, pl.ds(s * col, col)], wsem.at[3]) for s in range(ns)
+    ]
+    for copy in loads + [l_g, l_u] + d_loads:
+        copy.start()
+    for copy in loads:
+        copy.wait()
+
+    def out_part(d, c):
+        return mm(att[rows_at(d, rows), :], wo[:, rows_at(c, width)])
+
+    line_scatter(z, n, out_part, land, s1s, s1r, branch)
+    o_branch = pltpu.make_async_copy(branch, branch_out, osem)
+    o_branch.start()
+    gain_part[...] = jnp.zeros_like(gain_part)
+
+    @pl.loop(0, rows // BLOCK)
+    def _(i):
+        at = rows_at(i, BLOCK)
+        y = branch[at, :]
+        h = tok[at, :].astype(F32) + y * row_scale(y) * attn_gain[...]
+        h1[at, :] = h
+        h1r[pl.ds(pl.multiple_of(z * rows + i * BLOCK, BLOCK), BLOCK), :] = h.astype(BF16)
+
+    l_g.wait()
+    l_u.wait()
+    fw = ff // STEPS
+
+    def up_block(src):
+        at = rows_at(src, rows)
+
+        @pl.loop(0, STEPS)
+        def _(c):
+            cols = rows_at(c, fw)
+            x = h1r[at, :]
+            g = mm(x, wg[:, cols])
+            u = mm(x, wu[:, cols])
+            g_pre[at, cols] = g
+            u_pre[at, cols] = u
+            hidden[at, cols] = (g * sigmoid(g) * u).astype(BF16)
+
+    line_gather(z, n, h1r, rows, g1s, g1r, up_block)
+    for copy in d_loads:
+        copy.wait()
+
+    def down_part(d, c):
+        return mm(hidden[rows_at(d, rows), :], wd[:, rows_at(c, width)])
+
+    line_scatter(z, n, down_part, land, s2s, s2r, second)
+
+    @pl.loop(0, rows // BLOCK)
+    def _(i):
+        at = rows_at(i, BLOCK)
+        y = second[at, :]
+        scale = row_scale(y)
+        normed = y * scale
+        e = cot[at, :].astype(F32)
+        out[at, :] = (h1[at, :] + normed * mlp_gain[...]).astype(BF16)
+        gain_part[...] += jnp.sum(e * normed, axis=0, keepdims=True)
+        dy2[pl.ds(pl.multiple_of(z * rows + i * BLOCK, BLOCK), BLOCK), :] = norm_back(
+            e, normed, scale, mlp_gain[...]
+        ).astype(BF16)
+
+    def back_block(src):
+        at = rows_at(src, rows)
+
+        @pl.loop(0, STEPS)
+        def _(c):
+            cols = rows_at(c, fw)
+            dh = mm(dy2[at, :], wd[cols, :], NT)
+            g = g_pre[at, cols]
+            u = u_pre[at, cols]
+            sig = sigmoid(g)
+            du[at, cols] = (dh * g * sig).astype(BF16)
+            dg[at, cols] = (dh * u * sig * (1.0 + g * (1.0 - sig))).astype(BF16)
+
+    line_gather(z, n, dy2, rows, g2s, g2r, back_block)
+    o_branch.wait()
+
+
+def run_forward(n, ns, att, tok, cot, wod, wgu, attn_gain, mlp_gain):
+    rows, depth = tok.shape
+    tl, lw = att.shape
+    ff = wgu.shape[1] // 2
+    dma = pltpu.SemaphoreType.DMA
+    sems = line_sems(n)
+    shape = jax.ShapeDtypeStruct
+    return pl.pallas_call(
+        functools.partial(forward_kernel, n, ns),
+        out_shape=(
+            shape((rows, depth), BF16),
+            shape((tl, depth), BF16),
+            shape((rows, depth), F32),
+            shape((tl, ff), BF16),
+            shape((tl, depth), BF16),
+            shape((tl, ff), BF16),
+            shape((tl, ff), BF16),
+            shape((1, depth), F32),
+        ),
+        in_specs=[VMEM, VMEM, VMEM, ANY, ANY, VMEM, VMEM],
+        out_specs=(VMEM, VMEM, ANY, VMEM, VMEM, VMEM, VMEM, VMEM),
+        scratch_shapes=[
+            pltpu.VMEM((lw, depth), BF16),
+            pltpu.VMEM((ff, depth), BF16),
+            pltpu.VMEM((depth, ff), BF16),
+            pltpu.VMEM((depth, ff), BF16),
+            pltpu.VMEM((2, n, STEPS, rows, depth // STEPS), BF16),
+            pltpu.VMEM((rows, depth), F32),
+            pltpu.VMEM((rows, depth), F32),
+            pltpu.VMEM((rows, depth), F32),
+            pltpu.VMEM((tl, ff), F32),
+            pltpu.VMEM((tl, ff), F32),
+            dma((4,)),
+            dma,
+            *sems["gather"], *sems["scatter"], *sems["gather"], *sems["scatter"],
+        ],
+        compiler_params=pltpu.CompilerParams(
+            collective_id=1, has_side_effects=True, vmem_limit_bytes=VMEM_BYTES
+        ),
+        cost_estimate=pl.CostEstimate(flops=18 * 10**9, bytes_accessed=40 * 10**6, transcendentals=2 * 10**6),
+        name="feed_forward",
+    )(att, tok, cot, wod, wgu, attn_gain, mlp_gain)
+
+
+def backward_kernel(
+    n, ns,
+    dg, du, cot, branch, wod, wgu, attn_gain,
+    middle, dy1, datt, gain_part,
+    wo, wg, wu, land, total,
+    wsem, s1s, s1r, g1s, g1r,
+):
+    z = lax.axis_index("head")
+    rows, depth = cot.shape
+    lw, ff = datt.shape[1], dg.shape[1]
+    col = depth // ns
+    width = depth // STEPS
+    line_barrier(z, n)
+    l_g = pltpu.make_async_copy(wgu.at[:, pl.ds(0, ff)], wg, wsem.at[0])
+    l_u = pltpu.make_async_copy(wgu.at[:, pl.ds(ff, ff)], wu, wsem.at[1])
+    loads = [
+        pltpu.make_async_copy(wod.at[s, pl.ds(0, lw)], wo.at[:, pl.ds(s * col, col)], wsem.at[2]) for s in range(ns)
+    ]
+    for copy in [l_g, l_u] + loads:
+        copy.start()
+    l_g.wait()
+    l_u.wait()
+
+    def in_part(d, c):
+        at, cols = rows_at(d, rows), rows_at(c, width)
+        return mm(dg[at, :], wg[cols, :], NT) + mm(du[at, :], wu[cols, :], NT)
+
+    line_scatter(z, n, in_part, land, s1s, s1r, total)
+    gain_part[...] = jnp.zeros_like(gain_part)
+
+    @pl.loop(0, rows // BLOCK)
+    def _(i):
+        at = rows_at(i, BLOCK)
+        y = branch[at, :]
+        scale = row_scale(y)
+        normed = y * scale
+        e = cot[at, :].astype(F32) + total[at, :]
+        middle[at, :] = e
+        gain_part[...] += jnp.sum(e * normed, axis=0, keepdims=True)
+        dy1[pl.ds(pl.multiple_of(z * rows + i * BLOCK, BLOCK), BLOCK), :] = norm_back(
+            e, normed, scale, attn_gain[...]
+        ).astype(BF16)
+
+    for copy in loads:
+        copy.wait()
+
+    def att_block(src):
+        at = rows_at(src, rows)
+        datt[at, :] = mm(dy1[at, :], wo[...], NT).astype(BF16)
+
+    line_gather(z, n, dy1, rows, g1s, g1r, att_block)
+
+
+def run_backward(n, ns, dg, du, cot, branch, wod, wgu, attn_gain):
+    rows, depth = cot.shape
+    tl, ff = dg.shape
+    lw = wod.shape[1] - ff
+    dma = pltpu.SemaphoreType.DMA
+    sems = line_sems(n)
+    shape = jax.ShapeDtypeStruct
+    return pl.pallas_call(
+        functools.partial(backward_kernel, n, ns),
+        out_shape=(
+            shape((rows, depth), F32),
+            shape((tl, depth), BF16),
+            shape((tl, lw), BF16),
+            shape((1, depth), F32),
+        ),
+        in_specs=[VMEM, VMEM, VMEM, VMEM, ANY, ANY, VMEM],
+        out_specs=(VMEM, VMEM, VMEM, VMEM),
+        scratch_shapes=[
+            pltpu.VMEM((lw, depth), BF16),
+            pltpu.VMEM((depth, ff), BF16),
+            pltpu.VMEM((depth, ff), BF16),
+            pltpu.VMEM((2, n, STEPS, rows, depth // STEPS), BF16),
+            pltpu.VMEM((rows, depth), F32),
+            dma((3,)),
+            *sems["scatter"], *sems["gather"],
+        ],
+        compiler_params=pltpu.CompilerParams(
+            collective_id=2, has_side_effects=True, vmem_limit_bytes=VMEM_BYTES
+        ),
+        cost_estimate=pl.CostEstimate(flops=10 * 10**9, bytes_accessed=30 * 10**6, transcendentals=0),
+        name="into_attention",
+    )(dg, du, cot, branch, wod, wgu, attn_gain)
 
 
 def place_gain(vector, head_index, total_width):
@@ -128,9 +516,13 @@
     cosine_table, sine_table = rope_tables(positions)
     gain_query = lax.dynamic_slice_in_dim(q_gain, head_index * local_width, local_width)
     gain_key = lax.dynamic_slice_in_dim(k_gain, head_index * local_width, local_width)
-    w_query, w_key, w_value, w_out, w_gate, w_up, w_down = collect(
-        q_weight, k_weight, v_weight, o_weight, gate_weight, up_weight, down_weight
-    )
+    ns, nz = lax.axis_size("seq"), lax.axis_size("head")
+    w_qkv = lax.all_gather(
+        jnp.concatenate([q_weight, k_weight, v_weight], axis=1), "seq", axis=0, tiled=True
+    )
+    w_query, w_key, w_value = (w_qkv[:, i * local_width : (i + 1) * local_width] for i in range(3))
+    w_od = lax.all_gather(jnp.concatenate([o_weight, down_weight], axis=0), "seq", axis=0)
+    w_gu = lax.all_gather(jnp.concatenate([gate_weight, up_weight], axis=1), "seq", axis=0, tiled=True)
     queries = jnp.dot(gathered, w_query, preferred_element_type=f32)
     key_pre = jnp.dot(gathered, w_key, preferred_element_type=f32)
     value_pre = jnp.dot(gathered, w_value, preferred_element_type=f32)
@@ -201,56 +593,18 @@
         0, block_count, apply_step, jnp.zeros((tok_local, local_heads, HEAD_DIM), f32)
     )
     attended = summed.reshape(tok_local, local_width).astype(bf16)
-    branch = lax.psum_scatter(
-        jnp.dot(attended, w_out, preferred_element_type=f32).astype(jnp.bfloat16),
-        "head",
-        scatter_dimension=0,
-        tiled=True,
-    ).astype(jnp.float32)
-    attn_normed = rms_norm(branch)
-    hidden_in = tokens.astype(f32) + attn_normed * attn_gain
-    mlp_gathered = lax.all_gather(hidden_in.astype(bf16), "head", axis=0, tiled=True)
-    gate_pre = jnp.dot(mlp_gathered, w_gate, preferred_element_type=f32)
-    up_pre = jnp.dot(mlp_gathered, w_up, preferred_element_type=f32)
-    hidden = (jax.nn.silu(gate_pre) * up_pre).astype(bf16)
-    second = lax.psum_scatter(
-        jnp.dot(hidden, w_down, preferred_element_type=f32).astype(jnp.bfloat16),
-        "head",
-        scatter_dimension=0,
-        tiled=True,
-    ).astype(jnp.float32)
-    mlp_normed = rms_norm(second)
-    output = (hidden_in + mlp_normed * mlp_gain).astype(bf16)
-    w_query, w_key, w_value, w_out, w_gate, w_up, w_down = collect(
-        q_weight, k_weight, v_weight, o_weight, gate_weight, up_weight, down_weight
-    )
-    upstream = cotangent.astype(f32)
-    d_second, mlp_gain_part = norm_grad(mlp_normed, second, upstream, mlp_gain)
-    second_grads = lax.all_gather(d_second.astype(bf16), "head", axis=0, tiled=True)
+    output, mlp_gathered, branch, hidden, second_grads, d_gate, d_up, mlp_gain_part = run_forward(
+        nz, ns, attended, tokens, cotangent, w_od, w_gu, attn_gain[None], mlp_gain[None]
+    )
+    mlp_gain_part = mlp_gain_part[0]
     grad_down = jnp.einsum("tf,td->fd", hidden, second_grads, preferred_element_type=f32)
-    d_hidden = jnp.einsum("td,fd->tf", second_grads, w_down, preferred_element_type=f32)
-    sigmoid_gate = jax.nn.sigmoid(gate_pre)
-    d_up = (d_hidden * gate_pre * sigmoid_gate).astype(bf16)
-    d_gate = (d_hidden * up_pre * sigmoid_gate * (1.0 + gate_pre * (1.0 - sigmoid_gate))).astype(
-        bf16
-    )
     grad_gate = jnp.einsum("td,tf->df", mlp_gathered, d_gate, preferred_element_type=f32)
     grad_up = jnp.einsum("td,tf->df", mlp_gathered, d_up, preferred_element_type=f32)
-    d_middle = upstream + lax.psum_scatter(
-        (
-            jnp.einsum("tf,df->td", d_gate, w_gate, preferred_element_type=f32)
-            + jnp.einsum("tf,df->td", d_up, w_up, preferred_element_type=f32)
-        ).astype(jnp.bfloat16),
-        "head",
-        scatter_dimension=0,
-        tiled=True,
-    ).astype(jnp.float32)
-    d_branch, attn_gain_part = norm_grad(attn_normed, branch, d_middle, attn_gain)
-    branch_grads = lax.all_gather(d_branch.astype(bf16), "head", axis=0, tiled=True)
+    d_middle, branch_grads, d_attended, attn_gain_part = run_backward(
+        nz, ns, d_gate, d_up, cotangent, branch, w_od, w_gu, attn_gain[None]
+    )
+    attn_gain_part = attn_gain_part[0]
     grad_out = jnp.einsum("tc,td->cd", attended, branch_grads, preferred_element_type=f32)
-    d_attended = jnp.einsum("td,cd->tc", branch_grads, w_out, preferred_element_type=f32).astype(
-        bf16
-    )
     d_heads = d_attended.reshape(tok_local, local_heads, HEAD_DIM)
     delta_rows = jnp.transpose(jnp.sum(d_heads.astype(f32) * summed, axis=-1))
 

time: 1400 us -> 1280 us (0.914)
  waiting for transfers between devices: 1100 us -> 785 us
  Pallas kernels: 0 us -> 272 us
  matrix products: 150 us -> 79.6 us
    pallas_call x0 -> x2, Pallas kernels: none -> 272 us  [the longest x1 171 us: run_forward(): pl.pallas_call(functools.partial(forward_kernel, n, ns), out_shape=(shape...]
    all_gather x10 -> x3, waiting for transfers between devices: 368 us -> 194 us  [the longest x1 92.2 us: on_device(): lax.all_gather(jnp.concatenate([gate_weight, up_weight], axis=1), 'seq',...]
    reduce_scatter x3 -> x0, waiting for transfers between devices: 137 us -> none  [the longest x1 53.3 us: on_device(): lax.psum_scatter(jnp.dot(attended, w_out, preferred_element_type=f32).ast...]
    dot_general x8 -> x0, matrix products: 70.6 us -> none  [the longest x1 12.5 us: on_device(): up_pre = jnp.dot(mlp_gathered, w_up, preferred_element_type=f32)]
    reduce_scatter x1, waiting for transfers between devices: 34.9 us -> 1.71 us  [on_device(): lax.psum_scatter(grad_out.astype(jnp.bfloat16), 'seq', scatter_dimension=...]
    reduce_scatter x1, waiting for transfers between devices: 56.9 us -> 89 us  [on_device(): lax.psum_scatter(d_keys.astype(jnp.bfloat16), 'seq', scatter_dimension=0,...]
  transfers between devices with their start and end apart: 26 -> 16, of which waited for: 26 -> 16; matrix products, arithmetic and copies ran while one was open for 10% -> 9% of each run, Pallas kernels for 0% -> 0%
where the time goes in v1:
time: 1280 us; the launch traced here: 1270 us
  waiting for transfers between devices  785 us (61%)
  Pallas kernels  272 us (21%)
  matrix products  79.6 us (6%)
  blocking collectives  40.9 us (3%)
  other arithmetic  36.6 us (3%)
  local copies, waits for them, and re-layouts  30.4 us (2%)
  between operations  15.6 us (1%)
    pallas_call x1, Pallas kernels, run_forward(): pl.pallas_call(functools.partial(forward_kernel, n, ns), out_shape=(shape...  171 us
    pallas_call x1, Pallas kernels, run_backward(): pl.pallas_call(functools.partial(backward_kernel, n, ns), out_shape=(shap...  101 us
    all_gather x1, waiting for transfers between devices, on_device(): lax.all_gather(jnp.concatenate([gate_weight, up_weight], axis=1), 'seq',...  92.2 us
    reduce_scatter x1, waiting for transfers between devices, on_device(): lax.psum_scatter(d_keys.astype(jnp.bfloat16), 'seq', scatter_dimension=0,...  89 us
    reduce_scatter x1, waiting for transfers between devices, on_device(): lax.psum_scatter(grad_gate.astype(jnp.bfloat16), 'seq', scatter_dimension...  74.5 us
    reduce_scatter x1, waiting for transfers between devices, on_device(): lax.psum_scatter(grad_down.astype(jnp.bfloat16), 'seq', scatter_dimension...  72.2 us
    reduce_scatter x1, waiting for transfers between devices, on_device(): lax.psum_scatter(grad_up.astype(jnp.bfloat16), 'seq', scatter_dimension=0...  71.8 us
    all_gather x1, waiting for transfers between devices, on_device(): lax.all_gather(jnp.concatenate([o_weight, down_weight], axis=0), 'seq', a...  53.4 us
  transfers between devices with their start and end apart: 16, of which 16 were waited for; matrix products, arithmetic and copies ran while one was open for 9% of the time, Pallas kernels for 0%

profile of v1, /device:TPU:8, one launch (start us, length us, event | category | flops | bytes accessed | tf_op | source)
XLA Modules:
  0.0 1270.2 jit_solution(7023717802313773714)
XLA Ops:
  8.0 2.0 pad_maximum_fusion.4
  13.8 41.3 %all-gather.10.cloned.1.call-done = bf16[512,2048]{1,0:T(8,128)(2,1)} async-done(((bf16[128,2048]{1,0:T(8,128)(2,1)}), bf16[512,2048]{1,0:T(8,128)(2,1)}) %all-gather.10.cloned.1.call-update) | async-done | bytes 2097168 | tf_op jit(solution)/shard_map/all_gather | solution.py:512
  55.1 48.3 %all-gather.8.cloned.1.call-done = bf16[2048,1536]{1,0:T(8,128)(2,1)} async-done(((bf16[256,1536]{1,0:T(8,128)(2,1)}), bf16[2048,1536]{1,0:T(8,128)(2,1)}) %all-gather.8.cloned.1.call-update) | async-done | bytes 6291472 | tf_op jit(solution)/shard_map/all_gather | solution.py:520
  103.4 3.7 multiply_reduce_fusion.2
  107.2 3.3 multiply_reduce_fusion.1
  110.5 8.9 all-reduce.4
  122.0 4.5 fusion.50
  126.6 2.1 pad_maximum_fusion.1
  130.8 28.7 %all-gather.14.cloned.1.call-done = bf16[4096,512]{0,1:T(8,128)(2,1)} async-done(((bf16[512,512]{0,1:T(8,128)(2,1)}), bf16[4096,512]{0,1:T(8,128)(2,1)}) %all-gather.14.cloned.1.call-update) | async-done | bytes 4194320 | tf_op jit(solution)/shard_map/all_gather | solution.py:543
  159.5 6.2 while.45
  163.6 2.1 select_reduce_fusion.3
  165.8 33.5 %all-gather.12.cloned.1.call-done = bf16[4096,512]{0,1:T(8,128)(2,1)} async-done(((bf16[512,512]{0,1:T(8,128)(2,1)}), bf16[4096,512]{0,1:T(8,128)(2,1)}) %all-gather.12.cloned.1.call-update) | async-done | bytes 4194320 | tf_op jit(solution)/shard_map/all_gather | solution.py:544
  200.4 8.6 while.46
  204.0 5.0 fusion.127
  211.5 53.4 %all-gather.18.cloned.1.call-done = bf16[20480,256]{1,0:T(8,128)(2,1)} async-done(((bf16[2560,256]{1,0:T(8,128)(2,1)}), bf16[20480,256]{1,0:T(8,128)(2,1)}) %all-gather.18.cloned.1.call-update) | async-done | bytes 10485776 | tf_op jit(solution)/shard_map/all_gather | solution.py:524
  264.9 92.2 %all-gather.16.cloned.1.call-done.wgu = bf16[2048,4096]{1,0:T(8,128)(2,1)} async-done(((bf16[256,4096]{1,0:T(8,128)(2,1)}), bf16[2048,4096]{1,0:T(8,128)(2,1)}) %all-gather.16.cloned.1.call-update) | async-done | bytes 16777232 | tf_op jit(solution)/shard_map/all_gather | solution.py:525
  357.1 170.7 %feed_forward.1 = (bf16[128,2048]{1,0:T(8,128)(2,1)}, bf16[512,2048]{1,0:T(8,128)(2,1)}, f32[128,2048]{1,0:T(8,128)}, bf16[512,2048]{1,0:T(8,128)(2,1)}, bf16[51...) custom-call(bf16[512,512]{1,0:T(8,128)(2,1)} %copy.124.att, ...), custom_call_target="tpu_custom_call" | custom-call | flops 17999998976 | bytes 40000000 | tf_op jit(solution)/shard_map/feed_forward/pallas_call | solution.py:360
  527.8 101.5 %into_attention.1 = (f32[128,2048]{1,0:T(8,128)}, bf16[512,2048]{1,0:T(8,128)(2,1)}, bf16[512,512]{1,0:T(8,128)(2,1)}, f32[1,2048]{1,0:T(1,128)}) custom-call(bf16[512,2048]{1,0:T(8,128)(2,1)} %get-tuple-element.422.dg, bf16[512,2048]{1,0:T(8,128)(2,1)} %get-tuple-element.423.du, bf16[128,2048]{1,0:T(8,128)(2,1)} %cot.3, ...), custom_call_target="tpu_custom_call" | custom-call | flops 10000000000 | bytes 30000000 | tf_op jit(solution)/shard_map/into_attention/pallas_call | solution.py:457
  630.8 2.5 broadcast.290
  633.2 2.5 broadcast.290.clone
  635.8 22.8 %while.47 = (s32[]{:T(128)}, f32[512,4,128]{0,2,1:T(8,128)S(1)}, bf16[4096,512]{0,1:T(8,128)(2,1)}, bf16[4096,512]{0,1:T(8,128)(2,1)}, s32[]{:T(128)}, /*index=5...) while((s32[]{:T(128)}, f32[512,4,128]{0,2,1:T(8,128)S(1)}, ...), condition=%wide.region_19.20_spmd.clone, body=%wide.region_17.19_spmd.clone.sunk | while | flops 2708481536 | bytes 57198836 | solution.py:634
  649.1 3.4 fusion.139
  654.0 2.1 fusion.141
  659.5 4.3 convolution_convert_fusion.3
  665.2 89.0 %reduce-scatter.11.cloned.1.call-done = bf16[512,512]{0,1:T(8,128)(2,1)} async-done(((bf16[4096,512]{0,1:T(8,128)(2,1)}), bf16[512,512]{0,1:T(8,128)(2,1)}) %reduce-scatter.11.cloned.1.call-update) | async-done | bytes 524304 | tf_op jit(solution)/shard_map/reduce_scatter | solution.py:645
  759.8 23.2 %all-reduce.5 = (bf16[2048]{0:T(1024)(128)(2,1)S(1)}, bf16[2048]{0:T(1024)(128)(2,1)S(1)}, bf16[2048]{0:T(1024)(128)(2,1)S(1)}, bf16[2048]{0:T(1024)(128)(2,1)S(1)}) all-reduce(bf16[2048]{0:T(1024)(128)(2,1)S(1)} %dynamic_update_slice.16, ...), channel_id=13, replica_groups=mesh['seq'=8,'head'=4] {'seq'}, use_global_device_ids=true, to_apply=%region_36.37.clone | all-reduce | flops 8192 | bytes 32768
  783.2 8.9 all-reduce.6
  793.6 4.3 fusion.34
  798.4 4.3 fusion.33
  802.8 6.5 reduce-scatter.13.cloned.1.call-done
  809.3 3.6 fusion.35
  813.0 2.9 fusion.40
  815.9 3.0 fusion.36
  818.9 4.6 add_convert_fusion
  823.5 8.5 convolution_convert_fusion.2
  833.6 8.5 convolution_convert_fusion.1
  843.7 8.3 convolution_convert_fusion
  857.8 41.3 %reduce-scatter.19.cloned.1.call-done = bf16[256,512]{0,1:T(8,128)(2,1)} async-done(((bf16[2048,512]{0,1:T(8,128)(2,1)}), bf16[256,512]{0,1:T(8,128)(2,1)}) %reduce-scatter.19.cloned.1.call-update) | async-done | bytes 262160 | tf_op jit(solution)/shard_map/reduce_scatter | solution.py:692
  901.0 43.2 %reduce-scatter.17.cloned.1.call-done = bf16[256,512]{0,1:T(8,128)(2,1)} async-done(((bf16[2048,512]{0,1:T(8,128)(2,1)}), bf16[256,512]{0,1:T(8,128)(2,1)}) %reduce-scatter.17.cloned.1.call-update) | async-done | bytes 262160 | tf_op jit(solution)/shard_map/reduce_scatter | solution.py:689
  946.1 42.9 %reduce-scatter.21.cloned.1.call-done = bf16[256,512]{0,1:T(8,128)(2,1)} async-done(((bf16[2048,512]{0,1:T(8,128)(2,1)}), bf16[256,512]{0,1:T(8,128)(2,1)}) %reduce-scatter.21.cloned.1.call-update) | async-done | bytes 262160 | tf_op jit(solution)/shard_map/reduce_scatter | solution.py:695
  990.9 42.6 %reduce-scatter.15.cloned.1.call-done = bf16[128,2048]{1,0:T(8,128)(2,1)} async-done(((bf16[512,2048]{1,0:T(8,128)(2,1)}), bf16[128,2048]{1,0:T(8,128)(2,1)}) %reduce-scatter.15.cloned.1.call-update) | async-done | bytes 524304 | tf_op jit(solution)/shard_map/reduce_scatter | solution.py:678
  1033.5 2.1 convert_add_fusion
  1035.6 74.5 %reduce-scatter.25.cloned.1.call-done = bf16[256,2048]{1,0:T(8,128)(2,1)} async-done(((bf16[2048,2048]{1,0:T(8,128)(2,1)}), bf16[256,2048]{1,0:T(8,128)(2,1)}) %reduce-scatter.25.cloned.1.call-update) | async-done | bytes 1048592 | tf_op jit(solution)/shard_map/reduce_scatter | solution.py:701
  1110.1 2.8 convert_element_type.212
  1112.9 71.8 %reduce-scatter.27.cloned.1.call-done = bf16[256,2048]{1,0:T(8,128)(2,1)} async-done(((bf16[2048,2048]{1,0:T(8,128)(2,1)}), bf16[256,2048]{1,0:T(8,128)(2,1)}) %reduce-scatter.27.cloned.1.call-update) | async-done | bytes 1048592 | tf_op jit(solution)/shard_map/reduce_scatter | solution.py:704
  1184.7 2.8 convert_element_type.214
  1187.5 72.2 %reduce-scatter.29.cloned.1.call-done = bf16[2048,256]{1,0:T(8,128)(2,1)} async-done(((bf16[2048,2048]{1,0:T(8,128)(2,1)}), bf16[2048,256]{1,0:T(8,128)(2,1)}) %reduce-scatter.29.cloned.1.call-update) | async-done | bytes 1048592 | tf_op jit(solution)/shard_map/reduce_scatter | solution.py:707
  1259.7 2.7 convert_element_type.216
  (188 shorter events, 55.4 us)
Async XLA Ops:
  7.2 47.9 %all-gather.10.cloned.1.call-start = ((), (), s32[]{:S(2)}) async-start(), calls=%async_computation.11 | async-start | bytes 2621440 | tf_op jit(solution)/shard_map/all_gather | solution.py:512
  7.9 95.5 %all-gather.8.cloned.1.call-start = ((), (), s32[]{:S(2)}) async-start(), calls=%async_computation.10 | async-start | bytes 7077888 | tf_op jit(solution)/shard_map/all_gather | solution.py:520
  10.0 149.5 %all-gather.14.cloned.1.call-start = ((), (), s32[]{:S(2)}) async-start(), calls=%async_computation.13 | async-start | bytes 4718592 | tf_op jit(solution)/shard_map/all_gather | solution.py:543
  10.8 108.5 %copy-start.26 = (f32[512]{0:T(512)}, f32[512]{0:T(512)S(1)}, u32[]{:S(2)}) copy-start(f32[512]{0:T(512)S(1)} %dynamic_slice.31) | copy-start | bytes 6148
  11.6 108.0 %copy-start.24 = (f32[512]{0:T(512)}, f32[512]{0:T(512)S(1)}, u32[]{:S(2)}) copy-start(f32[512]{0:T(512)S(1)} %dynamic_slice.32) | copy-start | bytes 6148
  13.8 106.2 %copy-start.9 = (f32[512,64]{0,1:T(8,128)}, f32[512,64]{0,1:T(8,128)S(1)}, u32[]{:S(2)}) copy-start(f32[512,64]{0,1:T(8,128)S(1)} %get-tuple-element.846) | copy-start | bytes 393220
  13.8 106.2 %copy-start.11 = (f32[512,64]{0,1:T(8,128)}, f32[512,64]{0,1:T(8,128)S(1)}, u32[]{:S(2)}) copy-start(f32[512,64]{0,1:T(8,128)S(1)} %get-tuple-element.847) | copy-start | bytes 393220
  103.4 3.7 copy-start.30
  107.2 12.4 copy-start.2
  110.4 11.4 copy-start
  121.9 4.7 copy-start.13
  121.9 6.8 copy-start.15
  121.9 6.8 copy-start.16
  121.9 77.4 %all-gather.12.cloned.1.call-start = ((), (), s32[]{:S(2)}) async-start(), calls=%async_computation.12 | async-start | bytes 4718592 | tf_op jit(solution)/shard_map/all_gather | solution.py:544
  126.5 138.4 %all-gather.18.cloned.1.call-start = ((), (), s32[]{:S(2)}) async-start(), calls=%async_computation.25 | async-start | bytes 11796480 | tf_op jit(solution)/shard_map/all_gather | solution.py:524
  128.6 1.6 copy-start.32
  128.6 1.8 copy-start.17
  128.7 228.5 %all-gather.16.cloned.1.call-start = ((), (), s32[]{:S(2)}) async-start(), calls=%async_computation.14 | async-start | bytes 18874368 | tf_op jit(solution)/shard_map/all_gather | solution.py:525
  130.2 624.0 %reduce-scatter.11.cloned.1.call-start = ((), (), s32[]{:S(2)}) async-start(), calls=%async_computation.15 | async-start | bytes 4718592 | tf_op jit(solution)/shard_map/reduce_scatter | solution.py:645
  527.8 102.8 %copy-start.7 = (f32[512,4,128]{0,2,1:T(8,128)S(1)}, f32[512,4,128]{0,2,1:T(8,128)}, u32[]{:S(2)}) copy-start(f32[512,4,128]{0,2,1:T(8,128)} %get-tuple-element.420) | copy-start | bytes 3145732
  658.6 150.7 %reduce-scatter.13.cloned.1.call-start = ((), (), s32[]{:S(2)}) async-start(), calls=%async_computation.16 | async-start | bytes 4718592 | tf_op jit(solution)/shard_map/reduce_scatter | solution.py:648
  659.4 194.4 %reduce-scatter.23.cloned.1.call-start = ((), (), s32[]{:S(2)}) async-start(), calls=%async_computation.21 | async-start | bytes 2359296 | tf_op jit(solution)/shard_map/reduce_scatter | solution.py:698
  659.4 4.4 copy-start.33
  659.5 5.7 copy-start.29
  659.5 5.7 copy-start.28
  659.5 95.9 %copy-start.10 = (f32[512,64]{0,1:T(8,128)S(1)}, f32[512,64]{0,1:T(8,128)}, u32[]{:S(2)}) copy-start(f32[512,64]{0,1:T(8,128)} %copy-done.9) | copy-start | bytes 393220
  659.5 95.9 %copy-start.12 = (f32[512,64]{0,1:T(8,128)S(1)}, f32[512,64]{0,1:T(8,128)}, u32[]{:S(2)}) copy-start(f32[512,64]{0,1:T(8,128)} %copy-done.11) | copy-start | bytes 393220
  663.8 93.7 %copy-start.3 = (f32[512,512]{1,0:T(8,128)S(1)}, f32[512,512]{1,0:T(8,128)}, u32[]{:S(2)}) copy-start(f32[512,512]{1,0:T(8,128)} %copy-done.2) | copy-start | bytes 3145732
  663.8 93.7 %copy-start.23 = (f32[512]{0:T(512)S(1)}, f32[512]{0:T(512)}, u32[]{:S(2)}) copy-start(f32[512]{0:T(512)} %copy-done.22) | copy-start | bytes 6148
  663.8 93.7 %copy-start.27 = (f32[512]{0:T(512)S(1)}, f32[512]{0:T(512)}, u32[]{:S(2)}) copy-start(f32[512]{0:T(512)} %copy-done.26) | copy-start | bytes 6148
  663.8 235.3 %reduce-scatter.19.cloned.1.call-start = ((), (), s32[]{:S(2)}) async-start(), calls=%async_computation.19 | async-start | bytes 2359296 | tf_op jit(solution)/shard_map/reduce_scatter | solution.py:692
  756.4 1.7 copy-start.8
  756.5 2.7 copy-start.1
  756.5 2.7 copy-start.21
  756.5 2.7 copy-start.25
  793.6 4.6 copy-start.5
  797.9 146.3 %reduce-scatter.17.cloned.1.call-start = ((), (), s32[]{:S(2)}) async-start(), calls=%async_computation.18 | async-start | bytes 2359296 | tf_op jit(solution)/shard_map/reduce_scatter | solution.py:689
  798.4 10.9 copy-start.31
  802.8 186.2 %reduce-scatter.21.cloned.1.call-start = ((), (), s32[]{:S(2)}) async-start(), calls=%async_computation.20 | async-start | bytes 2359296 | tf_op jit(solution)/shard_map/reduce_scatter | solution.py:695
  813.0 220.5 %reduce-scatter.15.cloned.1.call-start = ((), (), s32[]{:S(2)}) async-start(), calls=%async_computation.17 | async-start | bytes 2621440 | tf_op jit(solution)/shard_map/reduce_scatter | solution.py:678
  815.9 3.0 copy-start.18
  818.9 4.7 copy-start.35
  823.5 286.6 %reduce-scatter.25.cloned.1.call-start = ((), (), s32[]{:S(2)}) async-start(), calls=%async_computation.22 | async-start | bytes 9437184 | tf_op jit(solution)/shard_map/reduce_scatter | solution.py:701
  832.1 352.6 %reduce-scatter.27.cloned.1.call-start = ((), (), s32[]{:S(2)}) async-start(), calls=%async_computation.23 | async-start | bytes 9437184 | tf_op jit(solution)/shard_map/reduce_scatter | solution.py:704
  842.1 1.6 copy-start.36
  842.1 417.6 %reduce-scatter.29.cloned.1.call-start = ((), (), s32[]{:S(2)}) async-start(), calls=%async_computation.24 | async-start | bytes 9437184 | tf_op jit(solution)/shard_map/reduce_scatter | solution.py:707
  852.1 181.4 %copy-start.14 = (f32[128,2048]{1,0:T(8,128)S(1)}, f32[128,2048]{1,0:T(8,128)}, u32[]{:S(2)}) copy-start(f32[128,2048]{1,0:T(8,128)} %get-tuple-element.425) | copy-start | bytes 3145732
  1035.6 226.8 %copy-start.19 = (bf16[128,2048]{1,0:T(8,128)(2,1)S(1)}, bf16[128,2048]{1,0:T(8,128)(2,1)}, u32[]{:S(2)}) copy-start(bf16[128,2048]{1,0:T(8,128)(2,1)} %get-tuple-element.1218) | copy-start | bytes 1572868
  (5 other events, 4.7 us)
Sparse Core Ops, SparseCore 0:
  9.6 45.4 all-gather.9
  57.6 45.8 all-gather.7
  122.0 37.4 all-gather.13
  161.8 37.4 all-gather.11
  201.6 63.2 all-gather.17
  267.2 89.8 all-gather.15
  658.8 95.3 reduce-scatter.10
  757.9 51.3 reduce-scatter.12
  812.6 41.1 reduce-scatter.22
  857.9 41.2 reduce-scatter.18
  903.0 41.2 reduce-scatter.16
  947.7 41.2 reduce-scatter.20
  991.8 41.5 reduce-scatter.14
  1037.2 72.8 reduce-scatter.24
  1113.4 71.2 reduce-scatter.26
  1188.4 71.2 reduce-scatter.28

commit v2 on v1

--- a/solution.py
+++ b/solution.py
@@ -481,6 +481,498 @@
     )(dg, du, cot, branch, wod, wgu, attn_gain)
 
 
+LOG2E = 1.4426950408889634
+NEG = -1e30
+
+
+def seq_barrier(s, ns):
+    bar = pltpu.get_barrier_semaphore()
+    for other in range(ns):
+
+        @pl.when(other != s)
+        def _():
+            pl.semaphore_signal(bar, inc=1, device_id={"seq": other}, device_id_type=MESH)
+
+    pl.semaphore_wait(bar, ns - 1)
+
+
+def share_of(s, ns, r):
+    per = ns // (2 * r)
+    chunk = s // per
+    low = chunk < r
+    sub = jnp.where(low, chunk, 2 * r - 1 - chunk)
+    return sub, jnp.where(low, s - chunk * per, per + s - chunk * per)
+
+
+def source_of(sub, i, ns, r):
+    per = ns // (2 * r)
+    return jnp.where(i < per, sub * per + i, (2 * r - 1 - sub) * per + i - per)
+
+
+def head_cols(h):
+    return pl.ds(pl.multiple_of(h * HEAD_DIM, HEAD_DIM), HEAD_DIM)
+
+
+def attend_kernel(
+    ns, heads, q_in, k_in, v_in, starts,
+    att, q_buf, k_buf, v_buf, o_buf, lse,
+    o_low, qs, qr, ks, kr, vs, vr, osend, orecv, local,
+):
+    s = lax.axis_index("seq")
+    r = ns // heads
+    blocks = ns // r
+    tl = q_in.shape[0]
+    mine, sub = s // r, s % r
+    parity = s % 2
+    seq_barrier(s, ns)
+    to_sub, to_row = share_of(s, ns, r)
+
+    def q_copy(h):
+        return pltpu.make_async_remote_copy(
+            src_ref=q_in.at[:, head_cols(h)],
+            dst_ref=q_buf.at[rows_at(to_row, tl)],
+            send_sem=qs.at[h],
+            recv_sem=qr.at[to_row],
+            device_id={"seq": h * r + to_sub},
+            device_id_type=MESH,
+        )
+
+    def q_recv(i):
+        return pltpu.make_async_remote_copy(
+            src_ref=q_buf.at[rows_at(i, tl)],
+            dst_ref=q_buf.at[rows_at(i, tl)],
+            send_sem=qs.at[0],
+            recv_sem=qr.at[i],
+            device_id={"seq": s ^ 1},
+            device_id_type=MESH,
+        )
+
+    def kv_copy(src, buf, send, recv, t, at):
+        return pltpu.make_async_remote_copy(
+            src_ref=src,
+            dst_ref=buf.at[rows_at(at, tl)],
+            send_sem=send,
+            recv_sem=recv.at[at],
+            device_id={"seq": t},
+            device_id_type=MESH,
+        )
+
+    kv = ((k_in, k_buf, ks, kr), (v_in, v_buf, vs, vr))
+    own = [pltpu.make_async_copy(x.at[:, head_cols(mine)], buf.at[rows_at(s, tl)], local.at[i])
+           for i, (x, buf, _, _) in enumerate(kv)]
+    own_q = pltpu.make_async_copy(q_in.at[:, head_cols(mine)], q_buf.at[rows_at(to_row, tl)], local.at[2])
+    for copy in own:
+        copy.start()
+
+    @pl.when(to_sub == sub)
+    def _():
+        own_q.start()
+
+    def far(t):
+        return (t != s) & (t % 2 == parity)
+
+    @pl.loop(1, ns)
+    def _(step):
+        t = s ^ step
+
+        @pl.when(far(t))
+        def _():
+            for x, buf, ss, rs in kv:
+                kv_copy(x.at[:, head_cols(t // r)], buf, ss.at[0, t], rs, t, s).start()
+
+    @pl.loop(0, heads)
+    def _(h):
+        @pl.when(h * r + to_sub != s)
+        def _():
+            q_copy(h).start()
+
+    for copy in own:
+        copy.wait()
+
+    def pass_on(src, start):
+        for _, buf, ss, rs in kv:
+            copy = kv_copy(buf.at[rows_at(src, tl)], buf, ss.at[1, src], rs, s ^ 1, src)
+            if start:
+                copy.start()
+            else:
+                copy.wait_send()
+
+    pass_on(s, True)
+
+    @pl.loop(1, ns)
+    def _(step):
+        src = s ^ step
+
+        @pl.when(far(src))
+        def _():
+            for x, buf, ss, rs in kv:
+                kv_copy(buf.at[rows_at(src, tl)], buf, ss.at[0, 0], rs, s ^ 1, src).wait_recv()
+            pass_on(src, True)
+
+    @pl.loop(0, ns)
+    def _(src):
+        @pl.when(src % 2 != parity)
+        def _():
+            for x, buf, ss, rs in kv:
+                kv_copy(buf.at[rows_at(src, tl)], buf, ss.at[0, 0], rs, s ^ 1, src).wait_recv()
+
+    @pl.when(to_sub == sub)
+    def _():
+        own_q.wait()
+
+    unit = HEAD_DIM ** (-0.5) * LOG2E
+
+    def o_copy(i, t):
+        return pltpu.make_async_remote_copy(
+            src_ref=o_low.at[rows_at(i, tl)],
+            dst_ref=att.at[:, head_cols(mine)],
+            send_sem=osend.at[i],
+            recv_sem=orecv.at[mine],
+            device_id={"seq": t},
+            device_id_type=MESH,
+        )
+
+    own_o = pltpu.make_async_copy(o_low.at[rows_at(to_row, tl)], att.at[:, head_cols(mine)], local.at[3])
+
+    @pl.loop(0, blocks)
+    def _(i):
+        src = source_of(sub, i, ns, r)
+
+        @pl.when(src != s)
+        def _():
+            q_recv(i).wait_recv()
+
+        q = q_buf[rows_at(i, tl), :]
+        start = starts[pl.ds(i, 1), :]
+        key_at = lax.broadcasted_iota(jnp.int32, (tl, tl), 0)
+
+        def step(j, carry, diagonal):
+            top, total, acc = carry
+            at = rows_at(j, tl)
+            scores = mm(k_buf[at, :], q, NT) * unit
+            allowed = key_at >= start - j * tl
+            if diagonal:
+                allowed = allowed & (key_at <= lax.broadcasted_iota(jnp.int32, (tl, tl), 1))
+            scores = jnp.where(allowed, scores, NEG)
+            new = jnp.maximum(top, jnp.max(scores, axis=0, keepdims=True))
+            terms = jnp.exp2(scores - new)
+            fade = jnp.exp2(top - new)
+            return (
+                new,
+                total * fade + jnp.sum(terms, axis=0, keepdims=True),
+                acc * fade + mm(v_buf[at, :], terms.astype(BF16), TN),
+            )
+
+        carry = (
+            jnp.full((1, tl), NEG, F32),
+            jnp.zeros((1, tl), F32),
+            jnp.zeros((HEAD_DIM, tl), F32),
+        )
+        carry = lax.fori_loop(0, src, lambda j, c: step(j, c, False), carry)
+        top, total, acc = step(src, carry, True)
+        lse[pl.ds(i, 1), :] = top + jnp.log(total) * LOG2E
+        o = jnp.transpose(acc / total)
+        o_buf[rows_at(i, tl), :] = o
+        o_low[rows_at(i, tl), :] = o.astype(BF16)
+
+        @pl.when(src != s)
+        def _():
+            o_copy(i, src).start()
+
+        @pl.when(src == s)
+        def _():
+            own_o.start()
+
+    @pl.when(to_sub == sub)
+    def _():
+        own_o.wait()
+
+    @pl.loop(0, heads)
+    def _(h):
+        @pl.when(h * r + to_sub != s)
+        def _():
+            q_copy(h).wait_send()
+            pltpu.make_async_remote_copy(
+                src_ref=o_low.at[rows_at(0, tl)],
+                dst_ref=att.at[:, head_cols(h)],
+                send_sem=osend.at[0],
+                recv_sem=orecv.at[h],
+                device_id={"seq": s ^ 1},
+                device_id_type=MESH,
+            ).wait_recv()
+
+    @pl.loop(0, blocks)
+    def _(i):
+        src = source_of(sub, i, ns, r)
+
+        @pl.when(src != s)
+        def _():
+            o_copy(i, src).wait_send()
+
+    pass_on(s, False)
+
+    @pl.loop(1, ns)
+    def _(step):
+        t = s ^ step
+
+        @pl.when(far(t))
+        def _():
+            for x, buf, ss, rs in kv:
+                kv_copy(x.at[:, head_cols(t // r)], buf, ss.at[0, t], rs, t, s).wait_send()
+            pass_on(t, False)
+
+
+def run_attend(ns, heads, q, k, v, starts):
+    tl, lw = q.shape
+    r = ns // heads
+    nq = ns // r * tl
+    nk = ns * tl
+    dma = pltpu.SemaphoreType.DMA
+    shape = jax.ShapeDtypeStruct
+    return pl.pallas_call(
+        functools.partial(attend_kernel, ns, heads),
+        out_shape=(
+            shape((tl, lw), BF16),
+            shape((nq, HEAD_DIM), BF16),
+            shape((nk, HEAD_DIM), BF16),
+            shape((nk, HEAD_DIM), BF16),
+            shape((nq, HEAD_DIM), F32),
+            shape((ns // r, tl), F32),
+        ),
+        in_specs=[VMEM] * 4,
+        out_specs=(VMEM,) * 6,
+        scratch_shapes=[
+            pltpu.VMEM((nq, HEAD_DIM), BF16),
+            dma((heads,)), dma((ns // r,)),
+            dma((2, ns)), dma((ns,)),
+            dma((2, ns)), dma((ns,)),
+            dma((ns // r,)), dma((heads,)),
+            dma((4,)),
+        ],
+        compiler_params=pltpu.CompilerParams(
+            collective_id=3, has_side_effects=True, vmem_limit_bytes=VMEM_BYTES
+        ),
+        cost_estimate=pl.CostEstimate(flops=3 * 10**9, bytes_accessed=8 * 10**6, transcendentals=5 * 10**6),
+        name="attend",
+    )(q, k, v, starts)
+
+
+def attend_back_kernel(
+    ns, heads, do_in, starts, q_buf, k_buf, v_buf, o_buf, lse,
+    dq, dk, dv,
+    do_buf, dq_low, dk_acc, dv_acc, low, pair, land,
+    ds_, dr_, ps, pr, gs, gr, qs, qr, local,
+):
+    s = lax.axis_index("seq")
+    r = ns // heads
+    blocks = ns // r
+    tl = do_in.shape[0]
+    mine, sub = s // r, s % r
+    parity = s % 2
+    seq_barrier(s, ns)
+    to_sub, to_row = share_of(s, ns, r)
+
+    def copy(src, dst, send, recv, t):
+        return pltpu.make_async_remote_copy(
+            src_ref=src, dst_ref=dst, send_sem=send, recv_sem=recv, device_id={"seq": t}, device_id_type=MESH
+        )
+
+    def do_copy(h):
+        return copy(
+            do_in.at[:, head_cols(h)], do_buf.at[rows_at(to_row, tl)], ds_.at[h], dr_.at[to_row], h * r + to_sub
+        )
+
+    own_do = pltpu.make_async_copy(do_in.at[:, head_cols(mine)], do_buf.at[rows_at(to_row, tl)], local.at[0])
+
+    @pl.when(to_sub == sub)
+    def _():
+        own_do.start()
+
+    @pl.loop(0, heads)
+    def _(h):
+        @pl.when(h * r + to_sub != s)
+        def _():
+            do_copy(h).start()
+
+    dk_acc[...] = jnp.zeros_like(dk_acc)
+    dv_acc[...] = jnp.zeros_like(dv_acc)
+
+    @pl.when(to_sub == sub)
+    def _():
+        own_do.wait()
+
+    scale = HEAD_DIM ** (-0.5)
+    unit = scale * LOG2E
+
+    def dq_copy(i, t):
+        return copy(dq_low.at[rows_at(i, tl)], dq.at[:, head_cols(mine)], qs.at[i], qr.at[mine], t)
+
+    own_dq = pltpu.make_async_copy(dq_low.at[rows_at(to_row, tl)], dq.at[:, head_cols(mine)], local.at[1])
+    ones = jnp.ones((8, HEAD_DIM), F32)
+
+    @pl.loop(0, blocks)
+    def _(i):
+        src = source_of(sub, i, ns, r)
+        rows = rows_at(i, tl)
+
+        @pl.when(src != s)
+        def _():
+            copy(do_buf.at[rows], do_buf.at[rows], ds_.at[0], dr_.at[i], s ^ 1).wait_recv()
+
+        q = q_buf[rows, :]
+        do = do_buf[rows, :]
+        start = starts[pl.ds(i, 1), :]
+        norm = lse[pl.ds(i, 1), :]
+        delta = lax.dot_general(
+            ones, do.astype(F32) * o_buf[rows, :], NT,
+            precision=lax.Precision.HIGHEST, preferred_element_type=F32,
+        )[:1]
+        key_at = lax.broadcasted_iota(jnp.int32, (tl, tl), 0)
+
+        def step(j, dq_sum, diagonal):
+            at = rows_at(j, tl)
+            keys = k_buf[at, :]
+            scores = mm(keys, q, NT) * unit
+            allowed = key_at >= start - j * tl
+            if diagonal:
+                allowed = allowed & (key_at <= lax.broadcasted_iota(jnp.int32, (tl, tl), 1))
+            p = jnp.where(allowed, jnp.exp2(scores - norm), 0.0)
+            dp = mm(v_buf[at, :], do, NT)
+            dscore = (p * (dp - delta)).astype(BF16)
+            dv_acc[at, :] += mm(p.astype(BF16), do)
+            dk_acc[at, :] += mm(dscore, q)
+            return dq_sum + mm(dscore, keys, TN)
+
+        dq_sum = lax.fori_loop(0, src, lambda j, c: step(j, c, False), jnp.zeros((tl, HEAD_DIM), F32))
+        dq_sum = step(src, dq_sum, True)
+        dq_low[rows, :] = (dq_sum * scale).astype(BF16)
+
+        @pl.when(src != s)
+        def _():
+            dq_copy(i, src).start()
+
+        @pl.when(src == s)
+        def _():
+            own_dq.start()
+
+    half = ns // 2
+
+    def pair_copy(w, i):
+        src = 2 * i + 1 - parity
+        return copy(low.at[w, rows_at(src, tl)], pair.at[w, rows_at(i, tl)], ps.at[w, i], pr.at[w, i], s ^ 1)
+
+    @pl.loop(0, half)
+    def _(i):
+        at = rows_at(2 * i + 1 - parity, tl)
+        low[0, at, :] = (dk_acc[at, :] * scale).astype(BF16)
+        pair_copy(0, i).start()
+        low[1, at, :] = dv_acc[at, :].astype(BF16)
+        pair_copy(1, i).start()
+
+    slot = sub // 2
+    outs = (dk, dv)
+
+    def back_copy(w, i):
+        dest = 2 * i + parity
+        return copy(
+            low.at[w, rows_at(dest, tl)], land.at[w, slot, :, head_cols(mine)], gs.at[w, i], gr.at[w, mine, slot], dest
+        )
+
+    @pl.loop(0, half)
+    def _(i):
+        dest = 2 * i + parity
+        at = rows_at(dest, tl)
+        for w, acc, factor in ((0, dk_acc, scale), (1, dv_acc, 1.0)):
+            copy(low.at[w, at], pair.at[w, rows_at(i, tl)], ps.at[w, i], pr.at[w, i], s ^ 1).wait_recv()
+            low[w, at, :] = (acc[at, :] * factor + pair[w, rows_at(i, tl), :].astype(F32)).astype(BF16)
+
+            @pl.when(dest != s)
+            def _():
+                back_copy(w, i).start()
+
+            @pl.when(dest == s)
+            def _():
+                land[w, slot, :, head_cols(mine)] = low[w, at, :]
+
+    @pl.loop(0, heads)
+    def _(h):
+        for w in range(2):
+            for k in range(r // 2):
+
+                @pl.when(h * r + 2 * k + parity != s)
+                def _():
+                    copy(
+                        low.at[w, rows_at(0, tl)], land.at[w, k, :, head_cols(h)], gs.at[w, 0], gr.at[w, h, k], s ^ 1
+                    ).wait_recv()
+
+    for w in range(2):
+        outs[w][...] = functools.reduce(
+            lambda a, b: a + b, [land[w, k].astype(F32) for k in range(r // 2)]
+        ).astype(BF16)
+
+    @pl.when(to_sub == sub)
+    def _():
+        own_dq.wait()
+
+    @pl.loop(0, heads)
+    def _(h):
+        @pl.when(h * r + to_sub != s)
+        def _():
+            do_copy(h).wait_send()
+            copy(dq_low.at[rows_at(0, tl)], dq.at[:, head_cols(h)], qs.at[0], qr.at[h], s ^ 1).wait_recv()
+
+    @pl.loop(0, blocks)
+    def _(i):
+        src = source_of(sub, i, ns, r)
+
+        @pl.when(src != s)
+        def _():
+            dq_copy(i, src).wait_send()
+
+    @pl.loop(0, half)
+    def _(i):
+        for w in range(2):
+            pair_copy(w, i).wait_send()
+
+            @pl.when(2 * i + parity != s)
+            def _():
+                back_copy(w, i).wait_send()
+
+
+def run_attend_back(ns, heads, do, starts, q, k, v, o, lse):
+    tl, lw = do.shape
+    r = ns // heads
+    nq = ns // r * tl
+    nk = ns * tl
+    dma = pltpu.SemaphoreType.DMA
+    shape = jax.ShapeDtypeStruct
+    return pl.pallas_call(
+        functools.partial(attend_back_kernel, ns, heads),
+        out_shape=(shape((tl, lw), BF16),) * 3,
+        in_specs=[VMEM] * 7,
+        out_specs=(VMEM,) * 3,
+        scratch_shapes=[
+            pltpu.VMEM((nq, HEAD_DIM), BF16),
+            pltpu.VMEM((nq, HEAD_DIM), BF16),
+            pltpu.VMEM((nk, HEAD_DIM), F32),
+            pltpu.VMEM((nk, HEAD_DIM), F32),
+            pltpu.VMEM((2, nk, HEAD_DIM), BF16),
+            pltpu.VMEM((2, nk // 2, HEAD_DIM), BF16),
+            pltpu.VMEM((2, r // 2, tl, lw), BF16),
+            dma((heads,)), dma((ns // r,)),
+            dma((2, ns // 2)), dma((2, ns // 2)),
+            dma((2, ns // 2)), dma((2, heads, r // 2)),
+            dma((ns // r,)), dma((heads,)),
+            dma((2,)),
+        ],
+        compiler_params=pltpu.CompilerParams(
+            collective_id=4, has_side_effects=True, vmem_limit_bytes=VMEM_BYTES
+        ),
+        cost_estimate=pl.CostEstimate(flops=8 * 10**9, bytes_accessed=10 * 10**6, transcendentals=5 * 10**6),
+        name="attend_back",
+    )(do, starts, q, k, v, o, lse)
+
+
 def place_gain(vector, head_index, total_width):
     return lax.dynamic_update_slice_in_dim(
         jnp.zeros((total_width,), jnp.float32), vector, head_index * vector.shape[0], 0
@@ -539,60 +1031,18 @@
     k_rot = rotate(
         (k_hat * gain_key).reshape(tok_local, local_heads, HEAD_DIM), cosine_table, sine_table
     ).astype(bf16)
-    key_all, value_all = (
-        lax.all_gather(k_rot.reshape(tok_local, local_width), "seq", axis=0, tiled=True),
-        lax.all_gather(value_pre.astype(bf16), "seq", axis=0, tiled=True),
-    )
-    score_scale = HEAD_DIM ** (-0.5)
-    block_count = ((seq_index + 1) * tok_local + KEY_BLOCK - 1) // KEY_BLOCK
-
-    def block_scores(block_id):
-        begin_row = block_id * KEY_BLOCK
-        key_slab = lax.dynamic_slice_in_dim(key_all, begin_row, KEY_BLOCK, 0).reshape(
-            KEY_BLOCK, local_heads, HEAD_DIM
-        )
-        value_slab = lax.dynamic_slice_in_dim(value_all, begin_row, KEY_BLOCK, 0).reshape(
-            KEY_BLOCK, local_heads, HEAD_DIM
-        )
-        scores = (
-            jnp.einsum("qhd,khd->hqk", q_rot, key_slab, preferred_element_type=f32) * score_scale
-        )
-        key_index = begin_row + jnp.arange(KEY_BLOCK, dtype=jnp.int32)
-        key_segment = segments_of(doc_lengths, key_index)
-        allowed_mask = (key_index[None, :] <= token_index[:, None]) & (
-            key_segment[None, :] == segment[:, None]
-        )
-        return (scores, allowed_mask, key_slab, value_slab)
-
-    def stats_step(block_id, carry):
-        row_top, row_total = carry
-        scores, allowed_mask, key_slab, value_slab = block_scores(block_id)
-        masked = jnp.where(allowed_mask[None], scores, -1e30)
-        new_top = jnp.maximum(row_top, jnp.max(masked, axis=-1))
-        terms = jnp.where(allowed_mask[None], jnp.exp(masked - new_top[:, :, None]), 0.0)
-        return (new_top, row_total * jnp.exp(row_top - new_top) + jnp.sum(terms, axis=-1))
-
-    row_top, row_total = lax.fori_loop(
-        0,
-        block_count,
-        stats_step,
-        (jnp.full((local_heads, tok_local), -1e30, f32), jnp.zeros((local_heads, tok_local), f32)),
-    )
-    log_total = row_top + jnp.log(row_total)
-
-    def apply_step(block_id, summed):
-        scores, allowed_mask, key_slab, value_slab = block_scores(block_id)
-        attn_weights = jnp.where(
-            allowed_mask[None], jnp.exp(scores - log_total[:, :, None]), 0.0
-        ).astype(bf16)
-        return summed + jnp.einsum(
-            "hqk,khd->qhd", attn_weights, value_slab, preferred_element_type=f32
-        )
-
-    summed = lax.fori_loop(
-        0, block_count, apply_step, jnp.zeros((tok_local, local_heads, HEAD_DIM), f32)
-    )
-    attended = summed.reshape(tok_local, local_width).astype(bf16)
+    share = ns // local_heads
+    sub = seq_index % share
+    sources = jnp.stack([source_of(sub, i, ns, share) for i in range(ns // share)])
+    query_index = sources[:, None] * tok_local + jnp.arange(tok_local, dtype=jnp.int32)[None, :]
+    doc_ends = jnp.cumsum(doc_lengths)
+    starts = jnp.sum(
+        jnp.where(query_index[:, :, None] >= doc_ends, doc_lengths, 0), axis=-1
+    ).astype(jnp.int32)
+    attended, q_held, k_held, v_held, o_held, lse = run_attend(
+        ns, local_heads, q_rot.reshape(tok_local, local_width), k_rot.reshape(tok_local, local_width),
+        value_pre.astype(bf16), starts,
+    )
     output, mlp_gathered, branch, hidden, second_grads, d_gate, d_up, mlp_gain_part = run_forward(
         nz, ns, attended, tokens, cotangent, w_od, w_gu, attn_gain[None], mlp_gain[None]
     )
@@ -605,50 +1055,11 @@
     )
     attn_gain_part = attn_gain_part[0]
     grad_out = jnp.einsum("tc,td->cd", attended, branch_grads, preferred_element_type=f32)
-    d_heads = d_attended.reshape(tok_local, local_heads, HEAD_DIM)
-    delta_rows = jnp.transpose(jnp.sum(d_heads.astype(f32) * summed, axis=-1))
-
-    def grad_step(block_id, carry):
-        d_query, d_keys, d_values = carry
-        scores, allowed_mask, key_slab, value_slab = block_scores(block_id)
-        attn_weights = jnp.where(allowed_mask[None], jnp.exp(scores - log_total[:, :, None]), 0.0)
-        weights_low = attn_weights.astype(bf16)
-        d_weights = jnp.einsum("qhd,khd->hqk", d_heads, value_slab, preferred_element_type=f32)
-        d_scores = (attn_weights * (d_weights - delta_rows[:, :, None])).astype(bf16)
-        d_query = (
-            d_query
-            + jnp.einsum("hqk,khd->qhd", d_scores, key_slab, preferred_element_type=f32)
-            * score_scale
-        )
-        key_part = (
-            jnp.einsum("hqk,qhd->khd", d_scores, q_rot, preferred_element_type=f32) * score_scale
-        ).reshape(KEY_BLOCK, local_width)
-        value_part = jnp.einsum(
-            "hqk,qhd->khd", weights_low, d_heads, preferred_element_type=f32
-        ).reshape(KEY_BLOCK, local_width)
-        begin_row = block_id * KEY_BLOCK
-        d_keys = lax.dynamic_update_slice_in_dim(d_keys, key_part, begin_row, 0)
-        d_values = lax.dynamic_update_slice_in_dim(d_values, value_part, begin_row, 0)
-        return (d_query, d_keys, d_values)
-
-    d_query, d_keys, d_values = lax.fori_loop(
-        0,
-        block_count,
-        grad_step,
-        (
-            jnp.zeros((tok_local, local_heads, HEAD_DIM), f32),
-            jnp.zeros((total_tokens, local_width), f32),
-            jnp.zeros((total_tokens, local_width), f32),
-        ),
-    )
-    key_grads, value_grads = (
-        lax.psum_scatter(
-            d_keys.astype(jnp.bfloat16), "seq", scatter_dimension=0, tiled=True
-        ).astype(jnp.float32),
-        lax.psum_scatter(
-            d_values.astype(jnp.bfloat16), "seq", scatter_dimension=0, tiled=True
-        ).astype(jnp.float32),
-    )
+    d_query, key_grads, value_grads = run_attend_back(
+        ns, local_heads, d_attended, starts, q_held, k_held, v_held, o_held, lse
+    )
+    d_query = d_query.astype(f32).reshape(tok_local, local_heads, HEAD_DIM)
+    key_grads = key_grads.astype(f32)
     d_qnorm = unrotate(d_query, cosine_table, sine_table).reshape(tok_local, local_width)
     d_knorm = unrotate(
         key_grads.reshape(tok_local, local_heads, HEAD_DIM), cosine_table, sine_table

time: 1280 us -> 1120 us (0.88)
  waiting for transfers between devices: 785 us -> 550 us
  Pallas kernels: 272 us -> 369 us
  matrix products: 79.6 us -> 59.3 us
    pallas_call x0 -> x2, Pallas kernels: none -> 97.5 us  [the longest x1 51 us: run_attend(): pl.pallas_call(functools.partial(attend_kernel, ns, heads), out_shape=(sh...]
    reduce_scatter x2 -> x0, waiting for transfers between devices: 95.5 us -> none  [the longest x1 89 us: on_device(): lax.psum_scatter(d_keys.astype(jnp.bfloat16), 'seq', scatter_dimension=0,...]
    all_gather x2 -> x0, waiting for transfers between devices: 62.3 us -> none  [the longest x1 33.5 us: on_device(): lax.all_gather(value_pre.astype(bf16), 'seq', axis=0, tiled=True)]
    all_gather x1, waiting for transfers between devices: 53.4 us -> 1.45 us  [on_device(): lax.all_gather(jnp.concatenate([o_weight, down_weight], axis=0), 'seq', a...]
    reduce_scatter x1, waiting for transfers between devices: 43.2 us -> 0.01 us  [on_device(): lax.psum_scatter(grad_query.astype(jnp.bfloat16), 'seq', scatter_dimensio...]
    reduce_scatter x1, waiting for transfers between devices: 1.71 us -> 43 us  [on_device(): lax.psum_scatter(grad_out.astype(jnp.bfloat16), 'seq', scatter_dimension=...]
    reduce_scatter x1, waiting for transfers between devices: 41.3 us -> 25.2 us  [on_device(): lax.psum_scatter(grad_key.astype(jnp.bfloat16), 'seq', scatter_dimension=...]
    dot_general x7 -> x0, matrix products: 15.9 us -> none  [the longest x1 4.97 us: apply_step(): jnp.einsum('hqk,khd->qhd', attn_weights, value_slab, preferred_element_ty...]
  transfers between devices with their start and end apart: 16 -> 12, of which waited for: 16 -> 11; matrix products, arithmetic and copies ran while one was open for 9% -> 9% of each run, Pallas kernels for 0% -> 5%
where the time goes in v2:
time: 1120 us; the launch traced here: 1110 us
  waiting for transfers between devices  550 us (49%)
  Pallas kernels  369 us (33%)
  matrix products  59.3 us (5%)
  blocking collectives  43.4 us (4%)
  local copies, waits for them, and re-layouts  39.6 us (4%)
  other arithmetic  34.9 us (3%)
  between operations  15.7 us (1%)
    pallas_call x1, Pallas kernels, run_forward(): pl.pallas_call(functools.partial(forward_kernel, n, ns), out_shape=(shape...  171 us
    pallas_call x1, Pallas kernels, run_backward(): pl.pallas_call(functools.partial(backward_kernel, n, ns), out_shape=(shap...  101 us
    all_gather x1, waiting for transfers between devices, on_device(): lax.all_gather(jnp.concatenate([gate_weight, up_weight], axis=1), 'seq',...  92.2 us
    reduce_scatter x1, waiting for transfers between devices, on_device(): lax.psum_scatter(grad_gate.astype(jnp.bfloat16), 'seq', scatter_dimension...  74.5 us
    reduce_scatter x1, waiting for transfers between devices, on_device(): lax.psum_scatter(grad_down.astype(jnp.bfloat16), 'seq', scatter_dimension...  72.2 us
    reduce_scatter x1, waiting for transfers between devices, on_device(): lax.psum_scatter(grad_up.astype(jnp.bfloat16), 'seq', scatter_dimension=0...  72 us
    pallas_call x1, Pallas kernels, run_attend(): pl.pallas_call(functools.partial(attend_kernel, ns, heads), out_shape=(sh...  51 us
    all_gather x1, waiting for transfers between devices, on_device(): lax.all_gather(jnp.concatenate([q_weight, k_weight, v_weight], axis=1), '...  48.3 us
  transfers between devices with their start and end apart: 12, of which 11 were waited for; matrix products, arithmetic and copies ran while one was open for 9% of the time, Pallas kernels for 5%

profile of v2, /device:TPU:8, one launch (start us, length us, event | category | flops | bytes accessed | tf_op | source)
XLA Modules:
  0.0 1113.9 jit_solution(8996208950247939723)
XLA Ops:
  8.0 2.0 pad_maximum_fusion.4
  18.1 1.8 multiply_cosine_fusion
  19.8 35.3 %all-gather.8.cloned.1.call-done = bf16[512,2048]{1,0:T(8,128)(2,1)} async-done(((bf16[128,2048]{1,0:T(8,128)(2,1)}), bf16[512,2048]{1,0:T(8,128)(2,1)}) %all-gather.8.cloned.1.call-update) | async-done | bytes 2097168 | tf_op jit(solution)/shard_map/all_gather | solution.py:1004
  55.1 48.3 %all-gather.6.cloned.1.call-done = bf16[2048,1536]{1,0:T(8,128)(2,1)} async-done(((bf16[256,1536]{1,0:T(8,128)(2,1)}), bf16[2048,1536]{1,0:T(8,128)(2,1)}) %all-gather.6.cloned.1.call-update) | async-done | bytes 6291472 | tf_op jit(solution)/shard_map/all_gather | solution.py:1012
  103.5 3.7 multiply_reduce_fusion
  107.2 2.9 multiply_reduce_fusion.1
  110.1 8.9 all-reduce.4
  121.6 2.4 copy.60
  125.2 2.4 copy.58
  127.6 2.3 copy.59
  130.0 2.4 subtract_convert_fusion
  135.6 3.6 fusion.17.v_in
  139.2 51.0 %attend.1 = (bf16[512,512]{1,0:T(8,128)(2,1)}, bf16[2048,128]{1,0:T(8,128)(2,1)}, bf16[4096,128]{1,0:T(8,128)(2,1)}, bf16[4096,128]{1,0:T(8,128)(2,1)}, f32[2048,128]{1,0:T(8,128)}, /*index=5*/f32[4,512]{1,0:T(4,128)}) custom-call(bf16[512,512]{1,0:T(8,128)(2,1)} %bitcast.97, bf16[512,512]{1,0:T(8,128)(2,1)} %bitcast.98, bf16[512,512]{1,0:T(8,128)(2,1)} %fusion.17.v_in, ...), custom_call_target="tpu_custom_call" | custom-call | flops 3000000000 | bytes 8000000 | tf_op jit(solution)/shard_map/attend/pallas_call | solution.py:732
  191.7 92.2 %all-gather.10.cloned.1.call-done.wgu = bf16[2048,4096]{1,0:T(8,128)(2,1)} async-done(((bf16[256,4096]{1,0:T(8,128)(2,1)}), bf16[2048,4096]{1,0:T(8,128)(2,1)}) %all-gather.10.cloned.1.call-update) | async-done | bytes 16777232 | tf_op jit(solution)/shard_map/all_gather | solution.py:1017
  283.9 170.6 %feed_forward.1 = (bf16[128,2048]{1,0:T(8,128)(2,1)}, bf16[512,2048]{1,0:T(8,128)(2,1)}, f32[128,2048]{1,0:T(8,128)}, bf16[512,2048]{1,0:T(8,128)(2,1)}, bf16[51...) custom-call(bf16[512,512]{1,0:T(8,128)(2,1)} %get-tuple-element.34.att, ...), custom_call_target="tpu_custom_call" | custom-call | flops 17999998976 | bytes 40000000 | tf_op jit(solution)/shard_map/feed_forward/pallas_call | solution.py:360
  454.5 101.4 %into_attention.1 = (f32[128,2048]{1,0:T(8,128)}, bf16[512,2048]{1,0:T(8,128)(2,1)}, bf16[512,512]{1,0:T(8,128)(2,1)}, f32[1,2048]{1,0:T(1,128)}) custom-call(bf16[512,2048]{1,0:T(8,128)(2,1)} %get-tuple-element.36.dg, bf16[512,2048]{1,0:T(8,128)(2,1)} %get-tuple-element.37.du, bf16[128,2048]{1,0:T(8,128)(2,1)} %cot.3, ...), custom_call_target="tpu_custom_call" | custom-call | flops 10000000000 | bytes 30000000 | tf_op jit(solution)/shard_map/into_attention/pallas_call | solution.py:457
  555.9 46.4 %attend_back.1 = (bf16[512,512]{1,0:T(8,128)(2,1)}, bf16[512,512]{1,0:T(8,128)(2,1)}, bf16[512,512]{1,0:T(8,128)(2,1)}) custom-call(bf16[512,512]{1,0:T(8,128)(2,1)} %get-tuple-element.40.do_in, s32[4,512]{1,0:T(4,128)} %select_reduce_fusion.starts, bf16[2048,128]{1,0:T(8,128)(2,1)} %get-tuple-element.41.q_buf, bf16[4096,128]{1,0:T(8,128)(2,1)} %get-tuple-element.42.k_buf, ...), custom_call_target="tpu_custom_call" | custom-call | flops 8000000000 | bytes 10000000 | tf_op jit(solution)/shard_map/attend_back/pallas_call | solution.py:949
  605.1 3.1 multiply_add_fusion
  608.2 1.6 pad_maximum_fusion.2
  614.9 1.6 copy.53
  617.4 22.9 %all-reduce.5 = (bf16[2048]{0:T(1024)(128)(2,1)S(1)}, bf16[2048]{0:T(1024)(128)(2,1)S(1)}, bf16[2048]{0:T(1024)(128)(2,1)S(1)}, bf16[2048]{0:T(1024)(128)(2,1)S(1)}) all-reduce(bf16[2048]{0:T(1024)(128)(2,1)S(1)} %dynamic_update_slice.6, ...), channel_id=11, replica_groups=mesh['seq'=8,'head'=4] {'seq'}, use_global_device_ids=true, to_apply=%region_21.22.clone | all-reduce | flops 8192 | bytes 32768
  640.5 11.7 %all-reduce.6 = (bf16[512]{0:T(512)(128)(2,1)S(1)}, bf16[512]{0:T(512)(128)(2,1)S(1)}, bf16[256]{0:T(256)(128)(2,1)S(1)}, bf16[256]{0:T(256)(128)(2,1)S(1)}, bf1...) all-reduce(bf16[512]{0:T(512)(128)(2,1)S(1)} %get-tuple-element.97,, ...), channel_id=1, replica_groups=mesh['seq'=8,'head'=4] {'head'}, use_global_device_ids=true, to_apply=%region_8.9 | all-reduce | flops 2048 | bytes 8192 | tf_op jit(solution)/shard_map/psum | solution.py:1072
  652.2 1.6 fusion.29
  654.6 2.6 fusion
  658.8 2.6 fusion.1
  662.5 4.4 fusion.2
  667.9 4.3 convolution_convert_fusion.3
  673.2 2.9 fusion.10
  676.1 2.9 fusion.6
  679.1 4.3 add_convert_fusion
  685.0 8.4 convolution_convert_fusion.2
  695.0 8.4 convolution_convert_fusion.1
  705.0 8.3 convolution_convert_fusion
  715.6 1.9 copy.54
  717.5 25.2 %reduce-scatter.13.cloned.1.call-done = bf16[256,512]{0,1:T(8,128)(2,1)} async-done(((bf16[2048,512]{0,1:T(8,128)(2,1)}), bf16[256,512]{0,1:T(8,128)(2,1)}) %reduce-scatter.13.cloned.1.call-update) | async-done | bytes 262160 | tf_op jit(solution)/shard_map/reduce_scatter | solution.py:1103
  742.7 1.9 copy.55
  744.6 42.6 %reduce-scatter.15.cloned.1.call-done = bf16[256,512]{0,1:T(8,128)(2,1)} async-done(((bf16[2048,512]{0,1:T(8,128)(2,1)}), bf16[256,512]{0,1:T(8,128)(2,1)}) %reduce-scatter.15.cloned.1.call-update) | async-done | bytes 262160 | tf_op jit(solution)/shard_map/reduce_scatter | solution.py:1106
  787.3 1.9 copy.56
  789.2 43.0 %reduce-scatter.17.cloned.1.call-done = bf16[512,256]{1,0:T(8,128)(2,1)} async-done(((bf16[512,2048]{1,0:T(8,128)(2,1)}), bf16[512,256]{1,0:T(8,128)(2,1)}) %reduce-scatter.17.cloned.1.call-update) | async-done | bytes 262160 | tf_op jit(solution)/shard_map/reduce_scatter | solution.py:1109
  832.2 1.8 convert_element_type.160
  833.9 42.7 %reduce-scatter.9.cloned.1.call-done = bf16[128,2048]{1,0:T(8,128)(2,1)} async-done(((bf16[512,2048]{1,0:T(8,128)(2,1)}), bf16[128,2048]{1,0:T(8,128)(2,1)}) %reduce-scatter.9.cloned.1.call-update) | async-done | bytes 524304 | tf_op jit(solution)/shard_map/reduce_scatter | solution.py:1089
  876.7 2.1 convert_add_fusion
  878.8 74.5 %reduce-scatter.19.cloned.1.call-done = bf16[256,2048]{1,0:T(8,128)(2,1)} async-done(((bf16[2048,2048]{1,0:T(8,128)(2,1)}), bf16[256,2048]{1,0:T(8,128)(2,1)}) %reduce-scatter.19.cloned.1.call-update) | async-done | bytes 1048592 | tf_op jit(solution)/shard_map/reduce_scatter | solution.py:1112
  953.3 2.8 convert_element_type.162
  956.1 72.0 %reduce-scatter.21.cloned.1.call-done = bf16[256,2048]{1,0:T(8,128)(2,1)} async-done(((bf16[2048,2048]{1,0:T(8,128)(2,1)}), bf16[256,2048]{1,0:T(8,128)(2,1)}) %reduce-scatter.21.cloned.1.call-update) | async-done | bytes 1048592 | tf_op jit(solution)/shard_map/reduce_scatter | solution.py:1115
  1028.0 2.8 convert_element_type.164
  1030.8 72.2 %reduce-scatter.23.cloned.1.call-done = bf16[2048,256]{1,0:T(8,128)(2,1)} async-done(((bf16[2048,2048]{1,0:T(8,128)(2,1)}), bf16[2048,256]{1,0:T(8,128)(2,1)}) %reduce-scatter.23.cloned.1.call-update) | async-done | bytes 1048592 | tf_op jit(solution)/shard_map/reduce_scatter | solution.py:1118
  1103.0 2.7 convert_element_type.166
  (128 shorter events, 38.8 us)
Async XLA Ops:
  7.2 2.9 copy-start.8
  7.2 2.9 copy-start.14
  7.2 47.9 %all-gather.8.cloned.1.call-start = ((), (), s32[]{:S(2)}) async-start(), calls=%async_computation.9 | async-start | bytes 2621440 | tf_op jit(solution)/shard_map/all_gather | solution.py:1004
  7.9 95.5 %all-gather.6.cloned.1.call-start = ((), (), s32[]{:S(2)}) async-start(), calls=%async_computation.8 | async-start | bytes 7077888 | tf_op jit(solution)/shard_map/all_gather | solution.py:1012
  10.0 1.5 copy-start.10
  10.1 2.0 copy-start.11
  10.1 181.6 %all-gather.12.cloned.1.call-start = ((), (), s32[]{:S(2)}) async-start(), calls=%async_computation.19 | async-start | bytes 11796480 | tf_op jit(solution)/shard_map/all_gather | solution.py:1016
  11.3 272.6 %all-gather.10.cloned.1.call-start = ((), (), s32[]{:S(2)}) async-start(), calls=%async_computation.10 | async-start | bytes 18874368 | tf_op jit(solution)/shard_map/all_gather | solution.py:1017
  13.5 0.7 copy-start.17
  13.5 2.4 copy-start.22
  13.5 702.1 %reduce-scatter.11.cloned.1.call-start = ((), (), s32[]{:S(2)}) async-start(), calls=%async_computation.12 | async-start | bytes 2359296 | tf_op jit(solution)/shard_map/reduce_scatter | solution.py:1100
  103.5 3.7 copy-start.18
  110.1 13.9 %copy-start = (f32[512,512]{1,0:T(8,128)}, f32[512,512]{1,0:T(8,128)S(1)}, u32[]{:S(2)}) copy-start(f32[512,512]{1,0:T(8,128)S(1)} %get-tuple-element.129) | copy-start | bytes 3145732
  125.2 4.8 copy-start.5
  133.1 2.5 copy-start.19
  608.2 3.1 copy-start.1
  611.3 1.0 copy-start.2
  611.4 1.6 copy-start.3
  611.4 1.9 copy-start.4
  614.9 1.9 copy-start.16
  614.9 2.0 copy-start.15
  652.2 2.4 copy-start.20
  653.8 0.8 copy-start.6
  657.2 85.5 %reduce-scatter.13.cloned.1.call-start = ((), (), s32[]{:S(2)}) async-start(), calls=%async_computation.13 | async-start | bytes 2359296 | tf_op jit(solution)/shard_map/reduce_scatter | solution.py:1103
  657.2 1.6 copy-start.21
  661.4 1.1 copy-start.12
  661.4 125.8 %reduce-scatter.15.cloned.1.call-start = ((), (), s32[]{:S(2)}) async-start(), calls=%async_computation.14 | async-start | bytes 2359296 | tf_op jit(solution)/shard_map/reduce_scatter | solution.py:1106
  666.8 1.1 copy-start.23
  666.9 165.3 %reduce-scatter.17.cloned.1.call-start = ((), (), s32[]{:S(2)}) async-start(), calls=%async_computation.15 | async-start | bytes 2359296 | tf_op jit(solution)/shard_map/reduce_scatter | solution.py:1109
  672.2 1.0 copy-start.7
  672.2 204.4 %reduce-scatter.9.cloned.1.call-start = ((), (), s32[]{:S(2)}) async-start(), calls=%async_computation.11 | async-start | bytes 2621440 | tf_op jit(solution)/shard_map/reduce_scatter | solution.py:1089
  683.4 1.6 copy-start.25
  683.4 269.9 %reduce-scatter.19.cloned.1.call-start = ((), (), s32[]{:S(2)}) async-start(), calls=%async_computation.16 | async-start | bytes 9437184 | tf_op jit(solution)/shard_map/reduce_scatter | solution.py:1112
  693.4 1.6 copy-start.24
  693.4 334.6 %reduce-scatter.21.cloned.1.call-start = ((), (), s32[]{:S(2)}) async-start(), calls=%async_computation.17 | async-start | bytes 9437184 | tf_op jit(solution)/shard_map/reduce_scatter | solution.py:1115
  703.4 1.6 copy-start.26
  703.4 399.6 %reduce-scatter.23.cloned.1.call-start = ((), (), s32[]{:S(2)}) async-start(), calls=%async_computation.18 | async-start | bytes 9437184 | tf_op jit(solution)/shard_map/reduce_scatter | solution.py:1118
  713.4 163.3 %copy-start.9 = (f32[128,2048]{1,0:T(8,128)S(1)}, f32[128,2048]{1,0:T(8,128)}, u32[]{:S(2)}) copy-start(f32[128,2048]{1,0:T(8,128)} %get-tuple-element.39) | copy-start | bytes 3145732
  1030.8 74.9 %copy-start.13 = (bf16[128,2048]{1,0:T(8,128)(2,1)S(1)}, bf16[128,2048]{1,0:T(8,128)(2,1)}, u32[]{:S(2)}) copy-start(bf16[128,2048]{1,0:T(8,128)(2,1)} %get-tuple-element.147) | copy-start | bytes 1572868
Sparse Core Ops, SparseCore 0:
  9.6 45.4 all-gather.7
  57.6 45.8 all-gather.5
  105.9 85.7 all-gather.11
  194.0 89.8 all-gather.9
  657.3 40.0 reduce-scatter.10
  701.5 41.2 reduce-scatter.12
  746.0 41.2 reduce-scatter.14
  790.9 41.2 reduce-scatter.16
  835.0 41.5 reduce-scatter.8
  880.4 72.8 reduce-scatter.18
  956.7 71.2 reduce-scatter.20
  1031.7 71.2 reduce-scatter.22

commit v3 on v2

--- a/solution.py
+++ b/solution.py
@@ -7,83 +7,9 @@
 from jax.experimental.pallas import tpu as pltpu
 from jax.sharding import PartitionSpec as P
 
-D = 2048
 HEAD_DIM = 128
-KEY_BLOCK = 1024
-
-
 epsilon = 1e-06
 rope_base = 500000.0
-
-
-def rms_norm(vector):
-    return vector * lax.rsqrt(jnp.mean(vector * vector, axis=-1, keepdims=True) + epsilon)
-
-
-def norm_grad(normed_rows, raw_rows, upstream, gain):
-    row_scale = lax.rsqrt(jnp.mean(raw_rows * raw_rows, axis=-1, keepdims=True) + epsilon)
-    grad_normed = upstream * gain
-    inner_sum = jnp.mean(grad_normed * normed_rows, axis=-1, keepdims=True)
-    return (
-        row_scale * (grad_normed - normed_rows * inner_sum),
-        jnp.sum(upstream * normed_rows, axis=0),
-    )
-
-
-def rope_tables(positions):
-    frequency = jnp.power(
-        rope_base, -jnp.arange(HEAD_DIM // 2, dtype=jnp.float32) * (2.0 / HEAD_DIM)
-    )
-    angles = positions.astype(jnp.float32)[:, None] * frequency[None, :]
-    return (jnp.cos(angles), jnp.sin(angles))
-
-
-def rotate(head_rows, cosine_table, sine_table):
-    half_dim = HEAD_DIM // 2
-    first_half = head_rows[..., :half_dim]
-    second_half = head_rows[..., half_dim:]
-    cosine_rows = cosine_table[:, None, :]
-    sine_rows = sine_table[:, None, :]
-    return jnp.concatenate(
-        [
-            first_half * cosine_rows - second_half * sine_rows,
-            second_half * cosine_rows + first_half * sine_rows,
-        ],
-        axis=-1,
-    )
-
-
-def unrotate(head_rows, cosine_table, sine_table):
-    half_dim = HEAD_DIM // 2
-    first_half = head_rows[..., :half_dim]
-    second_half = head_rows[..., half_dim:]
-    cosine_rows = cosine_table[:, None, :]
-    sine_rows = sine_table[:, None, :]
-    return jnp.concatenate(
-        [
-            first_half * cosine_rows + second_half * sine_rows,
-            second_half * cosine_rows - first_half * sine_rows,
-        ],
-        axis=-1,
-    )
-
-
-def segments_of(doc_lengths, token_index):
-    doc_ends = jnp.cumsum(doc_lengths)
-    return jnp.sum((token_index[:, None] >= doc_ends[None, :]).astype(jnp.int32), axis=1)
-
-
-def doc_layout(doc_lengths, first_row, row_count):
-    token_index = first_row + jnp.arange(row_count, dtype=jnp.int32)
-    doc_ends = jnp.cumsum(doc_lengths)
-    doc_starts = doc_ends - doc_lengths
-    segment = segments_of(doc_lengths, token_index)
-    inside = (token_index[:, None] >= doc_starts[None, :]) & (
-        token_index[:, None] < doc_ends[None, :]
-    )
-    positions = token_index - jnp.sum(jnp.where(inside, doc_starts[None, :], 0), axis=1)
-    return (token_index, segment, positions)
-
 
 MESH = pl.DeviceIdType.MESH
 F32 = jnp.float32
@@ -174,58 +100,75 @@
                 copy(src, c, 1).wait_send()
 
 
-def line_scatter(z, n, partial, land, send_sem, recv_sem, total):
-    width = total.shape[1] // STEPS
-
-    def copy(d, c, up):
+class LineScatter:
+    def __init__(self, z, n, partial, land, send_sem, recv_sem, total):
+        self.z, self.n, self.partial, self.land, self.total = z, n, partial, land, total
+        self.send_sem, self.recv_sem = send_sem, recv_sem
+
+    def copy(self, d, c, up):
         return pltpu.make_async_remote_copy(
-            src_ref=land.at[up, d, c],
-            dst_ref=land.at[up, d, c],
-            send_sem=send_sem.at[up, d, c],
-            recv_sem=recv_sem.at[up, d, c],
-            device_id={"head": z + 1 if up else z - 1},
+            src_ref=self.land.at[up, d, c],
+            dst_ref=self.land.at[up, d, c],
+            send_sem=self.send_sem.at[up, d, c],
+            recv_sem=self.recv_sem.at[up, d, c],
+            device_id={"head": self.z + 1 if up else self.z - 1},
             device_id_type=MESH,
         )
 
-    @pl.loop(0, (n - 1) * STEPS)
-    def _(t):
-        j, c = t // STEPS, t % STEPS
-        for d, there, first, up in ((n - 1 - j, n - 1 - j > z, z == 0, 1), (j, j < z, z == n - 1, 0)):
-
-            @pl.when(there)
-            def _():
-                mine = partial(d, c)
-
-                @pl.when(first)
+    def run(self, low, high):
+        z, n, land = self.z, self.n, self.land
+
+        @pl.loop(low * STEPS, high * STEPS)
+        def _(t):
+            j, c = t // STEPS, t % STEPS
+            for d, there, first, up in ((n - 1 - j, n - 1 - j > z, z == 0, 1), (j, j < z, z == n - 1, 0)):
+
+                @pl.when(there)
                 def _():
-                    land[up, d, c] = mine.astype(land.dtype)
-
-                @pl.when(jnp.logical_not(first))
+                    mine = self.partial(d, c)
+
+                    @pl.when(first)
+                    def _():
+                        land[up, d, c] = mine.astype(land.dtype)
+
+                    @pl.when(jnp.logical_not(first))
+                    def _():
+                        self.copy(d, c, up).wait_recv()
+                        land[up, d, c] = (land[up, d, c].astype(F32) + mine).astype(land.dtype)
+
+                    self.copy(d, c, up).start()
+
+    def own(self):
+        z, n, total = self.z, self.n, self.total
+        width = total.shape[1] // STEPS
+
+        @pl.loop(0, STEPS)
+        def _(c):
+            at = rows_at(c, width)
+            total[:, at] = self.partial(z, c)
+            for there, up in ((z > 0, 1), (z < n - 1, 0)):
+
+                @pl.when(there)
                 def _():
-                    copy(d, c, up).wait_recv()
-                    land[up, d, c] = (land[up, d, c].astype(F32) + mine).astype(land.dtype)
-
-                copy(d, c, up).start()
-
-    @pl.loop(0, STEPS)
-    def _(c):
-        at = rows_at(c, width)
-        total[:, at] = partial(z, c)
-        for there, up in ((z > 0, 1), (z < n - 1, 0)):
-
-            @pl.when(there)
-            def _():
-                copy(z, c, up).wait_recv()
-                total[:, at] += land[up, z, c].astype(F32)
-
-    @pl.loop(0, n * STEPS)
-    def _(t):
-        d, c = t // STEPS, t % STEPS
-        for there, up in ((d > z, 1), (d < z, 0)):
-
-            @pl.when(there)
-            def _():
-                copy(d, c, up).wait_send()
+                    self.copy(z, c, up).wait_recv()
+                    total[:, at] += self.land[up, z, c].astype(F32)
+
+    def finish(self):
+        @pl.loop(0, self.n * STEPS)
+        def _(t):
+            d, c = t // STEPS, t % STEPS
+            for there, up in ((d > self.z, 1), (d < self.z, 0)):
+
+                @pl.when(there)
+                def _():
+                    self.copy(d, c, up).wait_send()
+
+
+def line_scatter(z, n, partial, land, send_sem, recv_sem, total):
+    line = LineScatter(z, n, partial, land, send_sem, recv_sem, total)
+    line.run(0, n - 1)
+    line.own()
+    line.finish()
 
 
 def line_sems(n):
@@ -973,10 +916,503 @@
     )(do, starts, q, k, v, o, lse)
 
 
-def place_gain(vector, head_index, total_width):
-    return lax.dynamic_update_slice_in_dim(
-        jnp.zeros((total_width,), jnp.float32), vector, head_index * vector.shape[0], 0
+def cross_barrier(s, z, ns, n):
+    bar = pltpu.get_barrier_semaphore()
+    for axis, me, count in (("seq", s, ns), ("head", z, n)):
+        for other in range(count):
+
+            @pl.when(other != me)
+            def _():
+                pl.semaphore_signal(bar, inc=1, device_id={axis: other}, device_id_type=MESH)
+
+    pl.semaphore_wait(bar, ns - 1 + n - 1)
+
+
+def subsets(bits):
+    found = [0]
+    for bit in bits:
+        found += [bit | other for other in found]
+    return found
+
+
+def orders_of(ns):
+    chips = [1 << i for i in range(1, ns.bit_length() - 1)]
+    return (chips, chips[::-1])
+
+
+def remote(src, dst, send, recv, axis, to):
+    return pltpu.make_async_remote_copy(
+        src_ref=src, dst_ref=dst, send_sem=send, recv_sem=recv, device_id={axis: to}, device_id_type=MESH
     )
+
+
+class CubeGather:
+    def __init__(self, s, ns, buf, rows, send_sem, recv_sem):
+        self.s, self.buf, self.rows, self.send_sem, self.recv_sem = s, buf, rows, send_sem, recv_sem
+        self.orders = [order + [1] for order in orders_of(ns)]
+
+    def copy(self, half, bit, block):
+        part = self.rows // 2
+        at = pl.ds(pl.multiple_of(block * self.rows + half * part, part), part)
+        return remote(
+            self.buf.at[at], self.buf.at[at],
+            self.send_sem.at[bit.bit_length() - 1, block, half], self.recv_sem.at[block, half],
+            "seq", self.s ^ bit,
+        )
+
+    def start(self):
+        for i in range(len(self.orders[0])):
+            for half, order in enumerate(self.orders):
+                self.copy(half, order[i], self.s).start()
+
+    def level(self, i):
+        for j in range(2**i):
+            for half, order in enumerate(self.orders):
+                block = self.s ^ order[i] ^ subsets(order[:i])[j]
+                self.copy(half, order[i], block).wait_recv()
+                for bit in order[i + 1 :]:
+                    self.copy(half, bit, block).start()
+
+    def finish(self):
+        for half, order in enumerate(self.orders):
+            for i, bit in enumerate(order):
+                for other in subsets(order[:i]):
+                    self.copy(half, bit, self.s ^ other).wait_send()
+
+    @staticmethod
+    def sems(ns):
+        dma = pltpu.SemaphoreType.DMA
+        return [dma((ns.bit_length() - 1, ns, 2)), dma((ns, 2))]
+
+
+class CubeScatter:
+    def __init__(self, s, ns, block, rows, first, held, later, sems):
+        self.s, self.block, self.rows = s, block, rows
+        self.first, self.held, self.later = first, held, later
+        self.send0, self.recv0, self.send1, self.recv1 = sems
+        self.orders = orders_of(ns)
+        self.evens = range(0, ns, 2)
+
+    def core_copy(self, j):
+        return remote(self.first.at[j], self.held.at[j], self.send0.at[j], self.recv0.at[j], "seq", self.s ^ 1)
+
+    def send_core(self):
+        @pl.loop(0, len(self.evens))
+        def _(j):
+            self.first[j] = self.block(self.s ^ (2 * j + 1)).astype(BF16)
+            self.core_copy(j).start()
+
+    def moves(self, i):
+        part = self.rows // 2
+        base = sum(2 ** (len(self.orders[0]) - 1 - k) for k in range(i))
+        for half, order in enumerate(self.orders):
+            for j, other in enumerate(subsets(order[i + 1 :])):
+                slot = base + j
+                at = pl.ds(half * part, part)
+                yield other >> 1, at, half, slot, remote(
+                    self.held.at[(order[i] | other) >> 1, at], self.later.at[half, slot],
+                    self.send1.at[half, slot], self.recv1.at[half, slot], "seq", self.s ^ order[i],
+                )
+
+    def add_core(self):
+        @pl.loop(0, len(self.evens))
+        def _(j):
+            mine = self.block(self.s ^ (2 * j))
+            self.core_copy(j).wait_recv()
+            self.held[j] = (self.held[j].astype(F32) + mine).astype(BF16)
+
+        self.send(0)
+
+    def send(self, i):
+        for *_, copy in self.moves(i):
+            copy.start()
+
+    def take(self, i):
+        for j, at, half, slot, copy in self.moves(i):
+            copy.wait_recv()
+            self.held[j, at] = (self.held[j, at].astype(F32) + self.later[half, slot].astype(F32)).astype(BF16)
+
+    @property
+    def stages(self):
+        return len(self.orders[0])
+
+    def finish(self):
+        @pl.loop(0, len(self.evens))
+        def _(j):
+            self.core_copy(j).wait_send()
+
+        for i in range(self.stages):
+            for *_, copy in self.moves(i):
+                copy.wait_send()
+
+    @staticmethod
+    def scratch(ns, rows, width):
+        dma = pltpu.SemaphoreType.DMA
+        half = ns // 2
+        return [
+            pltpu.VMEM((half, rows, width), BF16),
+            pltpu.VMEM((half, rows, width), BF16),
+            pltpu.VMEM((2, half - 1, rows // 2, width), BF16),
+            dma((half,)), dma((half,)), dma((2, half - 1)), dma((2, half - 1)),
+        ]
+
+
+def row_sums(left, right):
+    ones = jnp.ones((8, left.shape[1]), F32)
+    both = [
+        lax.dot_general(ones, x, NT, precision=lax.Precision.HIGHEST, preferred_element_type=F32) for x in (left, right)
+    ]
+    return jnp.where(lax.broadcasted_iota(jnp.int32, both[0].shape, 0) < 4, both[0], both[1])
+
+
+def as_column(sums, row):
+    pick = (lax.broadcasted_iota(jnp.int32, (8, HEAD_DIM), 0) == row).astype(F32)
+    return lax.dot_general(sums, pick, TN, precision=lax.Precision.HIGHEST, preferred_element_type=F32)
+
+
+class SmallExchange:
+    def __init__(self, axis, me, count, land, send_sem, recv_sem):
+        self.axis, self.me, self.count, self.land = axis, me, count, land
+        self.send_sem, self.recv_sem = send_sem, recv_sem
+
+    def copy(self, slot, to):
+        return remote(self.land.at[slot], self.land.at[slot], self.send_sem.at[to], self.recv_sem.at[slot], self.axis, to)
+
+    def each(self, act):
+        @pl.loop(0, self.count)
+        def _(other):
+            @pl.when(other != self.me)
+            def _():
+                act(other)
+
+    def start(self):
+        self.each(lambda other: self.copy(self.me, other).start())
+
+    def receive(self):
+        self.each(lambda other: self.copy(other, other).wait_recv())
+
+    def finish(self):
+        self.each(lambda other: self.copy(self.me, other).wait_send())
+
+
+def turn(x, cos, sin):
+    return x * cos + pltpu.roll(x, HEAD_DIM // 2, 1) * sin
+
+
+def turn_back(x, cos, sin):
+    return x * cos - pltpu.roll(x, HEAD_DIM // 2, 1) * sin
+
+
+def project_kernel(
+    n, ns, depth_full,
+    tok, wq, wk, wv, gq, gk, cos, sin,
+    x, w, q_raw, k_raw, totals, q_rot, k_rot, v_low,
+    land, lsem, ags, agr, cgs, cgr, ss, sr,
+):
+    s, z = lax.axis_index("seq"), lax.axis_index("head")
+    rows, depth = tok.shape
+    block, lw = wq.shape
+    heads = lw // HEAD_DIM
+    cross_barrier(s, z, ns, n)
+    mine = rows_at(s, block)
+    loads = [pltpu.make_async_copy(tok, x.at[rows_at(z, rows)], lsem.at[0])] + [
+        pltpu.make_async_copy(m, w.at[mine, pl.ds(i * lw, lw)], lsem.at[i + 1]) for i, m in enumerate((wq, wk, wv))
+    ]
+    for copy in loads:
+        copy.start()
+    loads[0].wait()
+    cube = CubeGather(s, ns, w, block, cgs, cgr)
+    levels = len(cube.orders[0])
+    done = []
+
+    def weights(k):
+        todo = [0] if k == 0 and n > 2 else [i for i in range(levels) if i not in done]
+        for i in todo:
+            cube.level(i)
+            done.append(i)
+
+    def start_weights():
+        for copy in loads[1:]:
+            copy.wait()
+        cube.start()
+
+    def multiply(src):
+        at = rows_at(src, rows)
+        for i, to in enumerate((q_raw, k_raw)):
+            to[at, :] = mm(x[at, :], w[:, i * lw : (i + 1) * lw])
+        v_low[at, :] = mm(x[at, :], w[:, 2 * lw :]).astype(BF16)
+
+    part = rows // AG_CHUNKS
+
+    def copy(src, c, up):
+        at = pl.ds(pl.multiple_of(src * rows + c * part, part), part)
+        return remote(x.at[at], x.at[at], ags.at[up, src, c], agr.at[src, c], "head", z + 1 if up else z - 1)
+
+    more = (z > 0, z < n - 1)
+    for c in range(AG_CHUNKS):
+        for up in (0, 1):
+
+            @pl.when(more[up])
+            def _():
+                copy(z, c, up).start()
+
+    start_weights()
+
+    def sides(k):
+        return ((z + k, z + k < n, 0), (z - k, z - k >= 0, 1))
+
+    for k in range(1, n):
+        for c in range(AG_CHUNKS):
+            for src, there, up in sides(k):
+
+                @pl.when(there)
+                def _():
+                    copy(src, c, up).wait_recv()
+
+                    @pl.when(more[up])
+                    def _():
+                        copy(src, c, up).start()
+
+        if k <= 2:
+            weights(k - 1)
+        if k == min(2, n - 1):
+            multiply(z)
+            for src, there, _ in sides(1):
+                pl.when(there)(functools.partial(multiply, src))
+        if k > 1:
+            for src, there, _ in sides(k):
+                pl.when(there)(functools.partial(multiply, src))
+
+    totals[...] = row_sums(q_raw[...] * q_raw[...], k_raw[...] * k_raw[...])
+    land[z] = totals[...]
+    small = SmallExchange("head", z, n, land, ss, sr)
+    small.start()
+    small.receive()
+    total = land[0]
+    for k in range(1, n):
+        total = total + land[k]
+    totals[...] = total
+    for row, raw, gain, to in ((0, q_raw, gq, q_rot), (4, k_raw, gk, k_rot)):
+        scale = lax.rsqrt(as_column(total, row) / depth_full + epsilon)
+        for h in range(heads):
+            cols = slice(h * HEAD_DIM, (h + 1) * HEAD_DIM)
+            to[:, cols] = turn(raw[:, cols] * scale * gain[:, cols], cos[...], sin[...]).astype(BF16)
+    small.finish()
+    cube.finish()
+
+    @pl.loop(0, n)
+    def _(src):
+        for c in range(AG_CHUNKS):
+
+            @pl.when((src >= z) & (z > 0))
+            def _():
+                copy(src, c, 0).wait_send()
+
+            @pl.when((src <= z) & (z < n - 1))
+            def _():
+                copy(src, c, 1).wait_send()
+
+
+def run_project(n, ns, tok, wq, wk, wv, gq, gk, cos, sin):
+    rows, depth = tok.shape
+    tl = rows * n
+    lw = wq.shape[1]
+    dma = pltpu.SemaphoreType.DMA
+    shape = jax.ShapeDtypeStruct
+    return pl.pallas_call(
+        functools.partial(project_kernel, n, ns, depth),
+        out_shape=(
+            shape((tl, depth), BF16),
+            shape((depth, 3 * lw), BF16),
+            shape((tl, lw), F32),
+            shape((tl, lw), F32),
+            shape((8, tl), F32),
+            shape((tl, lw), BF16),
+            shape((tl, lw), BF16),
+            shape((tl, lw), BF16),
+        ),
+        in_specs=[ANY] * 4 + [VMEM] * 4,
+        out_specs=(VMEM,) * 8,
+        scratch_shapes=[
+            pltpu.VMEM((n, 8, tl), F32),
+            dma((4,)),
+            dma((2, n, AG_CHUNKS)), dma((n, AG_CHUNKS)),
+            *CubeGather.sems(ns),
+            dma((n,)), dma((n,)),
+        ],
+        compiler_params=pltpu.CompilerParams(
+            collective_id=5, has_side_effects=True, vmem_limit_bytes=VMEM_BYTES
+        ),
+        cost_estimate=pl.CostEstimate(flops=3 * 10**9, bytes_accessed=20 * 10**6, transcendentals=0),
+        name="project",
+    )(tok, wq, wk, wv, gq, gk, cos, sin)
+
+
+def input_kernel(
+    n, ns, depth_full,
+    dq, dk, dv, q_raw, k_raw, totals, gq, gk, cos, sin, x, w, middle, att, dy1, attn_part, mlp_part,
+    grad_in, grad_q, grad_k, grad_v, grad_o, gains,
+    dqkv, q_back, k_back, inner, land, total, message, message_z, gain_land,
+    first, held, later, c0s, c0r, c1s, c1r,
+    ss, sr, ms, mr, zs, zr, s1s, s1r,
+):
+    s, z = lax.axis_index("seq"), lax.axis_index("head")
+    rows, depth = grad_in.shape
+    tl, lw = dq.shape
+    block = depth // ns
+    heads = lw // HEAD_DIM
+    cross_barrier(s, z, ns, n)
+    sums = totals[...]
+    scales = [lax.rsqrt(as_column(sums, row) / depth_full + epsilon) for row in (0, 4)]
+    todo = ((dq, q_raw, gq, q_back), (dk, k_raw, gk, k_back))
+    message[...] = jnp.zeros_like(message)
+    products = []
+    for i, (grad, raw, gain, back) in enumerate(todo):
+        product = jnp.zeros((tl, HEAD_DIM), F32)
+        for h in range(heads):
+            cols = slice(h * HEAD_DIM, (h + 1) * HEAD_DIM)
+            hat = raw[:, cols] * scales[i]
+            turned = turn_back(grad[:, cols].astype(F32), cos[...], sin[...])
+            message[0, pl.ds(i, 1), cols] = jnp.sum(turned * hat, axis=0, keepdims=True)
+            turned = turned * gain[:, cols]
+            back[:, cols] = turned
+            product = product + turned * hat
+        products.append(product)
+    inner[z] = row_sums(*products)
+    small = SmallExchange("head", z, n, inner, ss, sr)
+    small.start()
+    for t in range(1, ns):
+        message[t, pl.ds(0, 2), pl.ds(0, lw)] = message[0, pl.ds(0, 2), pl.ds(0, lw)]
+    for t in range(ns):
+        for i, part in enumerate((attn_part, mlp_part)):
+            message[t, pl.ds(i, 1), pl.ds(lw, block)] = part[:, t * block : (t + 1) * block]
+
+    def message_copy(t, frm):
+        return remote(message.at[t], message_z.at[frm], ms.at[t], mr.at[frm], "seq", t)
+
+    def each_seq(act):
+        @pl.loop(0, ns)
+        def _(t):
+            @pl.when(t != s)
+            def _():
+                act(t)
+
+    message_z[s] = message[s]
+    each_seq(lambda t: message_copy(t, s).start())
+    dqkv[:, 2 * lw :] = dv[...]
+    small.receive()
+    sums = inner[0]
+    for k in range(1, n):
+        sums = sums + inner[k]
+    for i, (grad, raw, gain, back) in enumerate(todo):
+        mean = as_column(sums, 4 * i) / depth_full
+        for h in range(heads):
+            cols = slice(h * HEAD_DIM, (h + 1) * HEAD_DIM)
+            to = slice(i * lw + h * HEAD_DIM, i * lw + (h + 1) * HEAD_DIM)
+            dqkv[:, to] = (scales[i] * (back[:, cols] - raw[:, cols] * scales[i] * mean)).astype(BF16)
+
+    width = depth // STEPS
+
+    def weight_block(b):
+        cols = rows_at(b, block)
+        return jnp.concatenate([mm(x[:, cols], dqkv[...], TN), mm(dy1[:, cols], att[...], TN)], axis=1)
+
+    def in_part(d, c):
+        return mm(dqkv[rows_at(d, rows), :], w[rows_at(c, width), :], NT)
+
+    cube = CubeScatter(s, ns, weight_block, block, first, held, later, (c0s, c0r, c1s, c1r))
+    line = LineScatter(z, n, in_part, land, s1s, s1r, total)
+    cube.send_core()
+    line.run(0, 1)
+    cube.add_core()
+    for j in range(1, n - 1):
+        line.run(j, j + 1)
+        if j - 1 < cube.stages - 1:
+            cube.take(j - 1)
+            cube.send(j)
+    for i in range(max(n - 2, 0), cube.stages - 1):
+        cube.take(i)
+        cube.send(i + 1)
+
+    each_seq(lambda t: message_copy(t, t).wait_recv())
+    received = message_z[0]
+    for t in range(1, ns):
+        received = received + message_z[t]
+    each_seq(lambda t: message_copy(t, s).wait_send())
+    gain_land[z] = received
+    rounds = SmallExchange("head", z, n, gain_land, zs, zr)
+    rounds.start()
+    line.own()
+    grad_in[...] = middle[...] + total[...]
+    cube.take(cube.stages - 1)
+    for i, to in enumerate((grad_q, grad_k, grad_v)):
+        to[...] = held[0, :, i * lw : (i + 1) * lw].astype(F32)
+    grad_o[...] = jnp.transpose(held[0, :, 3 * lw :].astype(F32))
+    rounds.receive()
+    at = s * block
+    gains[...] = jnp.zeros_like(gains)
+    gains[0:2, :] = gain_land[at // lw, pl.ds(0, 2), pl.ds(pl.multiple_of(at % lw, block), block)]
+    both = gain_land[0, pl.ds(0, 2), pl.ds(lw, block)]
+    for k in range(1, n):
+        both = both + gain_land[k, pl.ds(0, 2), pl.ds(lw, block)]
+    gains[2:4, :] = both
+    cube.finish()
+    line.finish()
+    small.finish()
+    rounds.finish()
+
+
+def run_input(n, ns, dq, dk, dv, q_raw, k_raw, totals, gq, gk, cos, sin, x, w, middle, att, dy1, attn_part, mlp_part):
+    rows, depth = middle.shape
+    tl, lw = dq.shape
+    block = depth // ns
+    dma = pltpu.SemaphoreType.DMA
+    shape = jax.ShapeDtypeStruct
+    return pl.pallas_call(
+        functools.partial(input_kernel, n, ns, depth),
+        out_shape=(shape((rows, depth), F32),)
+        + (shape((block, lw), F32),) * 3
+        + (shape((lw, block), F32), shape((8, block), F32)),
+        in_specs=[VMEM] * 17,
+        out_specs=(VMEM,) * 6,
+        scratch_shapes=[
+            pltpu.VMEM((tl, 3 * lw), BF16),
+            pltpu.VMEM((tl, lw), F32),
+            pltpu.VMEM((tl, lw), F32),
+            pltpu.VMEM((n, 8, tl), F32),
+            pltpu.VMEM((2, n, STEPS, rows, depth // STEPS), BF16),
+            pltpu.VMEM((rows, depth), F32),
+            pltpu.VMEM((ns, 8, lw + block), F32),
+            pltpu.VMEM((ns, 8, lw + block), F32),
+            pltpu.VMEM((n, 8, lw + block), F32),
+            *CubeScatter.scratch(ns, block, 4 * lw),
+            dma((n,)), dma((n,)),
+            dma((ns,)), dma((ns,)),
+            dma((n,)), dma((n,)),
+            *line_sems(n)["scatter"],
+        ],
+        compiler_params=pltpu.CompilerParams(
+            collective_id=6, has_side_effects=True, vmem_limit_bytes=VMEM_BYTES
+        ),
+        cost_estimate=pl.CostEstimate(flops=8 * 10**9, bytes_accessed=30 * 10**6, transcendentals=0),
+        name="into_input",
+    )(dq, dk, dv, q_raw, k_raw, totals, gq, gk, cos, sin, x, w, middle, att, dy1, attn_part, mlp_part)
+
+
+def doc_starts(doc_lengths, token_index):
+    ends = jnp.cumsum(doc_lengths)
+    return jnp.sum(jnp.where(token_index[..., None] >= ends, doc_lengths, 0), axis=-1).astype(jnp.int32)
+
+
+def turn_tables(positions):
+    frequency = jnp.power(rope_base, -jnp.arange(HEAD_DIM // 2, dtype=F32) * (2.0 / HEAD_DIM))
+    angles = positions.astype(F32)[:, None] * frequency[None, :]
+    cos, sin = jnp.cos(angles), jnp.sin(angles)
+    return jnp.concatenate([cos, cos], axis=1), jnp.concatenate([-sin, sin], axis=1)
+
+
+def scatter_grad(grad):
+    return lax.psum_scatter(grad.astype(BF16), "seq", scatter_dimension=0, tiled=True)
 
 
 def on_device(
@@ -995,156 +1431,51 @@
     attn_gain,
     mlp_gain,
 ):
-    local_width = q_weight.shape[1]
-    local_heads = local_width // HEAD_DIM
-    seq_index = lax.axis_index("seq")
-    head_index = lax.axis_index("head")
-    f32 = jnp.float32
-    bf16 = jnp.bfloat16
-    gathered = lax.all_gather(tokens, "head", axis=0, tiled=True)
-    tok_local = gathered.shape[0]
-    total_tokens = tok_local * lax.axis_size("seq")
-    token_index, segment, positions = doc_layout(doc_lengths, seq_index * tok_local, tok_local)
-    cosine_table, sine_table = rope_tables(positions)
-    gain_query = lax.dynamic_slice_in_dim(q_gain, head_index * local_width, local_width)
-    gain_key = lax.dynamic_slice_in_dim(k_gain, head_index * local_width, local_width)
     ns, nz = lax.axis_size("seq"), lax.axis_size("head")
-    w_qkv = lax.all_gather(
-        jnp.concatenate([q_weight, k_weight, v_weight], axis=1), "seq", axis=0, tiled=True
-    )
-    w_query, w_key, w_value = (w_qkv[:, i * local_width : (i + 1) * local_width] for i in range(3))
+    seq_index, head_index = lax.axis_index("seq"), lax.axis_index("head")
+    lw = q_weight.shape[1]
+    heads = lw // HEAD_DIM
+    tl = tokens.shape[0] * nz
+    ff = gate_weight.shape[1]
+    token_index = seq_index * tl + jnp.arange(tl, dtype=jnp.int32)
+    cos, sin = turn_tables(token_index - doc_starts(doc_lengths, token_index))
+    share = ns // heads
+    sources = jnp.stack([source_of(seq_index % share, i, ns, share) for i in range(ns // share)])
+    starts = doc_starts(doc_lengths, sources[:, None] * tl + jnp.arange(tl, dtype=jnp.int32)[None, :])
+    gq = lax.dynamic_slice_in_dim(q_gain, head_index * lw, lw)[None]
+    gk = lax.dynamic_slice_in_dim(k_gain, head_index * lw, lw)[None]
+
     w_od = lax.all_gather(jnp.concatenate([o_weight, down_weight], axis=0), "seq", axis=0)
     w_gu = lax.all_gather(jnp.concatenate([gate_weight, up_weight], axis=1), "seq", axis=0, tiled=True)
-    queries = jnp.dot(gathered, w_query, preferred_element_type=f32)
-    key_pre = jnp.dot(gathered, w_key, preferred_element_type=f32)
-    value_pre = jnp.dot(gathered, w_value, preferred_element_type=f32)
-    q_total, k_total = lax.psum(
-        (jnp.sum(queries * queries, axis=1), jnp.sum(key_pre * key_pre, axis=1)), "head"
+    x, w_qkv, q_raw, k_raw, totals, q_rot, k_rot, v_low = run_project(
+        nz, ns, tokens, q_weight, k_weight, v_weight, gq, gk, cos, sin
     )
-    q_scale = lax.rsqrt(q_total / D + epsilon)
-    k_scale = lax.rsqrt(k_total / D + epsilon)
-    q_hat = queries * q_scale[:, None]
-    k_hat = key_pre * k_scale[:, None]
-    q_rot = rotate(
-        (q_hat * gain_query).reshape(tok_local, local_heads, HEAD_DIM), cosine_table, sine_table
-    ).astype(bf16)
-    k_rot = rotate(
-        (k_hat * gain_key).reshape(tok_local, local_heads, HEAD_DIM), cosine_table, sine_table
-    ).astype(bf16)
-    share = ns // local_heads
-    sub = seq_index % share
-    sources = jnp.stack([source_of(sub, i, ns, share) for i in range(ns // share)])
-    query_index = sources[:, None] * tok_local + jnp.arange(tok_local, dtype=jnp.int32)[None, :]
-    doc_ends = jnp.cumsum(doc_lengths)
-    starts = jnp.sum(
-        jnp.where(query_index[:, :, None] >= doc_ends, doc_lengths, 0), axis=-1
-    ).astype(jnp.int32)
-    attended, q_held, k_held, v_held, o_held, lse = run_attend(
-        ns, local_heads, q_rot.reshape(tok_local, local_width), k_rot.reshape(tok_local, local_width),
-        value_pre.astype(bf16), starts,
-    )
-    output, mlp_gathered, branch, hidden, second_grads, d_gate, d_up, mlp_gain_part = run_forward(
+    attended, q_held, k_held, v_held, o_held, lse = run_attend(ns, heads, q_rot, k_rot, v_low, starts)
+    output, h1r, branch, hidden, dy2, dg, du, mlp_part = run_forward(
         nz, ns, attended, tokens, cotangent, w_od, w_gu, attn_gain[None], mlp_gain[None]
     )
-    mlp_gain_part = mlp_gain_part[0]
-    grad_down = jnp.einsum("tf,td->fd", hidden, second_grads, preferred_element_type=f32)
-    grad_gate = jnp.einsum("td,tf->df", mlp_gathered, d_gate, preferred_element_type=f32)
-    grad_up = jnp.einsum("td,tf->df", mlp_gathered, d_up, preferred_element_type=f32)
-    d_middle, branch_grads, d_attended, attn_gain_part = run_backward(
-        nz, ns, d_gate, d_up, cotangent, branch, w_od, w_gu, attn_gain[None]
-    )
-    attn_gain_part = attn_gain_part[0]
-    grad_out = jnp.einsum("tc,td->cd", attended, branch_grads, preferred_element_type=f32)
-    d_query, key_grads, value_grads = run_attend_back(
-        ns, local_heads, d_attended, starts, q_held, k_held, v_held, o_held, lse
-    )
-    d_query = d_query.astype(f32).reshape(tok_local, local_heads, HEAD_DIM)
-    key_grads = key_grads.astype(f32)
-    d_qnorm = unrotate(d_query, cosine_table, sine_table).reshape(tok_local, local_width)
-    d_knorm = unrotate(
-        key_grads.reshape(tok_local, local_heads, HEAD_DIM), cosine_table, sine_table
-    ).reshape(tok_local, local_width)
-    q_gain_part = jnp.sum(d_qnorm * q_hat, axis=0)
-    k_gain_part = jnp.sum(d_knorm * k_hat, axis=0)
-    d_qhat = d_qnorm * gain_query
-    d_khat = d_knorm * gain_key
-    q_inner, k_inner, q_gain_full, k_gain_full, attn_gain_full, mlp_gain_full = (
-        lax.psum(jnp.sum(d_qhat * q_hat, axis=1).astype(jnp.bfloat16), "head").astype(jnp.float32),
-        lax.psum(jnp.sum(d_khat * k_hat, axis=1).astype(jnp.bfloat16), "head").astype(jnp.float32),
-        lax.psum(place_gain(q_gain_part, head_index, D).astype(jnp.bfloat16), "head").astype(
-            jnp.float32
-        ),
-        lax.psum(place_gain(k_gain_part, head_index, D).astype(jnp.bfloat16), "head").astype(
-            jnp.float32
-        ),
-        lax.psum(attn_gain_part.astype(jnp.bfloat16), "head").astype(jnp.float32),
-        lax.psum(mlp_gain_part.astype(jnp.bfloat16), "head").astype(jnp.float32),
-    )
-    d_q = (q_scale[:, None] * (d_qhat - q_hat * (q_inner / D)[:, None])).astype(bf16)
-    d_k = (k_scale[:, None] * (d_khat - k_hat * (k_inner / D)[:, None])).astype(bf16)
-    d_v = value_grads.astype(bf16)
-    grad_query = jnp.einsum("td,tc->dc", gathered, d_q, preferred_element_type=f32)
-    grad_key = jnp.einsum("td,tc->dc", gathered, d_k, preferred_element_type=f32)
-    grad_value = jnp.einsum("td,tc->dc", gathered, d_v, preferred_element_type=f32)
-    input_grad = d_middle + lax.psum_scatter(
-        (
-            jnp.einsum("tc,dc->td", d_q, w_query, preferred_element_type=f32)
-            + jnp.einsum("tc,dc->td", d_k, w_key, preferred_element_type=f32)
-            + jnp.einsum("tc,dc->td", d_v, w_value, preferred_element_type=f32)
-        ).astype(jnp.bfloat16),
-        "head",
-        scatter_dimension=0,
-        tiled=True,
-    ).astype(jnp.float32)
-    reduced = (
-        lax.psum_scatter(
-            grad_query.astype(jnp.bfloat16), "seq", scatter_dimension=0, tiled=True
-        ).astype(jnp.float32),
-        lax.psum_scatter(
-            grad_key.astype(jnp.bfloat16), "seq", scatter_dimension=0, tiled=True
-        ).astype(jnp.float32),
-        lax.psum_scatter(
-            grad_value.astype(jnp.bfloat16), "seq", scatter_dimension=0, tiled=True
-        ).astype(jnp.float32),
-        lax.psum_scatter(
-            grad_out.astype(jnp.bfloat16), "seq", scatter_dimension=1, tiled=True
-        ).astype(jnp.float32),
-        lax.psum_scatter(
-            grad_gate.astype(jnp.bfloat16), "seq", scatter_dimension=0, tiled=True
-        ).astype(jnp.float32),
-        lax.psum_scatter(
-            grad_up.astype(jnp.bfloat16), "seq", scatter_dimension=0, tiled=True
-        ).astype(jnp.float32),
-        lax.psum_scatter(
-            grad_down.astype(jnp.bfloat16), "seq", scatter_dimension=1, tiled=True
-        ).astype(jnp.float32),
-        lax.psum_scatter(
-            q_gain_full.astype(jnp.bfloat16), "seq", scatter_dimension=0, tiled=True
-        ).astype(jnp.float32),
-        lax.psum_scatter(
-            k_gain_full.astype(jnp.bfloat16), "seq", scatter_dimension=0, tiled=True
-        ).astype(jnp.float32),
-        lax.psum_scatter(
-            attn_gain_full.astype(jnp.bfloat16), "seq", scatter_dimension=0, tiled=True
-        ).astype(jnp.float32),
-        lax.psum_scatter(
-            mlp_gain_full.astype(jnp.bfloat16), "seq", scatter_dimension=0, tiled=True
-        ).astype(jnp.float32),
+    grad_gate = scatter_grad(mm(h1r, dg, TN))
+    grad_up = scatter_grad(mm(h1r, du, TN))
+    grad_down = scatter_grad(mm(dy2, hidden, TN))
+    middle, dy1, datt, attn_part = run_backward(nz, ns, dg, du, cotangent, branch, w_od, w_gu, attn_gain[None])
+    dq, dk, dv = run_attend_back(ns, heads, datt, starts, q_held, k_held, v_held, o_held, lse)
+    input_grad, grad_q, grad_k, grad_v, grad_o, gains = run_input(
+        nz, ns, dq, dk, dv, q_raw, k_raw, totals, gq, gk, cos, sin, x, w_qkv, middle, attended, dy1, attn_part, mlp_part
     )
     return (
         output,
         input_grad,
-        reduced[0],
-        reduced[1],
-        reduced[2],
-        reduced[3],
-        reduced[4],
-        reduced[5],
-        reduced[6],
-        reduced[7],
-        reduced[8],
-        reduced[9],
-        reduced[10],
+        grad_q,
+        grad_k,
+        grad_v,
+        grad_o,
+        grad_gate.astype(F32),
+        grad_up.astype(F32),
+        grad_down.astype(F32).T,
+        gains[0],
+        gains[1],
+        gains[2],
+        gains[3],
     )
 
 

time: 1120 us -> 683 us (0.61)
  waiting for transfers between devices: 550 us -> 66.5 us
  Pallas kernels: 369 us -> 538 us
  blocking collectives: 43.4 us -> 0 us
  matrix products: 59.3 us -> 27.3 us
  local copies, waits for them, and re-layouts: 39.6 us -> 14.3 us
  other arithmetic: 34.9 us -> 14.3 us
    reduce_scatter x8 -> x3, waiting for transfers between devices: 372 us -> 0.01 us  [scatter_grad(): lax.psum_scatter(grad.astype(BF16), 'seq', scatter_dimension=0, tiled=True)]
    pallas_call x0 -> x2, Pallas kernels: none -> 175 us  [the longest x1 108 us: run_input(): pl.pallas_call(functools.partial(input_kernel, n, ns, depth), out_shape=(...]
    all_gather x2 -> x0, waiting for transfers between devices: 83.6 us -> none  [the longest x1 48.3 us: on_device(): lax.all_gather(jnp.concatenate([q_weight, k_weight, v_weight], axis=1), '...]
    dot_general x13 -> x3, matrix products: 59.3 us -> 27.3 us  [mm(): return lax.dot_general(left, right, dims, preferred_element_type=F32)]
    all_gather x1, waiting for transfers between devices: 92.2 us -> 66.4 us  [on_device(): lax.all_gather(jnp.concatenate([gate_weight, up_weight], axis=1), 'seq',...]
    unnamed x1 -> x0, blocking collectives: 22.9 us -> none
    psum x2 -> x0, blocking collectives: 20.6 us -> none  [the longest x1 11.7 us: on_device(): lax.psum(jnp.sum(d_qhat * q_hat, axis=1).astype(jnp.bfloat16), 'head')]
    unnamed x69 -> x29, local copies, waits for them, and re-layouts: 29.7 us -> 10.2 us
  transfers between devices with their start and end apart: 12 -> 5, of which waited for: 11 -> 1; matrix products, arithmetic and copies ran while one was open for 9% -> 5% of each run, Pallas kernels for 5% -> 54%
where the time goes in v3:
time: 683 us; the launch traced here: 675 us
  Pallas kernels  538 us (79%)
  waiting for transfers between devices  66.5 us (10%)
  matrix products  27.3 us (4%)
  between operations  14.4 us (2%)
  local copies, waits for them, and re-layouts  14.3 us (2%)
  other arithmetic  14.3 us (2%)
    pallas_call x1, Pallas kernels, run_forward(): pl.pallas_call(functools.partial(forward_kernel, n, ns), out_shape=(shape...  171 us
    pallas_call x1, Pallas kernels, run_input(): pl.pallas_call(functools.partial(input_kernel, n, ns, depth), out_shape=(...  108 us
    pallas_call x1, Pallas kernels, run_backward(): pl.pallas_call(functools.partial(backward_kernel, n, ns), out_shape=(shap...  105 us
    pallas_call x1, Pallas kernels, run_project(): pl.pallas_call(functools.partial(project_kernel, n, ns, depth), out_shape...  67.1 us
    all_gather x1, waiting for transfers between devices, on_device(): lax.all_gather(jnp.concatenate([gate_weight, up_weight], axis=1), 'seq',...  66.4 us
    pallas_call x1, Pallas kernels, run_attend_back(): pl.pallas_call(functools.partial(attend_back_kernel, ns, heads), out_shap...  46.3 us
    pallas_call x1, Pallas kernels, run_attend(): pl.pallas_call(functools.partial(attend_kernel, ns, heads), out_shape=(sh...  41.4 us
    dot_general x3, matrix products, mm(): return lax.dot_general(left, right, dims, preferred_element_type=F32)  27.3 us
  transfers between devices with their start and end apart: 5, of which 1 were waited for; matrix products, arithmetic and copies ran while one was open for 5% of the time, Pallas kernels for 54%

profile of v3, /device:TPU:8, one launch (start us, length us, event | category | flops | bytes accessed | tf_op | source)
XLA Modules:
  0.0 675.3 jit_solution(13908665968514920503)
XLA Ops:
  7.2 0.0 all-gather.6.cloned.1.call-start
  7.2 2.5 pad_maximum_fusion.1
  9.8 0.0 all-gather.6.cloned.1.call-update
  9.8 0.0 all-gather.4.cloned.1.call-start
  9.9 1.5 pad_maximum_fusion
  11.3 0.0 all-gather.4.cloned.1.call-update
  11.4 0.0 reduce-scatter.8.cloned.1.call-start
  11.4 0.6 copy-done.8
  12.0 0.2 reduce-window.8
  12.2 1.3 dynamic_slice.6
  13.5 1.3 dynamic_slice.7
  14.9 0.1 add_multiply_fusion
  14.9 0.1 iota_add_fusion
  15.0 0.7 select_reduce_fusion.starts
  15.7 0.1 select_reduce_fusion.1
  15.8 1.0 fusion
  16.8 1.0 pad_maximum_fusion.2
  17.8 67.1 %project.1 = (bf16[512,2048]{1,0:T(8,128)(2,1)}, bf16[2048,1536]{1,0:T(8,128)(2,1)}, f32[512,512]{1,0:T(8,128)}, f32[512,512]{1,0:T(8,128)}, f32[8,512]{1,0:T(8,...) custom-call(bf16[128,2048]{1,0:T(8,128)(2,1)} %tok.3, bf16[256,512]{1,0:T(8,128)(2,1)} %wq.1, ...), custom_call_target="tpu_custom_call" | custom-call | flops 3000000000 | bytes 20000000 | tf_op jit(solution)/shard_map/project/pallas_call | solution.py:1222
  84.9 41.4 %attend.1 = (bf16[512,512]{1,0:T(8,128)(2,1)}, bf16[2048,128]{1,0:T(8,128)(2,1)}, bf16[4096,128]{1,0:T(8,128)(2,1)}, bf16[4096,128]{1,0:T(8,128)(2,1)}, f32[2048,128]{1,0:T(8,128)}, /*index=5*/f32[4,512]{1,0:T(4,128)}) custom-call(bf16[512,512]{1,0:T(8,128)(2,1)} %get-tuple-element.48.q_in, bf16[512,512]{1,0:T(8,128)(2,1)} %get-tuple-element.49.k_in, ...), custom_call_target="tpu_custom_call" | custom-call | flops 3000000000 | bytes 8000000 | tf_op jit(solution)/shard_map/attend/pallas_call | solution.py:675
  126.3 0.0 all-gather.6.cloned.1.call-done
  126.3 66.4 %all-gather.4.cloned.1.call-done.wgu = bf16[2048,4096]{1,0:T(8,128)(2,1)} async-done(((bf16[256,4096]{1,0:T(8,128)(2,1)}), bf16[2048,4096]{1,0:T(8,128)(2,1)}) %all-gather.4.cloned.1.call-update) | async-done | bytes 16777232 | tf_op jit(solution)/shard_map/all_gather | solution.py:1449
  192.7 170.6 %feed_forward.1 = (bf16[128,2048]{1,0:T(8,128)(2,1)}, bf16[512,2048]{1,0:T(8,128)(2,1)}, f32[128,2048]{1,0:T(8,128)}, bf16[512,2048]{1,0:T(8,128)(2,1)}, bf16[51...) custom-call(bf16[512,512]{1,0:T(8,128)(2,1)} %get-tuple-element.51.att, ...), custom_call_target="tpu_custom_call" | custom-call | flops 17999998976 | bytes 40000000 | tf_op jit(solution)/shard_map/feed_forward/pallas_call | solution.py:303
  363.4 10.1 %convolution_convert_fusion = bf16[2048,2048]{1,0:T(8,128)(2,1)} fusion(bf16[512,2048]{1,0:T(8,128)(2,1)} %get-tuple-element.80, bf16[512,2048]{1,0:T(8,128)(2,1)} %get-tuple-element.81), kind=kOutput, calls=%fused_computation | convolution fusion | flops 4299161600 | bytes 12582912 | tf_op jit(solution)/shard_map/dot_general | solution.py:28
  373.4 0.0 reduce-scatter.8.cloned.1.call-update
  373.4 0.3 reduce-scatter.4.cloned.1.call-start
  373.7 1.3 copy-done.9
  375.0 8.4 %convolution_convert_fusion.2 = bf16[2048,2048]{1,0:T(8,128)(2,1)} fusion(bf16[512,2048]{1,0:T(8,128)(2,1)} %get-tuple-element.79, bf16[512,2048]{1,0:T(8,128)(2,1)S(1)} %copy-done.9), kind=kOutput, calls=%fused_computation.2 | convolution fusion | flops 4299161600 | bytes 12582912 | tf_op jit(solution)/shard_map/dot_general | solution.py:28
  383.4 0.0 reduce-scatter.4.cloned.1.call-update
  383.5 0.0 reduce-scatter.6.cloned.1.call-start
  383.5 1.6 copy-done.10
  385.1 8.8 %convolution_convert_fusion.1 = bf16[2048,2048]{1,0:T(8,128)(2,1)} fusion(bf16[512,2048]{1,0:T(8,128)(2,1)} %get-tuple-element.79, bf16[512,2048]{1,0:T(8,128)(2,1)S(1)} %copy-done.10), kind=kOutput, calls=%fused_computation.1 | convolution fusion | flops 4299161600 | bytes 12582912 | tf_op jit(solution)/shard_map/dot_general | solution.py:28
  393.9 0.0 reduce-scatter.6.cloned.1.call-update
  393.9 105.1 %into_attention.1 = (f32[128,2048]{1,0:T(8,128)}, bf16[512,2048]{1,0:T(8,128)(2,1)}, bf16[512,512]{1,0:T(8,128)(2,1)}, f32[1,2048]{1,0:T(1,128)}) custom-call(bf16[512,2048]{1,0:T(8,128)(2,1)} %get-tuple-element.53.dg, bf16[512,2048]{1,0:T(8,128)(2,1)} %get-tuple-element.54.du, bf16[128,2048]{1,0:T(8,128)(2,1)} %cot.3, ...), custom_call_target="tpu_custom_call" | custom-call | flops 10000000000 | bytes 30000000 | tf_op jit(solution)/shard_map/into_attention/pallas_call | solution.py:400
  499.0 46.3 %attend_back.1 = (bf16[512,512]{1,0:T(8,128)(2,1)}, bf16[512,512]{1,0:T(8,128)(2,1)}, bf16[512,512]{1,0:T(8,128)(2,1)}) custom-call(bf16[512,512]{1,0:T(8,128)(2,1)} %get-tuple-element.56.do_in, s32[4,512]{1,0:T(4,128)} %select_reduce_fusion.starts, bf16[2048,128]{1,0:T(8,128)(2,1)} %get-tuple-element.57.q_buf, bf16[4096,128]{1,0:T(8,128)(2,1)} %get-tuple-element.58.k_buf, ...), custom_call_target="tpu_custom_call" | custom-call | flops 8000000000 | bytes 10000000 | tf_op jit(solution)/shard_map/attend_back/pallas_call | solution.py:892
  545.3 107.6 %into_input.1 = (f32[128,2048]{1,0:T(8,128)}, f32[256,512]{1,0:T(8,128)}, f32[256,512]{1,0:T(8,128)}, f32[256,512]{1,0:T(8,128)}, f32[512,256]{1,0:T(8,128)}, /*index=5*/f32[8,256]{1,0:T(8,128)}) custom-call(bf16[512,512]{1,0:T(8,128)(2,1)} %get-tuple-element.62.dq, bf16[512,512]{1,0:T(8,128)(2,1)} %get-tuple-element.63.dk, ...), custom_call_target="tpu_custom_call" | custom-call | flops 8000000000 | bytes 30000000 | tf_op jit(solution)/shard_map/into_input/pallas_call | solution.py:1371
  652.9 1.4 fusion.1
  654.4 1.5 convert_bitcast_fusion
  655.8 1.8 copy.28
  657.6 2.8 convert_element_type.25
  660.4 2.9 convert_element_type.27
  663.3 0.8 copy.35
  664.1 1.0 copy.36
  665.1 0.0 copy-done.7
  665.1 0.8 copy.37
  665.9 0.0 copy-done.6
  665.9 0.8 copy.38
  666.7 0.8 copy.39
  667.5 0.8 copy.40
  (23 shorter events, 0.1 us)
Async XLA Ops:
  7.2 2.7 copy-start.1
  7.2 2.7 copy-start.2
  7.2 119.1 %all-gather.6.cloned.1.call-start = ((), (), s32[]{:S(2)}) async-start(), calls=%async_computation.7 | async-start | bytes 11796480 | tf_op jit(solution)/shard_map/all_gather | solution.py:1448
  9.8 182.9 %all-gather.4.cloned.1.call-start = ((), (), s32[]{:S(2)}) async-start(), calls=%async_computation.3 | async-start | bytes 18874368 | tf_op jit(solution)/shard_map/all_gather | solution.py:1449
  11.3 0.7 copy-start.8
  11.4 643.0 %reduce-scatter.8.cloned.1.call-start = ((), (), s32[]{:S(2)}) async-start(), calls=%async_computation.6 | async-start | bytes 9437184 | tf_op jit(solution)/shard_map/reduce_scatter | solution.py:1415
  373.4 1.6 copy-start.9
  373.4 284.2 %reduce-scatter.4.cloned.1.call-start = ((), (), s32[]{:S(2)}) async-start(), calls=%async_computation.4 | async-start | bytes 9437184 | tf_op jit(solution)/shard_map/reduce_scatter | solution.py:1415
  383.4 1.7 copy-start.10
  383.5 277.0 %reduce-scatter.6.cloned.1.call-start = ((), (), s32[]{:S(2)}) async-start(), calls=%async_computation.5 | async-start | bytes 9437184 | tf_op jit(solution)/shard_map/reduce_scatter | solution.py:1415
  660.4 2.9 copy-start.3
  660.4 3.7 copy-start
  663.3 1.8 copy-start.7
  663.3 2.6 copy-start.6
  664.1 2.6 copy-start.5
  665.1 2.4 copy-start.4
Sparse Core Ops, SparseCore 0:
  10.5 82.0 all-gather.5
  95.0 97.6 all-gather.3
  373.6 75.3 reduce-scatter.7
  452.7 76.7 reduce-scatter.3
  532.8 89.2 reduce-scatter.5

commit v4 on v3

--- a/solution.py
+++ b/solution.py
@@ -15,8 +15,9 @@
 F32 = jnp.float32
 BF16 = jnp.bfloat16
 STEPS = 4
+LAG = 1
 AG_CHUNKS = 2
-VMEM_BYTES = 60 * 1024 * 1024
+VMEM_BYTES = 62 * 1024 * 1024
 ANY = pl.BlockSpec(memory_space=pl.ANY)
 VMEM = pl.BlockSpec(memory_space=pltpu.VMEM)
 NN = (((1,), (0,)), ((), ()))
@@ -32,18 +33,21 @@
     return pl.ds(pl.multiple_of(index * count, count), count)
 
 
-def line_barrier(z, n):
+def cube_barrier(s, z, ns, n):
     bar = pltpu.get_barrier_semaphore()
+    bits = [1 << i for i in range(ns.bit_length() - 1)]
+    for bit in bits:
+        pl.semaphore_signal(bar, inc=1, device_id={"seq": s ^ bit}, device_id_type=MESH)
     for other, there in ((z - 1, z > 0), (z + 1, z < n - 1)):
 
         @pl.when(there)
         def _():
             pl.semaphore_signal(bar, inc=1, device_id={"head": other}, device_id_type=MESH)
 
-    pl.semaphore_wait(bar, (z > 0).astype(jnp.int32) + (z < n - 1).astype(jnp.int32))
-
-
-def line_gather(z, n, buf, rows, send_sem, recv_sem, use):
+    pl.semaphore_wait(bar, len(bits) + (z > 0).astype(jnp.int32) + (z < n - 1).astype(jnp.int32))
+
+
+def line_gather(z, n, buf, rows, send_sem, recv_sem, use, hooks=(), ready=None):
     part = rows // AG_CHUNKS
 
     def copy(src, c, up):
@@ -65,6 +69,8 @@
             def _():
                 copy(z, c, up).start()
 
+    if ready is not None:
+        ready()
     use(z)
 
     @pl.loop(1, n)
@@ -86,6 +92,9 @@
             @pl.when(there)
             def _():
                 use(src)
+
+        for i, hook in enumerate(hooks):
+            pl.when(k == i + 1)(hook)
 
     @pl.loop(0, n)
     def _(src):
@@ -115,13 +124,24 @@
             device_id_type=MESH,
         )
 
-    def run(self, low, high):
+    @property
+    def slots(self):
+        return (self.n - 1) * (STEPS + LAG)
+
+    def run(self, low, high, before=None, after=None):
         z, n, land = self.z, self.n, self.land
 
-        @pl.loop(low * STEPS, high * STEPS)
-        def _(t):
-            j, c = t // STEPS, t % STEPS
-            for d, there, first, up in ((n - 1 - j, n - 1 - j > z, z == 0, 1), (j, j < z, z == n - 1, 0)):
+        @pl.loop(low, high)
+        def _(slot):
+            if before is not None:
+                before(slot)
+            for up in (1, 0):
+                t = slot - (z if up else n - 1 - z) * LAG
+                j = t // STEPS
+                c = t - j * STEPS
+                d = n - 1 - j if up else j
+                first = z == 0 if up else z == n - 1
+                there = (t >= 0) & (j < n - 1) & ((d > z) if up else (d < z))
 
                 @pl.when(there)
                 def _():
@@ -138,6 +158,16 @@
 
                     self.copy(d, c, up).start()
 
+            if after is not None:
+                after(slot)
+
+    def start_own(self):
+        width = self.total.shape[1] // STEPS
+
+        @pl.loop(0, STEPS)
+        def _(c):
+            self.total[:, rows_at(c, width)] = self.partial(self.z, c)
+
     def own(self):
         z, n, total = self.z, self.n, self.total
         width = total.shape[1] // STEPS
@@ -145,7 +175,6 @@
         @pl.loop(0, STEPS)
         def _(c):
             at = rows_at(c, width)
-            total[:, at] = self.partial(z, c)
             for there, up in ((z > 0, 1), (z < n - 1, 0)):
 
                 @pl.when(there)
@@ -162,13 +191,6 @@
                 @pl.when(there)
                 def _():
                     self.copy(d, c, up).wait_send()
-
-
-def line_scatter(z, n, partial, land, send_sem, recv_sem, total):
-    line = LineScatter(z, n, partial, land, send_sem, recv_sem, total)
-    line.run(0, n - 1)
-    line.own()
-    line.finish()
 
 
 def line_sems(n):
@@ -195,37 +217,202 @@
     return 1.0 / (1.0 + jnp.exp(-x))
 
 
+def subsets(bits):
+    found = [0]
+    for bit in bits:
+        found += [bit | other for other in found]
+    return found
+
+
+def orders_of(ns):
+    chips = [1 << i for i in range(1, ns.bit_length() - 1)]
+    return (chips, chips[::-1])
+
+
+def remote(src, dst, send, recv, axis, to):
+    return pltpu.make_async_remote_copy(
+        src_ref=src, dst_ref=dst, send_sem=send, recv_sem=recv, device_id={axis: to}, device_id_type=MESH
+    )
+
+
+class CubeGather:
+    def __init__(self, s, ns, buf, rows, send_sem, recv_sem):
+        self.s, self.buf, self.rows, self.send_sem, self.recv_sem = s, buf, rows, send_sem, recv_sem
+        self.orders = [order + [1] for order in orders_of(ns)]
+
+    def copy(self, half, bit, block):
+        part = self.rows // 2
+        at = pl.ds(pl.multiple_of(block * self.rows + half * part, part), part)
+        return remote(
+            self.buf.at[at], self.buf.at[at],
+            self.send_sem.at[bit.bit_length() - 1, block, half], self.recv_sem.at[block, half],
+            "seq", self.s ^ bit,
+        )
+
+    @property
+    def levels(self):
+        return len(self.orders[0])
+
+    def start(self):
+        for i in range(self.levels):
+            for half, order in enumerate(self.orders):
+                self.copy(half, order[i], self.s).start()
+
+    def level(self, i):
+        for j in range(2**i):
+            for half, order in enumerate(self.orders):
+                block = self.s ^ order[i] ^ subsets(order[:i])[j]
+                self.copy(half, order[i], block).wait_recv()
+                for bit in order[i + 1 :]:
+                    self.copy(half, bit, block).start()
+
+    def finish(self):
+        for half, order in enumerate(self.orders):
+            for i, bit in enumerate(order):
+                for other in subsets(order[:i]):
+                    self.copy(half, bit, self.s ^ other).wait_send()
+
+    @staticmethod
+    def sems(ns):
+        dma = pltpu.SemaphoreType.DMA
+        return [dma((ns.bit_length() - 1, ns, 2)), dma((ns, 2))]
+
+
+class CubeScatter:
+    def __init__(self, s, ns, block, rows, first, held, later, sems):
+        self.s, self.block, self.rows = s, block, rows
+        self.first, self.held, self.later = first, held, later
+        self.send0, self.recv0, self.send1, self.recv1 = sems
+        self.orders = orders_of(ns)
+        self.half = ns // 2
+
+    def core_copy(self, j):
+        return remote(self.first.at[j], self.held.at[j], self.send0.at[j], self.recv0.at[j], "seq", self.s ^ 1)
+
+    def send_core(self, j=None):
+        if j is None:
+            pl.loop(0, self.half)(self.send_core)
+            return
+        j = self.half - 1 - j
+        self.first[j] = self.block(self.s ^ (2 * j + 1)).astype(BF16)
+        self.core_copy(j).start()
+
+    def base(self, i):
+        return sum(2 ** (self.stages - 1 - k) for k in range(i))
+
+    def move(self, i, half, slot, other):
+        part = self.rows // 2
+        return remote(
+            self.held.at[(self.orders[half][i] | other) >> 1, pl.ds(half * part, part)],
+            self.later.at[half, slot], self.send1.at[half, slot], self.recv1.at[half, slot],
+            "seq", self.s ^ self.orders[half][i],
+        )
+
+    def moves(self, i):
+        part = self.rows // 2
+        for half, order in enumerate(self.orders):
+            for j, other in enumerate(subsets(order[i + 1 :])):
+                slot = self.base(i) + j
+                yield other >> 1, pl.ds(half * part, part), half, slot, self.move(i, half, slot, other)
+
+    def add_core(self, j=None):
+        if j is None:
+            pl.loop(0, self.half)(self.add_core)
+            return
+        j = self.half - 1 - j
+        mine = self.block(self.s ^ (2 * j))
+        self.core_copy(j).wait_recv()
+        self.held[j] = (self.held[j].astype(F32) + mine).astype(BF16)
+        for half, order in enumerate(self.orders):
+            for slot, other in enumerate(subsets(order[1:])):
+
+                @pl.when(j == (order[0] | other) >> 1)
+                def _():
+                    self.move(0, half, slot, other).start()
+
+    def send(self, i):
+        for *_, copy in self.moves(i):
+            copy.start()
+
+    def take(self, i):
+        for j, at, half, slot, copy in self.moves(i):
+            copy.wait_recv()
+            self.held[j, at] = (self.held[j, at].astype(F32) + self.later[half, slot].astype(F32)).astype(BF16)
+
+    def step(self, i):
+        self.take(i)
+        if i + 1 < self.stages:
+            self.send(i + 1)
+
+    @property
+    def stages(self):
+        return len(self.orders[0])
+
+    def core_sent(self):
+        @pl.loop(0, self.half)
+        def _(j):
+            self.core_copy(j).wait_send()
+
+    def finish(self):
+        for i in range(self.stages):
+            for *_, copy in self.moves(i):
+                copy.wait_send()
+
+    @staticmethod
+    def scratch(ns, rows, width):
+        dma = pltpu.SemaphoreType.DMA
+        half = ns // 2
+        return [
+            pltpu.VMEM((half, rows, width), BF16),
+            pltpu.VMEM((half, rows, width), BF16),
+            pltpu.VMEM((2, half - 1, rows // 2, width), BF16),
+            dma((half,)), dma((half,)), dma((2, half - 1)), dma((2, half - 1)),
+        ]
+
+
 def forward_kernel(
     n, ns,
-    att, tok, cot, wod, wgu, attn_gain, mlp_gain,
-    out, h1r, branch_out, hidden, dy2, dg, du, gain_part,
+    att, tok, cot, w_in, gate, up, down, attn_gain, mlp_gain,
+    out, h1r_out, branch_out, hidden_out, dy2_out, dg_out, du_out, gain_part, up_out,
+    h1r, hidden, dy2, dg, du,
     wo, wd, wg, wu, land, branch, h1, second, g_pre, u_pre,
-    wsem, osem, g1s, g1r, s1s, s1r, g2s, g2r, s2s, s2r,
+    wsem, osem, bsem, g1s, g1r, s1s, s1r, g2s, g2r, s2s, s2r, us, ur, ds, dr,
 ):
-    z = lax.axis_index("head")
+    s, z = lax.axis_index("seq"), lax.axis_index("head")
     rows, depth = tok.shape
-    lw, ff = att.shape[1], hidden.shape[1]
-    col = depth // ns
+    lw, ff = att.shape[1], up.shape[1]
+    block = depth // ns
     width = depth // STEPS
-    line_barrier(z, n)
-    loads = []
-    for s in range(ns):
-        loads.append(pltpu.make_async_copy(wod.at[s, pl.ds(0, lw)], wo.at[:, pl.ds(s * col, col)], wsem.at[0]))
-    l_g = pltpu.make_async_copy(wgu.at[:, pl.ds(0, ff)], wg, wsem.at[1])
-    l_u = pltpu.make_async_copy(wgu.at[:, pl.ds(ff, ff)], wu, wsem.at[2])
-    d_loads = [
-        pltpu.make_async_copy(wod.at[s, pl.ds(lw, ff)], wd.at[:, pl.ds(s * col, col)], wsem.at[3]) for s in range(ns)
-    ]
-    for copy in loads + [l_g, l_u] + d_loads:
+    mine = rows_at(s, block)
+    l_o = pltpu.make_async_copy(w_in.at[:, pl.ds(3 * lw, lw)], wo, wsem.at[0])
+    l_u = pltpu.make_async_copy(up, wu.at[mine], wsem.at[1])
+    l_g = pltpu.make_async_copy(gate, wg, wsem.at[2])
+    for copy in (l_o, l_u, l_g):
         copy.start()
-    for copy in loads:
-        copy.wait()
+    cube_barrier(s, z, ns, n)
+    cube_u = CubeGather(s, ns, wu, block, us, ur)
+    cube_d = CubeGather(s, ns, wd, block, ds, dr)
+    levels = cube_u.levels
+    l_u.wait()
+    cube_u.start()
+    l_o.wait()
 
     def out_part(d, c):
-        return mm(att[rows_at(d, rows), :], wo[:, rows_at(c, width)])
-
-    line_scatter(z, n, out_part, land, s1s, s1r, branch)
-    o_branch = pltpu.make_async_copy(branch, branch_out, osem)
+        return mm(att[rows_at(d, rows), :], wo[rows_at(c, width), :], NT)
+
+    line = LineScatter(z, n, out_part, land, s1s, s1r, branch)
+    line.run(0, STEPS)
+    line.start_own()
+    wd[mine, :] = jnp.transpose(down[...].astype(F32)).astype(BF16)
+    cube_u.level(0)
+    line.run(STEPS, 2 * STEPS)
+    for i in range(1, levels - 1):
+        cube_u.level(i)
+    cube_d.start()
+    line.run(2 * STEPS, line.slots)
+    line.own()
+    line.finish()
+    o_branch = pltpu.make_async_copy(branch, branch_out, osem.at[0])
     o_branch.start()
     gain_part[...] = jnp.zeros_like(gain_part)
 
@@ -237,9 +424,11 @@
         h1[at, :] = h
         h1r[pl.ds(pl.multiple_of(z * rows + i * BLOCK, BLOCK), BLOCK), :] = h.astype(BF16)
 
-    l_g.wait()
-    l_u.wait()
     fw = ff // STEPS
+    o_up = pltpu.make_async_copy(wu, up_out, osem.at[1])
+    o_h1r = pltpu.make_async_copy(h1r, h1r_out, osem.at[2])
+    o_hidden = pltpu.make_async_copy(hidden, hidden_out, osem.at[3])
+    o_dy2 = pltpu.make_async_copy(dy2, dy2_out, osem.at[4])
 
     def up_block(src):
         at = rows_at(src, rows)
@@ -254,14 +443,27 @@
             u_pre[at, cols] = u
             hidden[at, cols] = (g * sigmoid(g) * u).astype(BF16)
 
-    line_gather(z, n, h1r, rows, g1s, g1r, up_block)
-    for copy in d_loads:
-        copy.wait()
+    def weights_there():
+        l_g.wait()
+        cube_u.level(levels - 1)
+        o_up.start()
+
+    hooks = [functools.partial(cube_d.level, i) for i in range(levels)]
+    line_gather(z, n, h1r, rows, g1s, g1r, up_block, hooks[: n - 1], weights_there)
+    for hook in hooks[n - 1 :]:
+        hook()
+    o_h1r.start()
+    o_hidden.start()
 
     def down_part(d, c):
-        return mm(hidden[rows_at(d, rows), :], wd[:, rows_at(c, width)])
-
-    line_scatter(z, n, down_part, land, s2s, s2r, second)
+        return mm(hidden[rows_at(d, rows), :], wd[rows_at(c, width), :], NT)
+
+    line = LineScatter(z, n, down_part, land, s2s, s2r, second)
+    line.run(0, STEPS)
+    line.start_own()
+    line.run(STEPS, line.slots)
+    line.own()
+    line.finish()
 
     @pl.loop(0, rows // BLOCK)
     def _(i):
@@ -282,21 +484,41 @@
         @pl.loop(0, STEPS)
         def _(c):
             cols = rows_at(c, fw)
-            dh = mm(dy2[at, :], wd[cols, :], NT)
+            dh = mm(dy2[at, :], wd[:, cols])
             g = g_pre[at, cols]
             u = u_pre[at, cols]
             sig = sigmoid(g)
             du[at, cols] = (dh * g * sig).astype(BF16)
             dg[at, cols] = (dh * u * sig * (1.0 + g * (1.0 - sig))).astype(BF16)
 
+        for copy in grads_out(src):
+            copy.start()
+
+    def grads_out(src):
+        at = rows_at(src, rows)
+        return [
+            pltpu.make_async_copy(held.at[at], to.at[at], bsem.at[i, src])
+            for i, (held, to) in enumerate(((dg, dg_out), (du, du_out)))
+        ]
+
     line_gather(z, n, dy2, rows, g2s, g2r, back_block)
-    o_branch.wait()
-
-
-def run_forward(n, ns, att, tok, cot, wod, wgu, attn_gain, mlp_gain):
+    o_dy2.start()
+    for copy in (o_branch, o_up, o_h1r, o_hidden, o_dy2):
+        copy.wait()
+
+    @pl.loop(0, n)
+    def _(src):
+        for copy in grads_out(src):
+            copy.wait()
+
+    cube_u.finish()
+    cube_d.finish()
+
+
+def run_forward(n, ns, att, tok, cot, w, gate, up, down, attn_gain, mlp_gain):
     rows, depth = tok.shape
     tl, lw = att.shape
-    ff = wgu.shape[1] // 2
+    ff = up.shape[1]
     dma = pltpu.SemaphoreType.DMA
     sems = line_sems(n)
     shape = jax.ShapeDtypeStruct
@@ -311,12 +533,18 @@
             shape((tl, ff), BF16),
             shape((tl, ff), BF16),
             shape((1, depth), F32),
+            shape((depth, ff), BF16),
         ),
-        in_specs=[VMEM, VMEM, VMEM, ANY, ANY, VMEM, VMEM],
-        out_specs=(VMEM, VMEM, ANY, VMEM, VMEM, VMEM, VMEM, VMEM),
+        in_specs=[VMEM, VMEM, VMEM, ANY, ANY, ANY, VMEM, VMEM, VMEM],
+        out_specs=(VMEM, ANY, ANY, ANY, ANY, ANY, ANY, VMEM, ANY),
         scratch_shapes=[
-            pltpu.VMEM((lw, depth), BF16),
-            pltpu.VMEM((ff, depth), BF16),
+            pltpu.VMEM((tl, depth), BF16),
+            pltpu.VMEM((tl, ff), BF16),
+            pltpu.VMEM((tl, depth), BF16),
+            pltpu.VMEM((tl, ff), BF16),
+            pltpu.VMEM((tl, ff), BF16),
+            pltpu.VMEM((depth, lw), BF16),
+            pltpu.VMEM((depth, ff), BF16),
             pltpu.VMEM((depth, ff), BF16),
             pltpu.VMEM((depth, ff), BF16),
             pltpu.VMEM((2, n, STEPS, rows, depth // STEPS), BF16),
@@ -325,46 +553,96 @@
             pltpu.VMEM((rows, depth), F32),
             pltpu.VMEM((tl, ff), F32),
             pltpu.VMEM((tl, ff), F32),
-            dma((4,)),
-            dma,
+            dma((3,)),
+            dma((5,)),
+            dma((2, n)),
             *sems["gather"], *sems["scatter"], *sems["gather"], *sems["scatter"],
+            *CubeGather.sems(ns), *CubeGather.sems(ns),
         ],
         compiler_params=pltpu.CompilerParams(
             collective_id=1, has_side_effects=True, vmem_limit_bytes=VMEM_BYTES
         ),
         cost_estimate=pl.CostEstimate(flops=18 * 10**9, bytes_accessed=40 * 10**6, transcendentals=2 * 10**6),
         name="feed_forward",
-    )(att, tok, cot, wod, wgu, attn_gain, mlp_gain)
+    )(att, tok, cot, w, gate, up, down, attn_gain, mlp_gain)
 
 
 def backward_kernel(
     n, ns,
-    dg, du, cot, branch, wod, wgu, attn_gain,
-    middle, dy1, datt, gain_part,
-    wo, wg, wu, land, total,
-    wsem, s1s, s1r, g1s, g1r,
+    dg, du, h1r_in, cot, branch, w_in, gate, up, attn_gain,
+    middle, dy1, datt, gain_part, grad_gate, grad_up,
+    h1r, wo, wg, wu, land, total,
+    first, held_g, later_g, held_u, later_u,
+    wsem, osem, s1s, s1r, g1s, g1r,
+    ga, gb, gc, gd, ua, ub, uc, ud,
 ):
-    z = lax.axis_index("head")
+    s, z = lax.axis_index("seq"), lax.axis_index("head")
     rows, depth = cot.shape
     lw, ff = datt.shape[1], dg.shape[1]
-    col = depth // ns
+    block = depth // ns
     width = depth // STEPS
-    line_barrier(z, n)
-    l_g = pltpu.make_async_copy(wgu.at[:, pl.ds(0, ff)], wg, wsem.at[0])
-    l_u = pltpu.make_async_copy(wgu.at[:, pl.ds(ff, ff)], wu, wsem.at[1])
-    loads = [
-        pltpu.make_async_copy(wod.at[s, pl.ds(0, lw)], wo.at[:, pl.ds(s * col, col)], wsem.at[2]) for s in range(ns)
-    ]
-    for copy in [l_g, l_u] + loads:
-        copy.start()
-    l_g.wait()
-    l_u.wait()
+
+    def weights_in(c):
+        at = rows_at(c, width)
+        return [
+            pltpu.make_async_copy(m.at[at], to.at[at], wsem.at[i, c]) for i, (m, to) in enumerate(((gate, wg), (up, wu)))
+        ]
+
+    for c in range(STEPS):
+        for copy in weights_in(c):
+            copy.start()
+    l_h = pltpu.make_async_copy(h1r_in, h1r, osem.at[0])
+    l_o = pltpu.make_async_copy(w_in.at[:, pl.ds(3 * lw, lw)], wo, osem.at[1])
+    l_h.start()
+    l_o.start()
+    cube_barrier(s, z, ns, n)
+
+    def weight_block(grad):
+        return lambda b: mm(h1r[:, rows_at(b, block)], grad[...], TN)
+
+    cube_g = CubeScatter(s, ns, weight_block(dg), block, first, held_g, later_g, (ga, gb, gc, gd))
+    cube_u = CubeScatter(s, ns, weight_block(du), block, first, held_u, later_u, (ua, ub, uc, ud))
 
     def in_part(d, c):
         at, cols = rows_at(d, rows), rows_at(c, width)
         return mm(dg[at, :], wg[cols, :], NT) + mm(du[at, :], wu[cols, :], NT)
 
-    line_scatter(z, n, in_part, land, s1s, s1r, total)
+    line = LineScatter(z, n, in_part, land, s1s, s1r, total)
+    half = ns // 2
+
+    def there(slot):
+        @pl.when(slot < STEPS)
+        def _():
+            for copy in weights_in(slot):
+                copy.wait()
+
+    tasks = (cube_g.send_core, cube_g.add_core, cube_u.send_core)
+    begin = STEPS - 1
+
+    def task(slot):
+        @pl.when(slot == begin)
+        def _():
+            l_h.wait()
+
+        for i, act in enumerate(tasks):
+            low = begin + i * half
+            pl.when((slot >= low) & (slot < low + half))(functools.partial(task_of, act, slot - low, i))
+
+    def task_of(act, j, i):
+        if i == 2:
+            cube_g.core_copy(half - 1 - j).wait_send()
+        act(j)
+
+    line.run(0, 2 * STEPS, there, task)
+    line.start_own()
+    line.run(2 * STEPS, line.slots, None, task)
+
+    @pl.loop(line.slots, begin + 3 * half)
+    def _(slot):
+        task(slot)
+
+    line.own()
+    line.finish()
     gain_part[...] = jnp.zeros_like(gain_part)
 
     @pl.loop(0, rows // BLOCK)
@@ -380,23 +658,37 @@
             e, normed, scale, attn_gain[...]
         ).astype(BF16)
 
-    for copy in loads:
-        copy.wait()
+    l_o.wait()
 
     def att_block(src):
         at = rows_at(src, rows)
-        datt[at, :] = mm(dy1[at, :], wo[...], NT).astype(BF16)
-
-    line_gather(z, n, dy1, rows, g1s, g1r, att_block)
-
-
-def run_backward(n, ns, dg, du, cot, branch, wod, wgu, attn_gain):
+        datt[at, :] = mm(dy1[at, :], wo[...]).astype(BF16)
+
+    def second_cube():
+        cube_u.add_core()
+        cube_g.step(0)
+
+    todo = [functools.partial(cube_g.step, i) for i in range(1, cube_g.stages)]
+    todo += [functools.partial(cube_u.step, i) for i in range(cube_u.stages)]
+    line_gather(z, n, dy1, rows, g1s, g1r, att_block, todo[: n - 1], second_cube)
+    for step in todo[n - 1 :]:
+        step()
+    grad_gate[...] = held_g[0].astype(F32)
+    grad_up[...] = held_u[0].astype(F32)
+    cube_g.finish()
+    cube_u.core_sent()
+    cube_u.finish()
+
+
+def run_backward(n, ns, dg, du, h1r, cot, branch, w, gate, up, attn_gain):
     rows, depth = cot.shape
     tl, ff = dg.shape
-    lw = wod.shape[1] - ff
+    lw = w.shape[1] // 4
+    block = depth // ns
     dma = pltpu.SemaphoreType.DMA
     sems = line_sems(n)
     shape = jax.ShapeDtypeStruct
+    first, held, later, *cube_sems = CubeScatter.scratch(ns, block, ff)
     return pl.pallas_call(
         functools.partial(backward_kernel, n, ns),
         out_shape=(
@@ -404,24 +696,30 @@
             shape((tl, depth), BF16),
             shape((tl, lw), BF16),
             shape((1, depth), F32),
+            shape((block, ff), F32),
+            shape((block, ff), F32),
         ),
-        in_specs=[VMEM, VMEM, VMEM, VMEM, ANY, ANY, VMEM],
-        out_specs=(VMEM, VMEM, VMEM, VMEM),
+        in_specs=[VMEM, VMEM, ANY, VMEM, VMEM, ANY, ANY, ANY, VMEM],
+        out_specs=(VMEM,) * 6,
         scratch_shapes=[
-            pltpu.VMEM((lw, depth), BF16),
+            pltpu.VMEM((tl, depth), BF16),
+            pltpu.VMEM((depth, lw), BF16),
             pltpu.VMEM((depth, ff), BF16),
             pltpu.VMEM((depth, ff), BF16),
             pltpu.VMEM((2, n, STEPS, rows, depth // STEPS), BF16),
             pltpu.VMEM((rows, depth), F32),
-            dma((3,)),
+            first, held, later, held, later,
+            dma((2, STEPS)),
+            dma((2,)),
             *sems["scatter"], *sems["gather"],
+            *cube_sems, *cube_sems,
         ],
         compiler_params=pltpu.CompilerParams(
             collective_id=2, has_side_effects=True, vmem_limit_bytes=VMEM_BYTES
         ),
-        cost_estimate=pl.CostEstimate(flops=10 * 10**9, bytes_accessed=30 * 10**6, transcendentals=0),
+        cost_estimate=pl.CostEstimate(flops=18 * 10**9, bytes_accessed=30 * 10**6, transcendentals=0),
         name="into_attention",
-    )(dg, du, cot, branch, wod, wgu, attn_gain)
+    )(dg, du, h1r, cot, branch, w, gate, up, attn_gain)
 
 
 LOG2E = 1.4426950408889634
@@ -457,9 +755,9 @@
 
 
 def attend_kernel(
-    ns, heads, q_in, k_in, v_in, starts,
-    att, q_buf, k_buf, v_buf, o_buf, lse,
-    o_low, qs, qr, ks, kr, vs, vr, osend, orecv, local,
+    ns, heads, q_in, k_in, v_in, starts, gate,
+    att, q_buf, k_buf, v_buf, o_buf, lse, gate_out,
+    o_low, qs, qr, ks, kr, vs, vr, osend, orecv, local, cs, cr,
 ):
     s = lax.axis_index("seq")
     r = ns // heads
@@ -504,7 +802,10 @@
     own = [pltpu.make_async_copy(x.at[:, head_cols(mine)], buf.at[rows_at(s, tl)], local.at[i])
            for i, (x, buf, _, _) in enumerate(kv)]
     own_q = pltpu.make_async_copy(q_in.at[:, head_cols(mine)], q_buf.at[rows_at(to_row, tl)], local.at[2])
-    for copy in own:
+    block = gate.shape[0]
+    own_gate = pltpu.make_async_copy(gate, gate_out.at[rows_at(s, block)], local.at[4])
+    cube = CubeGather(s, ns, gate_out, block, cs, cr)
+    for copy in own + [own_gate]:
         copy.start()
 
     @pl.when(to_sub == sub)
@@ -577,8 +878,7 @@
 
     own_o = pltpu.make_async_copy(o_low.at[rows_at(to_row, tl)], att.at[:, head_cols(mine)], local.at[3])
 
-    @pl.loop(0, blocks)
-    def _(i):
+    def attend_block(i):
         src = source_of(sub, i, ns, r)
 
         @pl.when(src != s)
@@ -626,6 +926,16 @@
         def _():
             own_o.start()
 
+    own_gate.wait()
+    cube.start()
+    cuts = [0, blocks - 1, blocks, blocks]
+    for i in range(3):
+        pl.loop(cuts[i], cuts[i + 1])(attend_block)
+        if i < 2:
+            cube.level(i)
+    for i in range(2, cube.levels):
+        cube.level(i)
+
     @pl.when(to_sub == sub)
     def _():
         own_o.wait()
@@ -664,8 +974,10 @@
                 kv_copy(x.at[:, head_cols(t // r)], buf, ss.at[0, t], rs, t, s).wait_send()
             pass_on(t, False)
 
-
-def run_attend(ns, heads, q, k, v, starts):
+    cube.finish()
+
+
+def run_attend(ns, heads, q, k, v, starts, gate):
     tl, lw = q.shape
     r = ns // heads
     nq = ns // r * tl
@@ -681,29 +993,32 @@
             shape((nk, HEAD_DIM), BF16),
             shape((nq, HEAD_DIM), F32),
             shape((ns // r, tl), F32),
+            shape((gate.shape[0] * ns, gate.shape[1]), BF16),
         ),
-        in_specs=[VMEM] * 4,
-        out_specs=(VMEM,) * 6,
+        in_specs=[VMEM] * 4 + [ANY],
+        out_specs=(VMEM,) * 6 + (ANY,),
         scratch_shapes=[
             pltpu.VMEM((nq, HEAD_DIM), BF16),
             dma((heads,)), dma((ns // r,)),
             dma((2, ns)), dma((ns,)),
             dma((2, ns)), dma((ns,)),
             dma((ns // r,)), dma((heads,)),
-            dma((4,)),
+            dma((5,)),
+            *CubeGather.sems(ns),
         ],
         compiler_params=pltpu.CompilerParams(
             collective_id=3, has_side_effects=True, vmem_limit_bytes=VMEM_BYTES
         ),
         cost_estimate=pl.CostEstimate(flops=3 * 10**9, bytes_accessed=8 * 10**6, transcendentals=5 * 10**6),
         name="attend",
-    )(q, k, v, starts)
+    )(q, k, v, starts, gate)
 
 
 def attend_back_kernel(
-    ns, heads, do_in, starts, q_buf, k_buf, v_buf, o_buf, lse,
-    dq, dk, dv,
+    ns, heads, do_in, starts, q_buf, k_buf, v_buf, o_buf, lse, dy2, hidden,
+    dq, dk, dv, grad_down,
     do_buf, dq_low, dk_acc, dv_acc, low, pair, land,
+    first, held, later, ca, cb, cc, cd,
     ds_, dr_, ps, pr, gs, gr, qs, qr, local,
 ):
     s = lax.axis_index("seq")
@@ -737,8 +1052,14 @@
         def _():
             do_copy(h).start()
 
+    block = dy2.shape[1] // ns
+    cube = CubeScatter(
+        s, ns, lambda b: mm(dy2[:, rows_at(b, block)], hidden[...], TN), block, first, held, later, (ca, cb, cc, cd)
+    )
+    cube.send_core()
     dk_acc[...] = jnp.zeros_like(dk_acc)
     dv_acc[...] = jnp.zeros_like(dv_acc)
+    cube.add_core()
 
     @pl.when(to_sub == sub)
     def _():
@@ -753,8 +1074,7 @@
     own_dq = pltpu.make_async_copy(dq_low.at[rows_at(to_row, tl)], dq.at[:, head_cols(mine)], local.at[1])
     ones = jnp.ones((8, HEAD_DIM), F32)
 
-    @pl.loop(0, blocks)
-    def _(i):
+    def back_block(i):
         src = source_of(sub, i, ns, r)
         rows = rows_at(i, tl)
 
@@ -798,6 +1118,9 @@
         def _():
             own_dq.start()
 
+    pl.loop(0, blocks - 1)(back_block)
+    cube.step(0)
+    pl.loop(blocks - 1, blocks)(back_block)
     half = ns // 2
 
     def pair_copy(w, i):
@@ -881,8 +1204,14 @@
             def _():
                 back_copy(w, i).wait_send()
 
-
-def run_attend_back(ns, heads, do, starts, q, k, v, o, lse):
+    for i in range(1, cube.stages):
+        cube.step(i)
+    grad_down[...] = jnp.transpose(held[0].astype(F32))
+    cube.core_sent()
+    cube.finish()
+
+
+def run_attend_back(ns, heads, do, starts, q, k, v, o, lse, dy2, hidden):
     tl, lw = do.shape
     r = ns // heads
     nq = ns // r * tl
@@ -891,9 +1220,9 @@
     shape = jax.ShapeDtypeStruct
     return pl.pallas_call(
         functools.partial(attend_back_kernel, ns, heads),
-        out_shape=(shape((tl, lw), BF16),) * 3,
-        in_specs=[VMEM] * 7,
-        out_specs=(VMEM,) * 3,
+        out_shape=(shape((tl, lw), BF16),) * 3 + (shape((hidden.shape[1], dy2.shape[1] // ns), F32),),
+        in_specs=[VMEM] * 9,
+        out_specs=(VMEM,) * 4,
         scratch_shapes=[
             pltpu.VMEM((nq, HEAD_DIM), BF16),
             pltpu.VMEM((nq, HEAD_DIM), BF16),
@@ -902,6 +1231,7 @@
             pltpu.VMEM((2, nk, HEAD_DIM), BF16),
             pltpu.VMEM((2, nk // 2, HEAD_DIM), BF16),
             pltpu.VMEM((2, r // 2, tl, lw), BF16),
+            *CubeScatter.scratch(ns, dy2.shape[1] // ns, hidden.shape[1]),
             dma((heads,)), dma((ns // r,)),
             dma((2, ns // 2)), dma((2, ns // 2)),
             dma((2, ns // 2)), dma((2, heads, r // 2)),
@@ -913,7 +1243,7 @@
         ),
         cost_estimate=pl.CostEstimate(flops=8 * 10**9, bytes_accessed=10 * 10**6, transcendentals=5 * 10**6),
         name="attend_back",
-    )(do, starts, q, k, v, o, lse)
+    )(do, starts, q, k, v, o, lse, dy2, hidden)
 
 
 def cross_barrier(s, z, ns, n):
@@ -926,135 +1256,6 @@
                 pl.semaphore_signal(bar, inc=1, device_id={axis: other}, device_id_type=MESH)
 
     pl.semaphore_wait(bar, ns - 1 + n - 1)
-
-
-def subsets(bits):
-    found = [0]
-    for bit in bits:
-        found += [bit | other for other in found]
-    return found
-
-
-def orders_of(ns):
-    chips = [1 << i for i in range(1, ns.bit_length() - 1)]
-    return (chips, chips[::-1])
-
-
-def remote(src, dst, send, recv, axis, to):
-    return pltpu.make_async_remote_copy(
-        src_ref=src, dst_ref=dst, send_sem=send, recv_sem=recv, device_id={axis: to}, device_id_type=MESH
-    )
-
-
-class CubeGather:
-    def __init__(self, s, ns, buf, rows, send_sem, recv_sem):
-        self.s, self.buf, self.rows, self.send_sem, self.recv_sem = s, buf, rows, send_sem, recv_sem
-        self.orders = [order + [1] for order in orders_of(ns)]
-
-    def copy(self, half, bit, block):
-        part = self.rows // 2
-        at = pl.ds(pl.multiple_of(block * self.rows + half * part, part), part)
-        return remote(
-            self.buf.at[at], self.buf.at[at],
-            self.send_sem.at[bit.bit_length() - 1, block, half], self.recv_sem.at[block, half],
-            "seq", self.s ^ bit,
-        )
-
-    def start(self):
-        for i in range(len(self.orders[0])):
-            for half, order in enumerate(self.orders):
-                self.copy(half, order[i], self.s).start()
-
-    def level(self, i):
-        for j in range(2**i):
-            for half, order in enumerate(self.orders):
-                block = self.s ^ order[i] ^ subsets(order[:i])[j]
-                self.copy(half, order[i], block).wait_recv()
-                for bit in order[i + 1 :]:
-                    self.copy(half, bit, block).start()
-
-    def finish(self):
-        for half, order in enumerate(self.orders):
-            for i, bit in enumerate(order):
-                for other in subsets(order[:i]):
-                    self.copy(half, bit, self.s ^ other).wait_send()
-
-    @staticmethod
-    def sems(ns):
-        dma = pltpu.SemaphoreType.DMA
-        return [dma((ns.bit_length() - 1, ns, 2)), dma((ns, 2))]
-
-
-class CubeScatter:
-    def __init__(self, s, ns, block, rows, first, held, later, sems):
-        self.s, self.block, self.rows = s, block, rows
-        self.first, self.held, self.later = first, held, later
-        self.send0, self.recv0, self.send1, self.recv1 = sems
-        self.orders = orders_of(ns)
-        self.evens = range(0, ns, 2)
-
-    def core_copy(self, j):
-        return remote(self.first.at[j], self.held.at[j], self.send0.at[j], self.recv0.at[j], "seq", self.s ^ 1)
-
-    def send_core(self):
-        @pl.loop(0, len(self.evens))
-        def _(j):
-            self.first[j] = self.block(self.s ^ (2 * j + 1)).astype(BF16)
-            self.core_copy(j).start()
-
-    def moves(self, i):
-        part = self.rows // 2
-        base = sum(2 ** (len(self.orders[0]) - 1 - k) for k in range(i))
-        for half, order in enumerate(self.orders):
-            for j, other in enumerate(subsets(order[i + 1 :])):
-                slot = base + j
-                at = pl.ds(half * part, part)
-                yield other >> 1, at, half, slot, remote(
-                    self.held.at[(order[i] | other) >> 1, at], self.later.at[half, slot],
-                    self.send1.at[half, slot], self.recv1.at[half, slot], "seq", self.s ^ order[i],
-                )
-
-    def add_core(self):
-        @pl.loop(0, len(self.evens))
-        def _(j):
-            mine = self.block(self.s ^ (2 * j))
-            self.core_copy(j).wait_recv()
-            self.held[j] = (self.held[j].astype(F32) + mine).astype(BF16)
-
-        self.send(0)
-
-    def send(self, i):
-        for *_, copy in self.moves(i):
-            copy.start()
-
-    def take(self, i):
-        for j, at, half, slot, copy in self.moves(i):
-            copy.wait_recv()
-            self.held[j, at] = (self.held[j, at].astype(F32) + self.later[half, slot].astype(F32)).astype(BF16)
-
-    @property
-    def stages(self):
-        return len(self.orders[0])
-
-    def finish(self):
-        @pl.loop(0, len(self.evens))
-        def _(j):
-            self.core_copy(j).wait_send()
-
-        for i in range(self.stages):
-            for *_, copy in self.moves(i):
-                copy.wait_send()
-
-    @staticmethod
-    def scratch(ns, rows, width):
-        dma = pltpu.SemaphoreType.DMA
-        half = ns // 2
-        return [
-            pltpu.VMEM((half, rows, width), BF16),
-            pltpu.VMEM((half, rows, width), BF16),
-            pltpu.VMEM((2, half - 1, rows // 2, width), BF16),
-            dma((half,)), dma((half,)), dma((2, half - 1)), dma((2, half - 1)),
-        ]
 
 
 def row_sums(left, right):
@@ -1105,9 +1306,9 @@
 
 def project_kernel(
     n, ns, depth_full,
-    tok, wq, wk, wv, gq, gk, cos, sin,
-    x, w, q_raw, k_raw, totals, q_rot, k_rot, v_low,
-    land, lsem, ags, agr, cgs, cgr, ss, sr,
+    tok, wq, wk, wv, wo, gq, gk, cos, sin,
+    x_out, w_out, q_raw, k_raw, totals, q_rot, k_rot, v_low,
+    x, w, land, lsem, ags, agr, cgs, cgr, ss, sr,
 ):
     s, z = lax.axis_index("seq"), lax.axis_index("head")
     rows, depth = tok.shape
@@ -1132,6 +1333,7 @@
             done.append(i)
 
     def start_weights():
+        w[mine, 3 * lw :] = jnp.transpose(wo[...].astype(F32)).astype(BF16)
         for copy in loads[1:]:
             copy.wait()
         cube.start()
@@ -1140,7 +1342,7 @@
         at = rows_at(src, rows)
         for i, to in enumerate((q_raw, k_raw)):
             to[at, :] = mm(x[at, :], w[:, i * lw : (i + 1) * lw])
-        v_low[at, :] = mm(x[at, :], w[:, 2 * lw :]).astype(BF16)
+        v_low[at, :] = mm(x[at, :], w[:, 2 * lw : 3 * lw]).astype(BF16)
 
     part = rows // AG_CHUNKS
 
@@ -1183,6 +1385,9 @@
             for src, there, _ in sides(k):
                 pl.when(there)(functools.partial(multiply, src))
 
+    outs = [pltpu.make_async_copy(x, x_out, lsem.at[4]), pltpu.make_async_copy(w, w_out, lsem.at[5])]
+    for out in outs:
+        out.start()
     totals[...] = row_sums(q_raw[...] * q_raw[...], k_raw[...] * k_raw[...])
     land[z] = totals[...]
     small = SmallExchange("head", z, n, land, ss, sr)
@@ -1199,6 +1404,8 @@
             to[:, cols] = turn(raw[:, cols] * scale * gain[:, cols], cos[...], sin[...]).astype(BF16)
     small.finish()
     cube.finish()
+    for out in outs:
+        out.wait()
 
     @pl.loop(0, n)
     def _(src):
@@ -1213,7 +1420,7 @@
                 copy(src, c, 1).wait_send()
 
 
-def run_project(n, ns, tok, wq, wk, wv, gq, gk, cos, sin):
+def run_project(n, ns, tok, wq, wk, wv, wo, gq, gk, cos, sin):
     rows, depth = tok.shape
     tl = rows * n
     lw = wq.shape[1]
@@ -1223,7 +1430,7 @@
         functools.partial(project_kernel, n, ns, depth),
         out_shape=(
             shape((tl, depth), BF16),
-            shape((depth, 3 * lw), BF16),
+            shape((depth, 4 * lw), BF16),
             shape((tl, lw), F32),
             shape((tl, lw), F32),
             shape((8, tl), F32),
@@ -1231,11 +1438,13 @@
             shape((tl, lw), BF16),
             shape((tl, lw), BF16),
         ),
-        in_specs=[ANY] * 4 + [VMEM] * 4,
-        out_specs=(VMEM,) * 8,
+        in_specs=[ANY] * 4 + [VMEM] * 5,
+        out_specs=(ANY,) * 2 + (VMEM,) * 6,
         scratch_shapes=[
+            pltpu.VMEM((tl, depth), BF16),
+            pltpu.VMEM((depth, 4 * lw), BF16),
             pltpu.VMEM((n, 8, tl), F32),
-            dma((4,)),
+            dma((6,)),
             dma((2, n, AG_CHUNKS)), dma((n, AG_CHUNKS)),
             *CubeGather.sems(ns),
             dma((n,)), dma((n,)),
@@ -1245,7 +1454,7 @@
         ),
         cost_estimate=pl.CostEstimate(flops=3 * 10**9, bytes_accessed=20 * 10**6, transcendentals=0),
         name="project",
-    )(tok, wq, wk, wv, gq, gk, cos, sin)
+    )(tok, wq, wk, wv, wo, gq, gk, cos, sin)
 
 
 def input_kernel(
@@ -1318,21 +1527,23 @@
         return jnp.concatenate([mm(x[:, cols], dqkv[...], TN), mm(dy1[:, cols], att[...], TN)], axis=1)
 
     def in_part(d, c):
-        return mm(dqkv[rows_at(d, rows), :], w[rows_at(c, width), :], NT)
+        return mm(dqkv[rows_at(d, rows), :], w[rows_at(c, width), : 3 * lw], NT)
 
     cube = CubeScatter(s, ns, weight_block, block, first, held, later, (c0s, c0r, c1s, c1r))
     line = LineScatter(z, n, in_part, land, s1s, s1r, total)
-    cube.send_core()
-    line.run(0, 1)
-    cube.add_core()
-    for j in range(1, n - 1):
-        line.run(j, j + 1)
-        if j - 1 < cube.stages - 1:
-            cube.take(j - 1)
-            cube.send(j)
-    for i in range(max(n - 2, 0), cube.stages - 1):
-        cube.take(i)
-        cube.send(i + 1)
+    half = ns // 2
+
+    def task(slot):
+        for i, act in enumerate((cube.send_core, cube.add_core)):
+            low = 1 + i * half
+            pl.when((slot >= low) & (slot < low + half))(functools.partial(act, slot - low))
+
+    done = 1 + 2 * half
+    line.run(0, done, None, task)
+    line.start_own()
+    line.run(done, line.slots)
+    for i in range(cube.stages - 1):
+        cube.step(i)
 
     each_seq(lambda t: message_copy(t, t).wait_recv())
     received = message_z[0]
@@ -1344,7 +1555,7 @@
     rounds.start()
     line.own()
     grad_in[...] = middle[...] + total[...]
-    cube.take(cube.stages - 1)
+    cube.step(cube.stages - 1)
     for i, to in enumerate((grad_q, grad_k, grad_v)):
         to[...] = held[0, :, i * lw : (i + 1) * lw].astype(F32)
     grad_o[...] = jnp.transpose(held[0, :, 3 * lw :].astype(F32))
@@ -1356,6 +1567,7 @@
     for k in range(1, n):
         both = both + gain_land[k, pl.ds(0, 2), pl.ds(lw, block)]
     gains[2:4, :] = both
+    cube.core_sent()
     cube.finish()
     line.finish()
     small.finish()
@@ -1411,10 +1623,6 @@
     return jnp.concatenate([cos, cos], axis=1), jnp.concatenate([-sin, sin], axis=1)
 
 
-def scatter_grad(grad):
-    return lax.psum_scatter(grad.astype(BF16), "seq", scatter_dimension=0, tiled=True)
-
-
 def on_device(
     tokens,
     cotangent,
@@ -1445,22 +1653,23 @@
     gq = lax.dynamic_slice_in_dim(q_gain, head_index * lw, lw)[None]
     gk = lax.dynamic_slice_in_dim(k_gain, head_index * lw, lw)[None]
 
-    w_od = lax.all_gather(jnp.concatenate([o_weight, down_weight], axis=0), "seq", axis=0)
-    w_gu = lax.all_gather(jnp.concatenate([gate_weight, up_weight], axis=1), "seq", axis=0, tiled=True)
-    x, w_qkv, q_raw, k_raw, totals, q_rot, k_rot, v_low = run_project(
-        nz, ns, tokens, q_weight, k_weight, v_weight, gq, gk, cos, sin
+    x, w, q_raw, k_raw, totals, q_rot, k_rot, v_low = run_project(
+        nz, ns, tokens, q_weight, k_weight, v_weight, o_weight, gq, gk, cos, sin
     )
-    attended, q_held, k_held, v_held, o_held, lse = run_attend(ns, heads, q_rot, k_rot, v_low, starts)
-    output, h1r, branch, hidden, dy2, dg, du, mlp_part = run_forward(
-        nz, ns, attended, tokens, cotangent, w_od, w_gu, attn_gain[None], mlp_gain[None]
+    attended, q_held, k_held, v_held, o_held, lse, gate = run_attend(
+        ns, heads, q_rot, k_rot, v_low, starts, gate_weight
     )
-    grad_gate = scatter_grad(mm(h1r, dg, TN))
-    grad_up = scatter_grad(mm(h1r, du, TN))
-    grad_down = scatter_grad(mm(dy2, hidden, TN))
-    middle, dy1, datt, attn_part = run_backward(nz, ns, dg, du, cotangent, branch, w_od, w_gu, attn_gain[None])
-    dq, dk, dv = run_attend_back(ns, heads, datt, starts, q_held, k_held, v_held, o_held, lse)
+    output, h1r, branch, hidden, dy2, dg, du, mlp_part, up = run_forward(
+        nz, ns, attended, tokens, cotangent, w, gate, up_weight, down_weight, attn_gain[None], mlp_gain[None]
+    )
+    middle, dy1, datt, attn_part, grad_gate, grad_up = run_backward(
+        nz, ns, dg, du, h1r, cotangent, branch, w, gate, up, attn_gain[None]
+    )
+    dq, dk, dv, grad_down = run_attend_back(
+        ns, heads, datt, starts, q_held, k_held, v_held, o_held, lse, dy2, hidden
+    )
     input_grad, grad_q, grad_k, grad_v, grad_o, gains = run_input(
-        nz, ns, dq, dk, dv, q_raw, k_raw, totals, gq, gk, cos, sin, x, w_qkv, middle, attended, dy1, attn_part, mlp_part
+        nz, ns, dq, dk, dv, q_raw, k_raw, totals, gq, gk, cos, sin, x, w, middle, attended, dy1, attn_part, mlp_part
     )
     return (
         output,
@@ -1469,9 +1678,9 @@
         grad_k,
         grad_v,
         grad_o,
-        grad_gate.astype(F32),
-        grad_up.astype(F32),
-        grad_down.astype(F32).T,
+        grad_gate,
+        grad_up,
+        grad_down,
         gains[0],
         gains[1],
         gains[2],

time: 683 us -> 589 us (0.86)
  waiting for transfers between devices: 66.5 us -> 0 us
  matrix products: 27.3 us -> 0 us
  Pallas kernels: 538 us -> 557 us
  between operations: 14.4 us -> 1.19 us
  other arithmetic: 14.3 us -> 5.06 us
    all_gather x2 -> x0, waiting for transfers between devices: 66.4 us -> none  [the longest x1 66.4 us: on_device(): lax.all_gather(jnp.concatenate([gate_weight, up_weight], axis=1), 'seq',...]
    pallas_call x1, Pallas kernels: 41.4 us -> 82.9 us  [run_attend(): pl.pallas_call(functools.partial(attend_kernel, ns, heads), out_shape=(sh...]
    pallas_call x1, Pallas kernels: 108 us -> 73.8 us  [run_input(): pl.pallas_call(functools.partial(input_kernel, n, ns, depth), out_shape=(...]
    dot_general x3 -> x0, matrix products: 27.3 us -> none  [mm(): return lax.dot_general(left, right, dims, preferred_element_type=F32)]
    pallas_call x1, Pallas kernels: 46.3 us -> 66.3 us  [run_attend_back(): pl.pallas_call(functools.partial(attend_back_kernel, ns, heads), out_shap...]
    pallas_call x1, Pallas kernels: 67.1 us -> 56.4 us  [run_project(): pl.pallas_call(functools.partial(project_kernel, n, ns, depth), out_shape...]
  transfers between devices with their start and end apart: 5 -> 0, of which waited for: 1 -> 0; matrix products, arithmetic and copies ran while one was open for 5% -> 0% of each run, Pallas kernels for 54% -> 0%
where the time goes in v4:
time: 589 us; the launch traced here: 580 us
  Pallas kernels  557 us (95%)
  local copies, waits for them, and re-layouts  16.5 us (3%)
    pallas_call x1, Pallas kernels, run_forward(): pl.pallas_call(functools.partial(forward_kernel, n, ns), out_shape=(shape...  167 us
    pallas_call x1, Pallas kernels, run_backward(): pl.pallas_call(functools.partial(backward_kernel, n, ns), out_shape=(shap...  111 us
    pallas_call x1, Pallas kernels, run_attend(): pl.pallas_call(functools.partial(attend_kernel, ns, heads), out_shape=(sh...  82.9 us
    pallas_call x1, Pallas kernels, run_input(): pl.pallas_call(functools.partial(input_kernel, n, ns, depth), out_shape=(...  73.8 us
    pallas_call x1, Pallas kernels, run_attend_back(): pl.pallas_call(functools.partial(attend_back_kernel, ns, heads), out_shap...  66.3 us
    pallas_call x1, Pallas kernels, run_project(): pl.pallas_call(functools.partial(project_kernel, n, ns, depth), out_shape...  56.4 us
    unnamed x25, local copies, waits for them, and re-layouts  12.4 us

profile of v4, /device:TPU:8, one launch (start us, length us, event | category | flops | bytes accessed | tf_op | source)
XLA Modules:
  0.0 579.6 jit_solution(3030952214250604133)
XLA Ops:
  0.7 0.1 add_multiply_fusion
  0.7 0.8 reduce-window.8
  1.6 1.3 dynamic_slice.6
  2.9 1.3 dynamic_slice.7
  4.3 0.7 select_reduce_fusion.1
  5.0 0.1 iota_add_fusion
  5.1 1.3 select_reduce_fusion.starts
  6.4 1.0 fusion
  7.4 1.0 pad_maximum_fusion
  8.4 56.4 %project.1 = (bf16[512,2048]{1,0:T(8,128)(2,1)}, bf16[2048,2048]{1,0:T(8,128)(2,1)}, f32[512,512]{1,0:T(8,128)}, f32[512,512]{1,0:T(8,128)}, f32[8,512]{1,0:T(8,...) custom-call(bf16[128,2048]{1,0:T(8,128)(2,1)} %tok.3, bf16[256,512]{1,0:T(8,128)(2,1)} %wq.1, ...), custom_call_target="tpu_custom_call" | custom-call | flops 3000000000 | bytes 20000000 | tf_op jit(solution)/shard_map/project/pallas_call | solution.py:1429
  64.8 82.9 %attend.1 = (bf16[512,512]{1,0:T(8,128)(2,1)}, bf16[2048,128]{1,0:T(8,128)(2,1)}, bf16[4096,128]{1,0:T(8,128)(2,1)}, bf16[4096,128]{1,0:T(8,128)(2,1)}, f32[2048...) custom-call(bf16[512,512]{1,0:T(8,128)(2,1)} %get-tuple-element.53.q_in, ...), custom_call_target="tpu_custom_call" | custom-call | flops 3000000000 | bytes 8000000 | tf_op jit(solution)/shard_map/attend/pallas_call | solution.py:987
  147.7 166.7 %feed_forward.1 = (bf16[128,2048]{1,0:T(8,128)(2,1)}, bf16[512,2048]{1,0:T(8,128)(2,1)}, f32[128,2048]{1,0:T(8,128)}, bf16[512,2048]{1,0:T(8,128)(2,1)}, bf16[51...) custom-call(bf16[512,512]{1,0:T(8,128)(2,1)} %get-tuple-element.56.a, ...), custom_call_target="tpu_custom_call" | custom-call | flops 17999998976 | bytes 40000000 | tf_op jit(solution)/shard_map/feed_forward/pallas_call | solution.py:525
  314.4 110.9 %into_attention.1 = (f32[128,2048]{1,0:T(8,128)}, bf16[512,2048]{1,0:T(8,128)(2,1)}, bf16[512,512]{1,0:T(8,128)(2,1)}, f32[1,2048]{1,0:T(1,128)}, f32[256,2048]{1,0:T(8,128)}, /*index=5*/f32[256,2048]{1,0:T(8,128)}) custom-call(bf16[512,2048]{1,0:T(8,128)(2,1)} %get-tuple-element.60.dg, bf16[512,2048]{1,0:T(8,128)(2,1)} %get-tuple-element.61.du, ...), custom_call_target="tpu_custom_call" | custom-call | flops 17999998976 | bytes 30000000 | tf_op jit(solution)/shard_map/into_attention/pallas_call | solution.py:692
  425.3 66.3 %attend_back.1 = (bf16[512,512]{1,0:T(8,128)(2,1)}, bf16[512,512]{1,0:T(8,128)(2,1)}, bf16[512,512]{1,0:T(8,128)(2,1)}, f32[2048,256]{1,0:T(8,128)}) custom-call(bf16[512,512]{1,0:T(8,128)(2,1)} %get-tuple-element.65.do_in, s32[4,512]{1,0:T(4,128)} %select_reduce_fusion.starts, bf16[2048,128]{1,0:T(8,128)(2,1)} %get-tuple-element.66.q_buf, ...), custom_call_target="tpu_custom_call" | custom-call | flops 8000000000 | bytes 10000000 | tf_op jit(solution)/shard_map/attend_back/pallas_call | solution.py:1221
  491.5 0.0 copy-start.3
  491.5 73.8 %into_input.1 = (f32[128,2048]{1,0:T(8,128)}, f32[256,512]{1,0:T(8,128)}, f32[256,512]{1,0:T(8,128)}, f32[256,512]{1,0:T(8,128)}, f32[512,256]{1,0:T(8,128)}, /*index=5*/f32[8,256]{1,0:T(8,128)}) custom-call(bf16[512,512]{1,0:T(8,128)(2,1)} %get-tuple-element.73.dq, bf16[512,512]{1,0:T(8,128)(2,1)} %get-tuple-element.74.dk, ...), custom_call_target="tpu_custom_call" | custom-call | flops 8000000000 | bytes 30000000 | tf_op jit(solution)/shard_map/into_input/pallas_call | solution.py:1583
  565.3 0.0 copy-start.7
  565.4 1.4 fusion.1
  566.8 0.0 copy-done.3
  566.8 0.0 copy-start.6
  566.8 0.8 copy.36
  567.6 0.0 copy-start.5
  567.6 2.4 copy.37
  569.9 0.0 copy-done.7
  569.9 0.0 copy-start.4
  569.9 0.0 copy-start.1
  569.9 0.8 copy.38
  570.7 0.0 copy-done.6
  570.7 0.8 copy.39
  571.5 0.0 copy-done.5
  571.5 0.8 copy.40
  572.3 0.0 copy-done.4
  572.3 0.8 copy.41
  573.1 0.0 copy-done.1
  573.1 0.0 copy-start
  573.1 1.3 copy.42
  574.5 1.0 copy-done
  575.5 0.0 copy-start.2
  575.5 1.3 copy.43
  576.8 1.0 copy-done.2
  577.8 1.3 copy.44
  (3 shorter events, 0.0 us)
Async XLA Ops:
  491.5 75.3 %copy-start.3 = (bf16[128,2048]{1,0:T(8,128)(2,1)S(1)}, bf16[128,2048]{1,0:T(8,128)(2,1)}, u32[]{:S(2)}) copy-start(bf16[128,2048]{1,0:T(8,128)(2,1)} %get-tuple-element.115) | copy-start | bytes 1572868
  565.3 4.6 copy-start.7
  566.8 4.0 copy-start.6
  567.6 4.0 copy-start.5
  569.9 2.4 copy-start.4
  569.9 3.2 copy-start.1
  573.1 2.3 copy-start
  575.5 2.3 copy-start.2

commit v5 on v4

--- a/solution.py
+++ b/solution.py
@@ -33,7 +33,7 @@
     return pl.ds(pl.multiple_of(index * count, count), count)
 
 
-def cube_barrier(s, z, ns, n):
+def cube_barrier(s, z, ns, n, between=None):
     bar = pltpu.get_barrier_semaphore()
     bits = [1 << i for i in range(ns.bit_length() - 1)]
     for bit in bits:
@@ -44,6 +44,8 @@
         def _():
             pl.semaphore_signal(bar, inc=1, device_id={"head": other}, device_id_type=MESH)
 
+    if between is not None:
+        between()
     pl.semaphore_wait(bar, len(bits) + (z > 0).astype(jnp.int32) + (z < n - 1).astype(jnp.int32))
 
 
@@ -236,15 +238,19 @@
 
 
 class CubeGather:
-    def __init__(self, s, ns, buf, rows, send_sem, recv_sem):
+    def __init__(self, s, ns, buf, rows, send_sem, recv_sem, own=None):
+        self.own = own
         self.s, self.buf, self.rows, self.send_sem, self.recv_sem = s, buf, rows, send_sem, recv_sem
         self.orders = [order + [1] for order in orders_of(ns)]
 
     def copy(self, half, bit, block):
         part = self.rows // 2
         at = pl.ds(pl.multiple_of(block * self.rows + half * part, part), part)
+        source = self.buf.at[at]
+        if block is self.s and self.own is not None:
+            source = self.own.at[pl.ds(half * part, part)]
         return remote(
-            self.buf.at[at], self.buf.at[at],
+            source, self.buf.at[at],
             self.send_sem.at[bit.bit_length() - 1, block, half], self.recv_sem.at[block, half],
             "seq", self.s ^ bit,
         )
@@ -270,7 +276,7 @@
         for half, order in enumerate(self.orders):
             for i, bit in enumerate(order):
                 for other in subsets(order[:i]):
-                    self.copy(half, bit, self.s ^ other).wait_send()
+                    self.copy(half, bit, self.s ^ other if other else self.s).wait_send()
 
     @staticmethod
     def sems(ns):
@@ -616,31 +622,33 @@
             for copy in weights_in(slot):
                 copy.wait()
 
-    tasks = (cube_g.send_core, cube_g.add_core, cube_u.send_core)
-    begin = STEPS - 1
-
     def task(slot):
-        @pl.when(slot == begin)
+        @pl.when(slot == 1)
         def _():
             l_h.wait()
 
-        for i, act in enumerate(tasks):
-            low = begin + i * half
-            pl.when((slot >= low) & (slot < low + half))(functools.partial(task_of, act, slot - low, i))
-
-    def task_of(act, j, i):
-        if i == 2:
+        def during(phase, act):
+            low = 1 + phase * half
+            pl.when((slot >= low) & (slot < low + half))(lambda: act(slot - low))
+
+        def send_second(j):
             cube_g.core_copy(half - 1 - j).wait_send()
-        act(j)
+            cube_u.send_core(j)
+
+        during(0, cube_g.send_core)
+        during(1, cube_g.add_core)
+        during(1, send_second)
+        during(2, cube_u.add_core)
 
     line.run(0, 2 * STEPS, there, task)
     line.start_own()
     line.run(2 * STEPS, line.slots, None, task)
 
-    @pl.loop(line.slots, begin + 3 * half)
+    @pl.loop(line.slots, max(line.slots, 1 + 3 * half))
     def _(slot):
         task(slot)
 
+    cube_g.step(0)
     line.own()
     line.finish()
     gain_part[...] = jnp.zeros_like(gain_part)
@@ -664,17 +672,12 @@
         at = rows_at(src, rows)
         datt[at, :] = mm(dy1[at, :], wo[...]).astype(BF16)
 
-    def second_cube():
-        cube_u.add_core()
-        cube_g.step(0)
-
-    todo = [functools.partial(cube_g.step, i) for i in range(1, cube_g.stages)]
-    todo += [functools.partial(cube_u.step, i) for i in range(cube_u.stages)]
-    line_gather(z, n, dy1, rows, g1s, g1r, att_block, todo[: n - 1], second_cube)
+    todo = [functools.partial(cube.step, i) for i in range(1, cube_g.stages) for cube in (cube_g, cube_u)]
+    line_gather(z, n, dy1, rows, g1s, g1r, att_block, todo[: n - 1], functools.partial(cube_u.step, 0))
     for step in todo[n - 1 :]:
         step()
-    grad_gate[...] = held_g[0].astype(F32)
-    grad_up[...] = held_u[0].astype(F32)
+    grad_gate[...] = held_g[0]
+    grad_up[...] = held_u[0]
     cube_g.finish()
     cube_u.core_sent()
     cube_u.finish()
@@ -696,8 +699,8 @@
             shape((tl, depth), BF16),
             shape((tl, lw), BF16),
             shape((1, depth), F32),
-            shape((block, ff), F32),
-            shape((block, ff), F32),
+            shape((block, ff), BF16),
+            shape((block, ff), BF16),
         ),
         in_specs=[VMEM, VMEM, ANY, VMEM, VMEM, ANY, ANY, ANY, VMEM],
         out_specs=(VMEM,) * 6,
@@ -726,7 +729,7 @@
 NEG = -1e30
 
 
-def seq_barrier(s, ns):
+def seq_barrier(s, ns, between=None):
     bar = pltpu.get_barrier_semaphore()
     for other in range(ns):
 
@@ -734,6 +737,8 @@
         def _():
             pl.semaphore_signal(bar, inc=1, device_id={"seq": other}, device_id_type=MESH)
 
+    if between is not None:
+        between()
     pl.semaphore_wait(bar, ns - 1)
 
 
@@ -765,8 +770,17 @@
     tl = q_in.shape[0]
     mine, sub = s // r, s % r
     parity = s % 2
-    seq_barrier(s, ns)
     to_sub, to_row = share_of(s, ns, r)
+
+    def own_rows():
+        for x, buf in ((k_in, k_buf), (v_in, v_buf)):
+            buf[rows_at(s, tl), :] = x[:, head_cols(mine)]
+
+        @pl.when(to_sub == sub)
+        def _():
+            q_buf[rows_at(to_row, tl), :] = q_in[:, head_cols(mine)]
+
+    seq_barrier(s, ns, own_rows)
 
     def q_copy(h):
         return pltpu.make_async_remote_copy(
@@ -799,18 +813,10 @@
         )
 
     kv = ((k_in, k_buf, ks, kr), (v_in, v_buf, vs, vr))
-    own = [pltpu.make_async_copy(x.at[:, head_cols(mine)], buf.at[rows_at(s, tl)], local.at[i])
-           for i, (x, buf, _, _) in enumerate(kv)]
-    own_q = pltpu.make_async_copy(q_in.at[:, head_cols(mine)], q_buf.at[rows_at(to_row, tl)], local.at[2])
     block = gate.shape[0]
-    own_gate = pltpu.make_async_copy(gate, gate_out.at[rows_at(s, block)], local.at[4])
-    cube = CubeGather(s, ns, gate_out, block, cs, cr)
-    for copy in own + [own_gate]:
-        copy.start()
-
-    @pl.when(to_sub == sub)
-    def _():
-        own_q.start()
+    own_gate = pltpu.make_async_copy(gate, gate_out.at[rows_at(s, block)], local.at[0])
+    cube = CubeGather(s, ns, gate_out, block, cs, cr, gate)
+    own_gate.start()
 
     def far(t):
         return (t != s) & (t % 2 == parity)
@@ -829,9 +835,6 @@
         @pl.when(h * r + to_sub != s)
         def _():
             q_copy(h).start()
-
-    for copy in own:
-        copy.wait()
 
     def pass_on(src, start):
         for _, buf, ss, rs in kv:
@@ -859,10 +862,6 @@
         def _():
             for x, buf, ss, rs in kv:
                 kv_copy(buf.at[rows_at(src, tl)], buf, ss.at[0, 0], rs, s ^ 1, src).wait_recv()
-
-    @pl.when(to_sub == sub)
-    def _():
-        own_q.wait()
 
     unit = HEAD_DIM ** (-0.5) * LOG2E
 
@@ -875,8 +874,6 @@
             device_id={"seq": t},
             device_id_type=MESH,
         )
-
-    own_o = pltpu.make_async_copy(o_low.at[rows_at(to_row, tl)], att.at[:, head_cols(mine)], local.at[3])
 
     def attend_block(i):
         src = source_of(sub, i, ns, r)
@@ -924,9 +921,8 @@
 
         @pl.when(src == s)
         def _():
-            own_o.start()
-
-    own_gate.wait()
+            att[:, head_cols(mine)] = o.astype(BF16)
+
     cube.start()
     cuts = [0, blocks - 1, blocks, blocks]
     for i in range(3):
@@ -936,9 +932,7 @@
     for i in range(2, cube.levels):
         cube.level(i)
 
-    @pl.when(to_sub == sub)
-    def _():
-        own_o.wait()
+    own_gate.wait()
 
     @pl.loop(0, heads)
     def _(h):
@@ -995,7 +989,7 @@
             shape((ns // r, tl), F32),
             shape((gate.shape[0] * ns, gate.shape[1]), BF16),
         ),
-        in_specs=[VMEM] * 4 + [ANY],
+        in_specs=[VMEM] * 5,
         out_specs=(VMEM,) * 6 + (ANY,),
         scratch_shapes=[
             pltpu.VMEM((nq, HEAD_DIM), BF16),
@@ -1003,7 +997,7 @@
             dma((2, ns)), dma((ns,)),
             dma((2, ns)), dma((ns,)),
             dma((ns // r,)), dma((heads,)),
-            dma((5,)),
+            dma((1,)),
             *CubeGather.sems(ns),
         ],
         compiler_params=pltpu.CompilerParams(
@@ -1019,7 +1013,7 @@
     dq, dk, dv, grad_down,
     do_buf, dq_low, dk_acc, dv_acc, low, pair, land,
     first, held, later, ca, cb, cc, cd,
-    ds_, dr_, ps, pr, gs, gr, qs, qr, local,
+    ds_, dr_, ps, pr, gs, gr, qs, qr,
 ):
     s = lax.axis_index("seq")
     r = ns // heads
@@ -1027,7 +1021,12 @@
     tl = do_in.shape[0]
     mine, sub = s // r, s % r
     parity = s % 2
-    seq_barrier(s, ns)
+
+    def clear():
+        dk_acc[...] = jnp.zeros_like(dk_acc)
+        dv_acc[...] = jnp.zeros_like(dv_acc)
+
+    seq_barrier(s, ns, clear)
     to_sub, to_row = share_of(s, ns, r)
 
     def copy(src, dst, send, recv, t):
@@ -1039,12 +1038,6 @@
         return copy(
             do_in.at[:, head_cols(h)], do_buf.at[rows_at(to_row, tl)], ds_.at[h], dr_.at[to_row], h * r + to_sub
         )
-
-    own_do = pltpu.make_async_copy(do_in.at[:, head_cols(mine)], do_buf.at[rows_at(to_row, tl)], local.at[0])
-
-    @pl.when(to_sub == sub)
-    def _():
-        own_do.start()
 
     @pl.loop(0, heads)
     def _(h):
@@ -1057,13 +1050,11 @@
         s, ns, lambda b: mm(dy2[:, rows_at(b, block)], hidden[...], TN), block, first, held, later, (ca, cb, cc, cd)
     )
     cube.send_core()
-    dk_acc[...] = jnp.zeros_like(dk_acc)
-    dv_acc[...] = jnp.zeros_like(dv_acc)
     cube.add_core()
 
     @pl.when(to_sub == sub)
     def _():
-        own_do.wait()
+        do_buf[rows_at(to_row, tl), :] = do_in[:, head_cols(mine)]
 
     scale = HEAD_DIM ** (-0.5)
     unit = scale * LOG2E
@@ -1071,7 +1062,6 @@
     def dq_copy(i, t):
         return copy(dq_low.at[rows_at(i, tl)], dq.at[:, head_cols(mine)], qs.at[i], qr.at[mine], t)
 
-    own_dq = pltpu.make_async_copy(dq_low.at[rows_at(to_row, tl)], dq.at[:, head_cols(mine)], local.at[1])
     ones = jnp.ones((8, HEAD_DIM), F32)
 
     def back_block(i):
@@ -1116,7 +1106,7 @@
 
         @pl.when(src == s)
         def _():
-            own_dq.start()
+            dq[:, head_cols(mine)] = dq_low[rows, :]
 
     pl.loop(0, blocks - 1)(back_block)
     cube.step(0)
@@ -1176,10 +1166,6 @@
             lambda a, b: a + b, [land[w, k].astype(F32) for k in range(r // 2)]
         ).astype(BF16)
 
-    @pl.when(to_sub == sub)
-    def _():
-        own_dq.wait()
-
     @pl.loop(0, heads)
     def _(h):
         @pl.when(h * r + to_sub != s)
@@ -1206,7 +1192,7 @@
 
     for i in range(1, cube.stages):
         cube.step(i)
-    grad_down[...] = jnp.transpose(held[0].astype(F32))
+    grad_down[...] = jnp.transpose(held[0].astype(F32)).astype(BF16)
     cube.core_sent()
     cube.finish()
 
@@ -1220,7 +1206,7 @@
     shape = jax.ShapeDtypeStruct
     return pl.pallas_call(
         functools.partial(attend_back_kernel, ns, heads),
-        out_shape=(shape((tl, lw), BF16),) * 3 + (shape((hidden.shape[1], dy2.shape[1] // ns), F32),),
+        out_shape=(shape((tl, lw), BF16),) * 3 + (shape((hidden.shape[1], dy2.shape[1] // ns), BF16),),
         in_specs=[VMEM] * 9,
         out_specs=(VMEM,) * 4,
         scratch_shapes=[
@@ -1236,7 +1222,6 @@
             dma((2, ns // 2)), dma((2, ns // 2)),
             dma((2, ns // 2)), dma((2, heads, r // 2)),
             dma((ns // r,)), dma((heads,)),
-            dma((2,)),
         ],
         compiler_params=pltpu.CompilerParams(
             collective_id=4, has_side_effects=True, vmem_limit_bytes=VMEM_BYTES
@@ -1246,7 +1231,7 @@
     )(do, starts, q, k, v, o, lse, dy2, hidden)
 
 
-def cross_barrier(s, z, ns, n):
+def cross_barrier(s, z, ns, n, between=None):
     bar = pltpu.get_barrier_semaphore()
     for axis, me, count in (("seq", s, ns), ("head", z, n)):
         for other in range(count):
@@ -1255,6 +1240,8 @@
             def _():
                 pl.semaphore_signal(bar, inc=1, device_id={axis: other}, device_id_type=MESH)
 
+    if between is not None:
+        between()
     pl.semaphore_wait(bar, ns - 1 + n - 1)
 
 
@@ -1316,6 +1303,10 @@
     heads = lw // HEAD_DIM
     cross_barrier(s, z, ns, n)
     mine = rows_at(s, block)
+
+    def head_gain(h):
+        return head_cols(z * heads + h)
+
     loads = [pltpu.make_async_copy(tok, x.at[rows_at(z, rows)], lsem.at[0])] + [
         pltpu.make_async_copy(m, w.at[mine, pl.ds(i * lw, lw)], lsem.at[i + 1]) for i, m in enumerate((wq, wk, wv))
     ]
@@ -1401,7 +1392,7 @@
         scale = lax.rsqrt(as_column(total, row) / depth_full + epsilon)
         for h in range(heads):
             cols = slice(h * HEAD_DIM, (h + 1) * HEAD_DIM)
-            to[:, cols] = turn(raw[:, cols] * scale * gain[:, cols], cos[...], sin[...]).astype(BF16)
+            to[:, cols] = turn(raw[:, cols] * scale * gain[:, head_gain(h)], cos[...], sin[...]).astype(BF16)
     small.finish()
     cube.finish()
     for out in outs:
@@ -1459,42 +1450,50 @@
 
 def input_kernel(
     n, ns, depth_full,
-    dq, dk, dv, q_raw, k_raw, totals, gq, gk, cos, sin, x, w, middle, att, dy1, attn_part, mlp_part,
-    grad_in, grad_q, grad_k, grad_v, grad_o, gains,
-    dqkv, q_back, k_back, inner, land, total, message, message_z, gain_land,
+    dq, dk, dv, q_raw, k_raw, totals, gq, gk, cos, sin, x, w, att, dy1, attn_part, mlp_part,
+    total, grad_q, grad_k, grad_v, grad_o, gains,
+    dqkv, q_back, k_back, inner, land, message, message_z, gain_land,
     first, held, later, c0s, c0r, c1s, c1r,
+    first_o, held_o, later_o, o0s, o0r, o1s, o1r,
     ss, sr, ms, mr, zs, zr, s1s, s1r,
 ):
     s, z = lax.axis_index("seq"), lax.axis_index("head")
-    rows, depth = grad_in.shape
+    rows, depth = total.shape
     tl, lw = dq.shape
     block = depth // ns
     heads = lw // HEAD_DIM
-    cross_barrier(s, z, ns, n)
+
+    def head_gain(h):
+        return head_cols(z * heads + h)
+
     sums = totals[...]
     scales = [lax.rsqrt(as_column(sums, row) / depth_full + epsilon) for row in (0, 4)]
     todo = ((dq, q_raw, gq, q_back), (dk, k_raw, gk, k_back))
-    message[...] = jnp.zeros_like(message)
     products = []
-    for i, (grad, raw, gain, back) in enumerate(todo):
-        product = jnp.zeros((tl, HEAD_DIM), F32)
-        for h in range(heads):
-            cols = slice(h * HEAD_DIM, (h + 1) * HEAD_DIM)
-            hat = raw[:, cols] * scales[i]
-            turned = turn_back(grad[:, cols].astype(F32), cos[...], sin[...])
-            message[0, pl.ds(i, 1), cols] = jnp.sum(turned * hat, axis=0, keepdims=True)
-            turned = turned * gain[:, cols]
-            back[:, cols] = turned
-            product = product + turned * hat
-        products.append(product)
-    inner[z] = row_sums(*products)
+
+    def turn_all():
+        message[...] = jnp.zeros_like(message)
+        for i, (grad, raw, gain, back) in enumerate(todo):
+            product = jnp.zeros((tl, HEAD_DIM), F32)
+            for h in range(heads):
+                cols = slice(h * HEAD_DIM, (h + 1) * HEAD_DIM)
+                hat = raw[:, cols] * scales[i]
+                turned = turn_back(grad[:, cols].astype(F32), cos[...], sin[...])
+                message[0, pl.ds(i, 1), cols] = jnp.sum(turned * hat, axis=0, keepdims=True)
+                turned = turned * gain[:, head_gain(h)]
+                back[:, cols] = turned
+                product = product + turned * hat
+            products.append(product)
+        inner[z] = row_sums(*products)
+        for t in range(1, ns):
+            message[t, pl.ds(0, 2), pl.ds(0, lw)] = message[0, pl.ds(0, 2), pl.ds(0, lw)]
+        for t in range(ns):
+            for i, part in enumerate((attn_part, mlp_part)):
+                message[t, pl.ds(i, 1), pl.ds(lw, block)] = part[:, t * block : (t + 1) * block]
+
+    cross_barrier(s, z, ns, n, turn_all)
     small = SmallExchange("head", z, n, inner, ss, sr)
     small.start()
-    for t in range(1, ns):
-        message[t, pl.ds(0, 2), pl.ds(0, lw)] = message[0, pl.ds(0, 2), pl.ds(0, lw)]
-    for t in range(ns):
-        for i, part in enumerate((attn_part, mlp_part)):
-            message[t, pl.ds(i, 1), pl.ds(lw, block)] = part[:, t * block : (t + 1) * block]
 
     def message_copy(t, frm):
         return remote(message.at[t], message_z.at[frm], ms.at[t], mr.at[frm], "seq", t)
@@ -1509,6 +1508,11 @@
     message_z[s] = message[s]
     each_seq(lambda t: message_copy(t, s).start())
     dqkv[:, 2 * lw :] = dv[...]
+    cube_o = CubeScatter(
+        s, ns, lambda b: mm(dy1[:, rows_at(b, block)], att[...], TN), block, first_o, held_o, later_o, (o0s, o0r, o1s, o1r)
+    )
+    cube_o.send_core()
+    cube_o.add_core()
     small.receive()
     sums = inner[0]
     for k in range(1, n):
@@ -1524,7 +1528,7 @@
 
     def weight_block(b):
         cols = rows_at(b, block)
-        return jnp.concatenate([mm(x[:, cols], dqkv[...], TN), mm(dy1[:, cols], att[...], TN)], axis=1)
+        return mm(x[:, cols], dqkv[...], TN)
 
     def in_part(d, c):
         return mm(dqkv[rows_at(d, rows), :], w[rows_at(c, width), : 3 * lw], NT)
@@ -1535,13 +1539,20 @@
 
     def task(slot):
         for i, act in enumerate((cube.send_core, cube.add_core)):
-            low = 1 + i * half
-            pl.when((slot >= low) & (slot < low + half))(functools.partial(act, slot - low))
-
-    done = 1 + 2 * half
+            low = 1 + i * (half // 2)
+
+            @pl.when((slot >= low) & (slot < low + half // 2))
+            def _():
+                for j in range(2):
+                    act(2 * (slot - low) + j)
+
+    done = 1 + half
     line.run(0, done, None, task)
     line.start_own()
-    line.run(done, line.slots)
+    line.run(done, done + 3)
+    for i in range(cube.stages - 1):
+        cube_o.step(i)
+    line.run(done + 3, line.slots)
     for i in range(cube.stages - 1):
         cube.step(i)
 
@@ -1554,11 +1565,11 @@
     rounds = SmallExchange("head", z, n, gain_land, zs, zr)
     rounds.start()
     line.own()
-    grad_in[...] = middle[...] + total[...]
+    cube_o.step(cube.stages - 1)
+    grad_o[...] = jnp.transpose(held_o[0].astype(F32)).astype(BF16)
     cube.step(cube.stages - 1)
     for i, to in enumerate((grad_q, grad_k, grad_v)):
-        to[...] = held[0, :, i * lw : (i + 1) * lw].astype(F32)
-    grad_o[...] = jnp.transpose(held[0, :, 3 * lw :].astype(F32))
+        to[...] = held[0, :, i * lw : (i + 1) * lw]
     rounds.receive()
     at = s * block
     gains[...] = jnp.zeros_like(gains)
@@ -1567,25 +1578,26 @@
     for k in range(1, n):
         both = both + gain_land[k, pl.ds(0, 2), pl.ds(lw, block)]
     gains[2:4, :] = both
-    cube.core_sent()
-    cube.finish()
+    for one in (cube, cube_o):
+        one.core_sent()
+        one.finish()
     line.finish()
     small.finish()
     rounds.finish()
 
 
-def run_input(n, ns, dq, dk, dv, q_raw, k_raw, totals, gq, gk, cos, sin, x, w, middle, att, dy1, attn_part, mlp_part):
-    rows, depth = middle.shape
+def run_input(n, ns, dq, dk, dv, q_raw, k_raw, totals, gq, gk, cos, sin, x, w, att, dy1, attn_part, mlp_part):
     tl, lw = dq.shape
+    rows, depth = tl // n, x.shape[1]
     block = depth // ns
     dma = pltpu.SemaphoreType.DMA
     shape = jax.ShapeDtypeStruct
     return pl.pallas_call(
         functools.partial(input_kernel, n, ns, depth),
         out_shape=(shape((rows, depth), F32),)
-        + (shape((block, lw), F32),) * 3
-        + (shape((lw, block), F32), shape((8, block), F32)),
-        in_specs=[VMEM] * 17,
+        + (shape((block, lw), BF16),) * 3
+        + (shape((lw, block), BF16), shape((8, block), F32)),
+        in_specs=[VMEM] * 16,
         out_specs=(VMEM,) * 6,
         scratch_shapes=[
             pltpu.VMEM((tl, 3 * lw), BF16),
@@ -1593,11 +1605,11 @@
             pltpu.VMEM((tl, lw), F32),
             pltpu.VMEM((n, 8, tl), F32),
             pltpu.VMEM((2, n, STEPS, rows, depth // STEPS), BF16),
-            pltpu.VMEM((rows, depth), F32),
             pltpu.VMEM((ns, 8, lw + block), F32),
             pltpu.VMEM((ns, 8, lw + block), F32),
             pltpu.VMEM((n, 8, lw + block), F32),
-            *CubeScatter.scratch(ns, block, 4 * lw),
+            *CubeScatter.scratch(ns, block, 3 * lw),
+            *CubeScatter.scratch(ns, block, lw),
             dma((n,)), dma((n,)),
             dma((ns,)), dma((ns,)),
             dma((n,)), dma((n,)),
@@ -1608,7 +1620,7 @@
         ),
         cost_estimate=pl.CostEstimate(flops=8 * 10**9, bytes_accessed=30 * 10**6, transcendentals=0),
         name="into_input",
-    )(dq, dk, dv, q_raw, k_raw, totals, gq, gk, cos, sin, x, w, middle, att, dy1, attn_part, mlp_part)
+    )(dq, dk, dv, q_raw, k_raw, totals, gq, gk, cos, sin, x, w, att, dy1, attn_part, mlp_part)
 
 
 def doc_starts(doc_lengths, token_index):
@@ -1650,8 +1662,7 @@
     share = ns // heads
     sources = jnp.stack([source_of(seq_index % share, i, ns, share) for i in range(ns // share)])
     starts = doc_starts(doc_lengths, sources[:, None] * tl + jnp.arange(tl, dtype=jnp.int32)[None, :])
-    gq = lax.dynamic_slice_in_dim(q_gain, head_index * lw, lw)[None]
-    gk = lax.dynamic_slice_in_dim(k_gain, head_index * lw, lw)[None]
+    gq, gk = q_gain[None], k_gain[None]
 
     x, w, q_raw, k_raw, totals, q_rot, k_rot, v_low = run_project(
         nz, ns, tokens, q_weight, k_weight, v_weight, o_weight, gq, gk, cos, sin
@@ -1668,19 +1679,19 @@
     dq, dk, dv, grad_down = run_attend_back(
         ns, heads, datt, starts, q_held, k_held, v_held, o_held, lse, dy2, hidden
     )
-    input_grad, grad_q, grad_k, grad_v, grad_o, gains = run_input(
-        nz, ns, dq, dk, dv, q_raw, k_raw, totals, gq, gk, cos, sin, x, w, middle, attended, dy1, attn_part, mlp_part
+    last, grad_q, grad_k, grad_v, grad_o, gains = run_input(
+        nz, ns, dq, dk, dv, q_raw, k_raw, totals, gq, gk, cos, sin, x, w, attended, dy1, attn_part, mlp_part
     )
     return (
         output,
-        input_grad,
-        grad_q,
-        grad_k,
-        grad_v,
-        grad_o,
-        grad_gate,
-        grad_up,
-        grad_down,
+        middle + last,
+        grad_q.astype(F32),
+        grad_k.astype(F32),
+        grad_v.astype(F32),
+        grad_o.astype(F32),
+        grad_gate.astype(F32),
+        grad_up.astype(F32),
+        grad_down.astype(F32),
         gains[0],
         gains[1],
         gains[2],

time: 589 us -> 550 us (0.934)
  Pallas kernels: 557 us -> 524 us
  local copies, waits for them, and re-layouts: 16.5 us -> 1.41 us
  other arithmetic: 5.06 us -> 15.5 us
    pallas_call x1, Pallas kernels: 82.9 us -> 67.1 us  [run_attend(): pl.pallas_call(functools.partial(attend_kernel, ns, heads), out_shape=(sh...]
    unnamed x25 -> x21, local copies, waits for them, and re-layouts: 12.4 us -> 0.83 us
    pallas_call x1, Pallas kernels: 73.8 us -> 63.3 us  [run_input(): pl.pallas_call(functools.partial(input_kernel, n, ns, depth), out_shape=(...]
    convert_element_type x0 -> x7, other arithmetic: none -> 7.99 us  [the longest x1 1.56 us: on_device(): grad_gate.astype(F32)]
where the time goes in v5:
time: 550 us; the launch traced here: 542 us
  Pallas kernels  524 us (95%)
  other arithmetic  15.5 us (3%)
    pallas_call x1, Pallas kernels, run_forward(): pl.pallas_call(functools.partial(forward_kernel, n, ns), out_shape=(shape...  167 us
    pallas_call x1, Pallas kernels, run_backward(): pl.pallas_call(functools.partial(backward_kernel, n, ns), out_shape=(shap...  105 us
    pallas_call x1, Pallas kernels, run_attend(): pl.pallas_call(functools.partial(attend_kernel, ns, heads), out_shape=(sh...  67.1 us
    pallas_call x1, Pallas kernels, run_attend_back(): pl.pallas_call(functools.partial(attend_back_kernel, ns, heads), out_shap...  65.6 us
    pallas_call x1, Pallas kernels, run_input(): pl.pallas_call(functools.partial(input_kernel, n, ns, depth), out_shape=(...  63.3 us
    pallas_call x1, Pallas kernels, run_project(): pl.pallas_call(functools.partial(project_kernel, n, ns, depth), out_shape...  56.3 us

profile of v5, /device:TPU:8, one launch (start us, length us, event | category | flops | bytes accessed | tf_op | source)
XLA Modules:
  0.0 542.4 jit_solution(11482875832783745649)
XLA Ops:
  0.7 0.1 add_multiply_fusion
  0.7 0.8 reduce-window.8
  1.6 0.7 select_reduce_fusion.1
  2.3 0.1 iota_add_fusion
  2.4 1.3 select_reduce_fusion.starts
  3.7 1.0 fusion
  4.7 1.0 pad_maximum_fusion
  5.7 56.3 %project.1 = (bf16[512,2048]{1,0:T(8,128)(2,1)}, bf16[2048,2048]{1,0:T(8,128)(2,1)}, f32[512,512]{1,0:T(8,128)}, f32[512,512]{1,0:T(8,128)}, f32[8,512]{1,0:T(8,...) custom-call(bf16[128,2048]{1,0:T(8,128)(2,1)} %tok.3, bf16[256,512]{1,0:T(8,128)(2,1)} %wq.1, ...), custom_call_target="tpu_custom_call" | custom-call | flops 3000000000 | bytes 20000000 | tf_op jit(solution)/shard_map/project/pallas_call | solution.py:1420
  62.1 67.1 %attend.1 = (bf16[512,512]{1,0:T(8,128)(2,1)}, bf16[2048,128]{1,0:T(8,128)(2,1)}, bf16[4096,128]{1,0:T(8,128)(2,1)}, bf16[4096,128]{1,0:T(8,128)(2,1)}, f32[2048...) custom-call(bf16[512,512]{1,0:T(8,128)(2,1)} %get-tuple-element.53.q_in, ...), custom_call_target="tpu_custom_call" | custom-call | flops 3000000000 | bytes 8000000 | tf_op jit(solution)/shard_map/attend/pallas_call | solution.py:981
  129.1 166.8 %feed_forward.1 = (bf16[128,2048]{1,0:T(8,128)(2,1)}, bf16[512,2048]{1,0:T(8,128)(2,1)}, f32[128,2048]{1,0:T(8,128)}, bf16[512,2048]{1,0:T(8,128)(2,1)}, bf16[51...) custom-call(bf16[512,512]{1,0:T(8,128)(2,1)} %get-tuple-element.56.a, ...), custom_call_target="tpu_custom_call" | custom-call | flops 17999998976 | bytes 40000000 | tf_op jit(solution)/shard_map/feed_forward/pallas_call | solution.py:531
  295.9 105.2 %into_attention.1 = (f32[128,2048]{1,0:T(8,128)}, bf16[512,2048]{1,0:T(8,128)(2,1)}, bf16[512,512]{1,0:T(8,128)(2,1)}, f32[1,2048]{1,0:T(1,128)}, bf16[256,2048]{1,0:T(8,128)(2,1)}, /*index=5*/bf16[256,2048]{1,0:T(8,128)(2,1)}) custom-call(bf16[512,2048]{1,0:T(8,128)(2,1)} %get-tuple-element.60.dg, bf16[512,2048]{1,0:T(8,128)(2,1)} %get-tuple-element.61.du, ...), custom_call_target="tpu_custom_call" | custom-call | flops 17999998976 | bytes 30000000 | tf_op jit(solution)/shard_map/into_attention/pallas_call | solution.py:695
  401.2 65.6 %attend_back.1 = (bf16[512,512]{1,0:T(8,128)(2,1)}, bf16[512,512]{1,0:T(8,128)(2,1)}, bf16[512,512]{1,0:T(8,128)(2,1)}, bf16[2048,256]{1,0:T(8,128)(2,1)}) custom-call(bf16[512,512]{1,0:T(8,128)(2,1)} %get-tuple-element.66.do_in, s32[4,512]{1,0:T(4,128)} %select_reduce_fusion.starts, bf16[2048,128]{1,0:T(8,128)(2,1)} %get-tuple-element.67.q_buf, ...), custom_call_target="tpu_custom_call" | custom-call | flops 8000000000 | bytes 10000000 | tf_op jit(solution)/shard_map/attend_back/pallas_call | solution.py:1207
  466.8 0.0 copy-start.3
  466.8 63.3 %into_input.1 = (f32[128,2048]{1,0:T(8,128)}, bf16[256,512]{1,0:T(8,128)(2,1)}, bf16[256,512]{1,0:T(8,128)(2,1)}, bf16[256,512]{1,0:T(8,128)(2,1)}, bf16[512,256]{1,0:T(8,128)(2,1)}, /*index=5*/f32[8,256]{1,0:T(8,128)}) custom-call(bf16[512,512]{1,0:T(8,128)(2,1)} %get-tuple-element.74.dq, bf16[512,512]{1,0:T(8,128)(2,1)} %get-tuple-element.75.dk, ...), custom_call_target="tpu_custom_call" | custom-call | flops 8000000000 | bytes 30000000 | tf_op jit(solution)/shard_map/into_input/pallas_call | solution.py:1595
  530.1 0.0 copy-start.9
  530.1 0.0 copy-start.8
  530.1 0.0 copy-start.7
  530.1 0.0 copy-done.3
  530.1 0.0 copy-start.6
  530.1 0.0 copy-start.5
  530.1 2.4 add.63
  532.5 0.0 copy-done.9
  532.5 0.0 copy-start.2
  532.5 0.6 fusion.1
  533.1 0.0 copy-done.8
  533.1 0.9 convert_element_type.29
  534.0 0.0 copy-done.7
  534.0 0.9 convert_element_type.30
  534.8 0.0 copy-done.6
  534.8 0.9 convert_element_type.31
  535.7 0.0 copy-done.5
  535.7 0.0 copy-start.1
  535.7 0.8 convert_element_type.32
  536.5 0.0 copy-done.2
  536.5 1.5 convert_element_type.35
  538.0 0.0 copy-done.1
  538.0 0.0 copy-start
  538.0 1.6 convert_element_type.33
  539.6 0.0 copy-done
  539.6 0.0 copy-start.4
  539.6 1.6 convert_element_type.34
  541.1 0.0 copy-done.4
  541.1 0.8 copy.28
  (3 shorter events, 0.0 us)
Async XLA Ops:
  466.8 63.4 %copy-start.3 = (f32[128,2048]{1,0:T(8,128)S(1)}, f32[128,2048]{1,0:T(8,128)}, u32[]{:S(2)}) copy-start(f32[128,2048]{1,0:T(8,128)} %get-tuple-element.65) | copy-start | bytes 3145732
  530.1 2.5 copy-start.9
  530.1 3.0 copy-start.8
  530.1 3.9 copy-start.7
  530.1 4.7 copy-start.6
  530.1 5.6 %copy-start.5 = (bf16[512,256]{1,0:T(8,128)(2,1)S(1)}, bf16[512,256]{1,0:T(8,128)(2,1)}, u32[]{:S(2)}) copy-start(bf16[512,256]{1,0:T(8,128)(2,1)} %get-tuple-element.88) | copy-start | bytes 786436
  532.5 4.0 copy-start.2
  535.7 2.3 copy-start.1
  538.0 1.6 copy-start
  539.6 1.6 copy-start.4

commit v6 on v5

--- a/solution.py
+++ b/solution.py
@@ -16,17 +16,31 @@
 BF16 = jnp.bfloat16
 STEPS = 4
 LAG = 1
+EARLY = (7, 16)
 AG_CHUNKS = 2
 VMEM_BYTES = 62 * 1024 * 1024
 ANY = pl.BlockSpec(memory_space=pl.ANY)
 VMEM = pl.BlockSpec(memory_space=pltpu.VMEM)
+SMEM = pl.BlockSpec(memory_space=pltpu.SMEM)
 NN = (((1,), (0,)), ((), ()))
 NT = (((1,), (1,)), ((), ()))
 TN = (((0,), (0,)), ((), ()))
 
 
+def first_of_document(docs, token):
+    end, first = jnp.int32(0), jnp.zeros_like(token)
+    for i in range(docs.shape[0]):
+        end = end + docs[i]
+        first = first + jnp.where(token >= end, docs[i], 0)
+    return first
+
+
 def mm(left, right, dims=NN):
     return lax.dot_general(left, right, dims, preferred_element_type=F32)
+
+
+def early_part(ff):
+    return ff * EARLY[0] // EARLY[1] // HEAD_DIM * HEAD_DIM
 
 
 def rows_at(index, count):
@@ -378,7 +392,7 @@
 
 def forward_kernel(
     n, ns,
-    att, tok, cot, w_in, gate, up, down, attn_gain, mlp_gain,
+    att, tok, cot, more, gate_b, up, down, attn_gain, mlp_gain,
     out, h1r_out, branch_out, hidden_out, dy2_out, dg_out, du_out, gain_part, up_out,
     h1r, hidden, dy2, dg, du,
     wo, wd, wg, wu, land, branch, h1, second, g_pre, u_pre,
@@ -390,10 +404,12 @@
     block = depth // ns
     width = depth // STEPS
     mine = rows_at(s, block)
-    l_o = pltpu.make_async_copy(w_in.at[:, pl.ds(3 * lw, lw)], wo, wsem.at[0])
+    l_o = pltpu.make_async_copy(more.at[:, pl.ds(0, lw)], wo, wsem.at[0])
     l_u = pltpu.make_async_copy(up, wu.at[mine], wsem.at[1])
-    l_g = pltpu.make_async_copy(gate, wg, wsem.at[2])
-    for copy in (l_o, l_u, l_g):
+    early = more.shape[1] - lw
+    l_g = pltpu.make_async_copy(more.at[:, pl.ds(lw, early)], wg.at[:, pl.ds(0, early)], wsem.at[2])
+    l_h = pltpu.make_async_copy(gate_b, wg.at[:, pl.ds(early, ff - early)], wsem.at[3])
+    for copy in (l_o, l_u, l_g, l_h):
         copy.start()
     cube_barrier(s, z, ns, n)
     cube_u = CubeGather(s, ns, wu, block, us, ur)
@@ -451,6 +467,7 @@
 
     def weights_there():
         l_g.wait()
+        l_h.wait()
         cube_u.level(levels - 1)
         o_up.start()
 
@@ -521,7 +538,7 @@
     cube_d.finish()
 
 
-def run_forward(n, ns, att, tok, cot, w, gate, up, down, attn_gain, mlp_gain):
+def run_forward(n, ns, att, tok, cot, more, gate_b, up, down, attn_gain, mlp_gain):
     rows, depth = tok.shape
     tl, lw = att.shape
     ff = up.shape[1]
@@ -559,7 +576,7 @@
             pltpu.VMEM((rows, depth), F32),
             pltpu.VMEM((tl, ff), F32),
             pltpu.VMEM((tl, ff), F32),
-            dma((3,)),
+            dma((4,)),
             dma((5,)),
             dma((2, n)),
             *sems["gather"], *sems["scatter"], *sems["gather"], *sems["scatter"],
@@ -570,12 +587,12 @@
         ),
         cost_estimate=pl.CostEstimate(flops=18 * 10**9, bytes_accessed=40 * 10**6, transcendentals=2 * 10**6),
         name="feed_forward",
-    )(att, tok, cot, w, gate, up, down, attn_gain, mlp_gain)
+    )(att, tok, cot, more, gate_b, up, down, attn_gain, mlp_gain)
 
 
 def backward_kernel(
     n, ns,
-    dg, du, h1r_in, cot, branch, w_in, gate, up, attn_gain,
+    dg, du, h1r_in, cot, branch, more, gate_b, up, attn_gain,
     middle, dy1, datt, gain_part, grad_gate, grad_up,
     h1r, wo, wg, wu, land, total,
     first, held_g, later_g, held_u, later_u,
@@ -587,19 +604,22 @@
     lw, ff = datt.shape[1], dg.shape[1]
     block = depth // ns
     width = depth // STEPS
+    early = more.shape[1] - lw
 
     def weights_in(c):
         at = rows_at(c, width)
         return [
-            pltpu.make_async_copy(m.at[at], to.at[at], wsem.at[i, c]) for i, (m, to) in enumerate(((gate, wg), (up, wu)))
+            pltpu.make_async_copy(more.at[at, pl.ds(lw, early)], wg.at[at, pl.ds(0, early)], wsem.at[0, c]),
+            pltpu.make_async_copy(gate_b.at[at], wg.at[at, pl.ds(early, ff - early)], wsem.at[1, c]),
+            pltpu.make_async_copy(up.at[at], wu.at[at], wsem.at[2, c]),
         ]
 
+    l_h = pltpu.make_async_copy(h1r_in, h1r, osem.at[0])
+    l_o = pltpu.make_async_copy(more.at[:, pl.ds(0, lw)], wo, osem.at[1])
+    l_h.start()
     for c in range(STEPS):
         for copy in weights_in(c):
             copy.start()
-    l_h = pltpu.make_async_copy(h1r_in, h1r, osem.at[0])
-    l_o = pltpu.make_async_copy(w_in.at[:, pl.ds(3 * lw, lw)], wo, osem.at[1])
-    l_h.start()
     l_o.start()
     cube_barrier(s, z, ns, n)
 
@@ -623,28 +643,27 @@
                 copy.wait()
 
     def task(slot):
-        @pl.when(slot == 1)
-        def _():
-            l_h.wait()
-
-        def during(phase, act):
-            low = 1 + phase * half
-            pl.when((slot >= low) & (slot < low + half))(lambda: act(slot - low))
+        def during(low, count, act):
+            @pl.when((slot >= low) & (slot < low + half // count))
+            def _():
+                for i in range(count):
+                    act(count * (slot - low) + i)
 
         def send_second(j):
             cube_g.core_copy(half - 1 - j).wait_send()
             cube_u.send_core(j)
 
-        during(0, cube_g.send_core)
-        during(1, cube_g.add_core)
-        during(1, send_second)
-        during(2, cube_u.add_core)
-
+        during(0, 2, cube_g.add_core)
+        during(half // 2, 1, send_second)
+        during(half // 2 + half, 1, cube_u.add_core)
+
+    l_h.wait()
+    cube_g.send_core()
     line.run(0, 2 * STEPS, there, task)
     line.start_own()
     line.run(2 * STEPS, line.slots, None, task)
 
-    @pl.loop(line.slots, max(line.slots, 1 + 3 * half))
+    @pl.loop(line.slots, max(line.slots, half // 2 + 2 * half))
     def _(slot):
         task(slot)
 
@@ -683,10 +702,10 @@
     cube_u.finish()
 
 
-def run_backward(n, ns, dg, du, h1r, cot, branch, w, gate, up, attn_gain):
+def run_backward(n, ns, dg, du, h1r, cot, branch, more, gate_b, up, attn_gain):
     rows, depth = cot.shape
     tl, ff = dg.shape
-    lw = w.shape[1] // 4
+    lw = more.shape[1] + gate_b.shape[1] - ff
     block = depth // ns
     dma = pltpu.SemaphoreType.DMA
     sems = line_sems(n)
@@ -712,7 +731,7 @@
             pltpu.VMEM((2, n, STEPS, rows, depth // STEPS), BF16),
             pltpu.VMEM((rows, depth), F32),
             first, held, later, held, later,
-            dma((2, STEPS)),
+            dma((3, STEPS)),
             dma((2,)),
             *sems["scatter"], *sems["gather"],
             *cube_sems, *cube_sems,
@@ -722,7 +741,7 @@
         ),
         cost_estimate=pl.CostEstimate(flops=18 * 10**9, bytes_accessed=30 * 10**6, transcendentals=0),
         name="into_attention",
-    )(dg, du, h1r, cot, branch, w, gate, up, attn_gain)
+    )(dg, du, h1r, cot, branch, more, gate_b, up, attn_gain)
 
 
 LOG2E = 1.4426950408889634
@@ -760,7 +779,7 @@
 
 
 def attend_kernel(
-    ns, heads, q_in, k_in, v_in, starts, gate,
+    ns, heads, q_in, k_in, v_in, docs, gate,
     att, q_buf, k_buf, v_buf, o_buf, lse, gate_out,
     o_low, qs, qr, ks, kr, vs, vr, osend, orecv, local, cs, cr,
 ):
@@ -814,8 +833,10 @@
 
     kv = ((k_in, k_buf, ks, kr), (v_in, v_buf, vs, vr))
     block = gate.shape[0]
-    own_gate = pltpu.make_async_copy(gate, gate_out.at[rows_at(s, block)], local.at[0])
-    cube = CubeGather(s, ns, gate_out, block, cs, cr, gate)
+    late = gate_out.shape[1]
+    own = gate.at[:, pl.ds(gate.shape[1] - late, late)]
+    own_gate = pltpu.make_async_copy(own, gate_out.at[rows_at(s, block)], local.at[0])
+    cube = CubeGather(s, ns, gate_out, block, cs, cr, own)
     own_gate.start()
 
     def far(t):
@@ -883,7 +904,7 @@
             q_recv(i).wait_recv()
 
         q = q_buf[rows_at(i, tl), :]
-        start = starts[pl.ds(i, 1), :]
+        start = first_of_document(docs, src * tl + lax.broadcasted_iota(jnp.int32, (1, tl), 1))
         key_at = lax.broadcasted_iota(jnp.int32, (tl, tl), 0)
 
         def step(j, carry, diagonal):
@@ -971,7 +992,7 @@
     cube.finish()
 
 
-def run_attend(ns, heads, q, k, v, starts, gate):
+def run_attend(ns, heads, q, k, v, docs, gate):
     tl, lw = q.shape
     r = ns // heads
     nq = ns // r * tl
@@ -987,9 +1008,9 @@
             shape((nk, HEAD_DIM), BF16),
             shape((nq, HEAD_DIM), F32),
             shape((ns // r, tl), F32),
-            shape((gate.shape[0] * ns, gate.shape[1]), BF16),
+            shape((gate.shape[0] * ns, gate.shape[1] - early_part(gate.shape[1])), BF16),
         ),
-        in_specs=[VMEM] * 5,
+        in_specs=[VMEM] * 3 + [SMEM, VMEM],
         out_specs=(VMEM,) * 6 + (ANY,),
         scratch_shapes=[
             pltpu.VMEM((nq, HEAD_DIM), BF16),
@@ -1005,11 +1026,11 @@
         ),
         cost_estimate=pl.CostEstimate(flops=3 * 10**9, bytes_accessed=8 * 10**6, transcendentals=5 * 10**6),
         name="attend",
-    )(q, k, v, starts, gate)
+    )(q, k, v, docs, gate)
 
 
 def attend_back_kernel(
-    ns, heads, do_in, starts, q_buf, k_buf, v_buf, o_buf, lse, dy2, hidden,
+    ns, heads, do_in, docs, q_buf, k_buf, v_buf, o_buf, lse, dy2, hidden,
     dq, dk, dv, grad_down,
     do_buf, dq_low, dk_acc, dv_acc, low, pair, land,
     first, held, later, ca, cb, cc, cd,
@@ -1047,7 +1068,7 @@
 
     block = dy2.shape[1] // ns
     cube = CubeScatter(
-        s, ns, lambda b: mm(dy2[:, rows_at(b, block)], hidden[...], TN), block, first, held, later, (ca, cb, cc, cd)
+        s, ns, lambda b: mm(dy2[:, rows_at(b, block)], hidden[:, : grad_down.shape[0]], TN), block, first, held, later, (ca, cb, cc, cd)
     )
     cube.send_core()
     cube.add_core()
@@ -1074,7 +1095,7 @@
 
         q = q_buf[rows, :]
         do = do_buf[rows, :]
-        start = starts[pl.ds(i, 1), :]
+        start = first_of_document(docs, src * tl + lax.broadcasted_iota(jnp.int32, (1, tl), 1))
         norm = lse[pl.ds(i, 1), :]
         delta = lax.dot_general(
             ones, do.astype(F32) * o_buf[rows, :], NT,
@@ -1197,7 +1218,7 @@
     cube.finish()
 
 
-def run_attend_back(ns, heads, do, starts, q, k, v, o, lse, dy2, hidden):
+def run_attend_back(ns, heads, do, docs, q, k, v, o, lse, dy2, hidden):
     tl, lw = do.shape
     r = ns // heads
     nq = ns // r * tl
@@ -1206,8 +1227,8 @@
     shape = jax.ShapeDtypeStruct
     return pl.pallas_call(
         functools.partial(attend_back_kernel, ns, heads),
-        out_shape=(shape((tl, lw), BF16),) * 3 + (shape((hidden.shape[1], dy2.shape[1] // ns), BF16),),
-        in_specs=[VMEM] * 9,
+        out_shape=(shape((tl, lw), BF16),) * 3 + (shape((hidden.shape[1] - lw, dy2.shape[1] // ns), BF16),),
+        in_specs=[VMEM, SMEM] + [VMEM] * 7,
         out_specs=(VMEM,) * 4,
         scratch_shapes=[
             pltpu.VMEM((nq, HEAD_DIM), BF16),
@@ -1217,7 +1238,7 @@
             pltpu.VMEM((2, nk, HEAD_DIM), BF16),
             pltpu.VMEM((2, nk // 2, HEAD_DIM), BF16),
             pltpu.VMEM((2, r // 2, tl, lw), BF16),
-            *CubeScatter.scratch(ns, dy2.shape[1] // ns, hidden.shape[1]),
+            *CubeScatter.scratch(ns, dy2.shape[1] // ns, hidden.shape[1] - lw),
             dma((heads,)), dma((ns // r,)),
             dma((2, ns // 2)), dma((2, ns // 2)),
             dma((2, ns // 2)), dma((2, heads, r // 2)),
@@ -1228,7 +1249,7 @@
         ),
         cost_estimate=pl.CostEstimate(flops=8 * 10**9, bytes_accessed=10 * 10**6, transcendentals=5 * 10**6),
         name="attend_back",
-    )(do, starts, q, k, v, o, lse, dy2, hidden)
+    )(do, docs, q, k, v, o, lse, dy2, hidden)
 
 
 def cross_barrier(s, z, ns, n, between=None):
@@ -1293,9 +1314,9 @@
 
 def project_kernel(
     n, ns, depth_full,
-    tok, wq, wk, wv, wo, gq, gk, cos, sin,
-    x_out, w_out, q_raw, k_raw, totals, q_rot, k_rot, v_low,
-    x, w, land, lsem, ags, agr, cgs, cgr, ss, sr,
+    tok, wq, wk, wv, wo, gate, gq, gk, docs, turns,
+    x_out, w_out, more_out, q_raw, k_raw, totals, q_rot, k_rot, v_low, cos, sin,
+    x, w, own, land, lsem, ags, agr, cgs, cgr, egs, egr, ss, sr,
 ):
     s, z = lax.axis_index("seq"), lax.axis_index("head")
     rows, depth = tok.shape
@@ -1314,17 +1335,20 @@
         copy.start()
     loads[0].wait()
     cube = CubeGather(s, ns, w, block, cgs, cgr)
-    levels = len(cube.orders[0])
-    done = []
+    own_more = pltpu.make_async_copy(own, more_out.at[mine], lsem.at[6])
+    cube_e = CubeGather(s, ns, more_out, block, egs, egr, own)
+    levels = cube.levels
 
     def weights(k):
-        todo = [0] if k == 0 and n > 2 else [i for i in range(levels) if i not in done]
-        for i in todo:
-            cube.level(i)
-            done.append(i)
+        if k == 0:
+            cube.level(0)
+        else:
+            for i in range(1, levels):
+                cube.level(i)
+                if i == levels - 2:
+                    cube_e.start()
 
     def start_weights():
-        w[mine, 3 * lw :] = jnp.transpose(wo[...].astype(F32)).astype(BF16)
         for copy in loads[1:]:
             copy.wait()
         cube.start()
@@ -1333,7 +1357,7 @@
         at = rows_at(src, rows)
         for i, to in enumerate((q_raw, k_raw)):
             to[at, :] = mm(x[at, :], w[:, i * lw : (i + 1) * lw])
-        v_low[at, :] = mm(x[at, :], w[:, 2 * lw : 3 * lw]).astype(BF16)
+        v_low[at, :] = mm(x[at, :], w[:, 2 * lw :]).astype(BF16)
 
     part = rows // AG_CHUNKS
 
@@ -1350,6 +1374,14 @@
                 copy(z, c, up).start()
 
     start_weights()
+    own[:, :lw] = jnp.transpose(wo[...].astype(F32)).astype(BF16)
+    own[:, lw:] = gate[:, : own.shape[1] - lw]
+    own_more.start()
+    token = s * x.shape[0] + lax.broadcasted_iota(jnp.int32, cos.shape, 0)
+    angle = (token - first_of_document(docs, token)).astype(F32) * turns[...]
+    flip = jnp.where(lax.broadcasted_iota(jnp.int32, cos.shape, 1) < HEAD_DIM // 2, -1.0, 1.0)
+    cos[...] = jnp.cos(angle)
+    sin[...] = jnp.sin(angle) * flip
 
     def sides(k):
         return ((z + k, z + k < n, 0), (z - k, z - k >= 0, 1))
@@ -1393,9 +1425,14 @@
         for h in range(heads):
             cols = slice(h * HEAD_DIM, (h + 1) * HEAD_DIM)
             to[:, cols] = turn(raw[:, cols] * scale * gain[:, head_gain(h)], cos[...], sin[...]).astype(BF16)
+        if row == 0:
+            cube_e.level(0)
+    for i in range(1, levels):
+        cube_e.level(i)
     small.finish()
     cube.finish()
-    for out in outs:
+    cube_e.finish()
+    for out in [*outs, own_more]:
         out.wait()
 
     @pl.loop(0, n)
@@ -1411,7 +1448,7 @@
                 copy(src, c, 1).wait_send()
 
 
-def run_project(n, ns, tok, wq, wk, wv, wo, gq, gk, cos, sin):
+def run_project(n, ns, tok, wq, wk, wv, wo, gate, gq, gk, docs, turns):
     rows, depth = tok.shape
     tl = rows * n
     lw = wq.shape[1]
@@ -1421,23 +1458,27 @@
         functools.partial(project_kernel, n, ns, depth),
         out_shape=(
             shape((tl, depth), BF16),
-            shape((depth, 4 * lw), BF16),
+            shape((depth, 3 * lw), BF16),
+            shape((depth, lw + early_part(gate.shape[1])), BF16),
             shape((tl, lw), F32),
             shape((tl, lw), F32),
             shape((8, tl), F32),
             shape((tl, lw), BF16),
             shape((tl, lw), BF16),
             shape((tl, lw), BF16),
+            shape((tl, HEAD_DIM), F32),
+            shape((tl, HEAD_DIM), F32),
         ),
-        in_specs=[ANY] * 4 + [VMEM] * 5,
-        out_specs=(ANY,) * 2 + (VMEM,) * 6,
+        in_specs=[ANY] * 4 + [VMEM] * 4 + [SMEM, VMEM],
+        out_specs=(ANY,) * 3 + (VMEM,) * 8,
         scratch_shapes=[
             pltpu.VMEM((tl, depth), BF16),
-            pltpu.VMEM((depth, 4 * lw), BF16),
+            pltpu.VMEM((depth, 3 * lw), BF16),
+            pltpu.VMEM((wq.shape[0], lw + early_part(gate.shape[1])), BF16),
             pltpu.VMEM((n, 8, tl), F32),
-            dma((6,)),
+            dma((7,)),
             dma((2, n, AG_CHUNKS)), dma((n, AG_CHUNKS)),
-            *CubeGather.sems(ns),
+            *CubeGather.sems(ns), *CubeGather.sems(ns),
             dma((n,)), dma((n,)),
         ],
         compiler_params=pltpu.CompilerParams(
@@ -1445,14 +1486,14 @@
         ),
         cost_estimate=pl.CostEstimate(flops=3 * 10**9, bytes_accessed=20 * 10**6, transcendentals=0),
         name="project",
-    )(tok, wq, wk, wv, wo, gq, gk, cos, sin)
+    )(tok, wq, wk, wv, wo, gate, gq, gk, docs, turns)
 
 
 def input_kernel(
     n, ns, depth_full,
-    dq, dk, dv, q_raw, k_raw, totals, gq, gk, cos, sin, x, w, att, dy1, attn_part, mlp_part,
-    total, grad_q, grad_k, grad_v, grad_o, gains,
-    dqkv, q_back, k_back, inner, land, message, message_z, gain_land,
+    dq, dk, dv, q_raw, k_raw, totals, gq, gk, cos, sin, x, w, att, dy1, attn_part, mlp_part, dy2_in, hidden_in,
+    total, grad_q, grad_k, grad_v, grad_o, grad_down, gains,
+    dy2, hidden, lsem, dqkv, q_back, k_back, inner, land, message, message_z, gain_land,
     first, held, later, c0s, c0r, c1s, c1r,
     first_o, held_o, later_o, o0s, o0r, o1s, o1r,
     ss, sr, ms, mr, zs, zr, s1s, s1r,
@@ -1470,6 +1511,11 @@
     scales = [lax.rsqrt(as_column(sums, row) / depth_full + epsilon) for row in (0, 4)]
     todo = ((dq, q_raw, gq, q_back), (dk, k_raw, gk, k_back))
     products = []
+
+    l_d = pltpu.make_async_copy(dy2_in, dy2, lsem.at[0])
+    l_h = pltpu.make_async_copy(hidden_in.at[:, pl.ds(hidden_in.shape[1] - lw, lw)], hidden, lsem.at[1])
+    l_d.start()
+    l_h.start()
 
     def turn_all():
         message[...] = jnp.zeros_like(message)
@@ -1508,8 +1554,15 @@
     message_z[s] = message[s]
     each_seq(lambda t: message_copy(t, s).start())
     dqkv[:, 2 * lw :] = dv[...]
+    l_d.wait()
+    l_h.wait()
+
+    def early_block(b):
+        cols = rows_at(b, block)
+        return jnp.concatenate([mm(dy1[:, cols], att[...], TN), mm(dy2[:, cols], hidden[...], TN)], axis=1)
+
     cube_o = CubeScatter(
-        s, ns, lambda b: mm(dy1[:, rows_at(b, block)], att[...], TN), block, first_o, held_o, later_o, (o0s, o0r, o1s, o1r)
+        s, ns, early_block, block, first_o, held_o, later_o, (o0s, o0r, o1s, o1r)
     )
     cube_o.send_core()
     cube_o.add_core()
@@ -1531,7 +1584,7 @@
         return mm(x[:, cols], dqkv[...], TN)
 
     def in_part(d, c):
-        return mm(dqkv[rows_at(d, rows), :], w[rows_at(c, width), : 3 * lw], NT)
+        return mm(dqkv[rows_at(d, rows), :], w[rows_at(c, width), :], NT)
 
     cube = CubeScatter(s, ns, weight_block, block, first, held, later, (c0s, c0r, c1s, c1r))
     line = LineScatter(z, n, in_part, land, s1s, s1r, total)
@@ -1566,7 +1619,8 @@
     rounds.start()
     line.own()
     cube_o.step(cube.stages - 1)
-    grad_o[...] = jnp.transpose(held_o[0].astype(F32)).astype(BF16)
+    grad_o[...] = jnp.transpose(held_o[0, :, :lw].astype(F32)).astype(BF16)
+    grad_down[...] = jnp.transpose(held_o[0, :, lw:].astype(F32)).astype(BF16)
     cube.step(cube.stages - 1)
     for i, to in enumerate((grad_q, grad_k, grad_v)):
         to[...] = held[0, :, i * lw : (i + 1) * lw]
@@ -1586,7 +1640,7 @@
     rounds.finish()
 
 
-def run_input(n, ns, dq, dk, dv, q_raw, k_raw, totals, gq, gk, cos, sin, x, w, att, dy1, attn_part, mlp_part):
+def run_input(n, ns, dq, dk, dv, q_raw, k_raw, totals, gq, gk, cos, sin, x, w, att, dy1, attn_part, mlp_part, dy2, hidden):
     tl, lw = dq.shape
     rows, depth = tl // n, x.shape[1]
     block = depth // ns
@@ -1596,10 +1650,13 @@
         functools.partial(input_kernel, n, ns, depth),
         out_shape=(shape((rows, depth), F32),)
         + (shape((block, lw), BF16),) * 3
-        + (shape((lw, block), BF16), shape((8, block), F32)),
-        in_specs=[VMEM] * 16,
-        out_specs=(VMEM,) * 6,
+        + (shape((lw, block), BF16), shape((lw, block), BF16), shape((8, block), F32)),
+        in_specs=[VMEM] * 16 + [ANY] * 2,
+        out_specs=(VMEM,) * 7,
         scratch_shapes=[
+            pltpu.VMEM((tl, depth), BF16),
+            pltpu.VMEM((tl, lw), BF16),
+            dma((2,)),
             pltpu.VMEM((tl, 3 * lw), BF16),
             pltpu.VMEM((tl, lw), F32),
             pltpu.VMEM((tl, lw), F32),
@@ -1609,7 +1666,7 @@
             pltpu.VMEM((ns, 8, lw + block), F32),
             pltpu.VMEM((n, 8, lw + block), F32),
             *CubeScatter.scratch(ns, block, 3 * lw),
-            *CubeScatter.scratch(ns, block, lw),
+            *CubeScatter.scratch(ns, block, 2 * lw),
             dma((n,)), dma((n,)),
             dma((ns,)), dma((ns,)),
             dma((n,)), dma((n,)),
@@ -1620,19 +1677,54 @@
         ),
         cost_estimate=pl.CostEstimate(flops=8 * 10**9, bytes_accessed=30 * 10**6, transcendentals=0),
         name="into_input",
-    )(dq, dk, dv, q_raw, k_raw, totals, gq, gk, cos, sin, x, w, att, dy1, attn_part, mlp_part)
-
-
-def doc_starts(doc_lengths, token_index):
-    ends = jnp.cumsum(doc_lengths)
-    return jnp.sum(jnp.where(token_index[..., None] >= ends, doc_lengths, 0), axis=-1).astype(jnp.int32)
-
-
-def turn_tables(positions):
-    frequency = jnp.power(rope_base, -jnp.arange(HEAD_DIM // 2, dtype=F32) * (2.0 / HEAD_DIM))
-    angles = positions.astype(F32)[:, None] * frequency[None, :]
-    cos, sin = jnp.cos(angles), jnp.sin(angles)
-    return jnp.concatenate([cos, cos], axis=1), jnp.concatenate([-sin, sin], axis=1)
+    )(dq, dk, dv, q_raw, k_raw, totals, gq, gk, cos, sin, x, w, att, dy1, attn_part, mlp_part, dy2, hidden)
+
+
+def widen_kernel(count, *refs):
+    spec = WIDEN
+    ins, rest = refs[:count], refs[count:]
+    outs, rest = rest[: len(spec)], rest[len(spec) :]
+    held, rest = rest[:count], rest[count:]
+    wide, (load_sem, store_sem) = rest[: len(spec)], rest[len(spec) :]
+    loads = [pltpu.make_async_copy(a, b, load_sem.at[i]) for i, (a, b) in enumerate(zip(ins, held))]
+    stores = [pltpu.make_async_copy(a, b, store_sem.at[i]) for i, (a, b) in enumerate(zip(wide, outs))]
+    for copy in loads:
+        copy.start()
+    at = 0
+    for (parts, stacked), to, store in zip(spec, wide, stores):
+        row = 0
+        for i in range(at, at + parts):
+            loads[i].wait()
+            block = held[i][...].astype(to.dtype)
+            if stacked:
+                to[row : row + block.shape[0], :] = block
+                row += block.shape[0]
+            elif i == at:
+                to[...] = block
+            else:
+                to[...] += block
+        at += parts
+        store.start()
+    for copy in stores:
+        copy.wait()
+
+
+WIDEN = ((1, False), (1, False), (1, False), (2, True), (1, False), (1, False), (1, False), (1, False), (2, False))
+
+
+def run_widen(arrays, outs):
+    dma = pltpu.SemaphoreType.DMA
+    return pl.pallas_call(
+        functools.partial(widen_kernel, len(arrays)),
+        out_shape=tuple(outs),
+        in_specs=[ANY] * len(arrays),
+        out_specs=(ANY,) * len(outs),
+        scratch_shapes=[pltpu.VMEM(a.shape, a.dtype) for a in arrays]
+        + [pltpu.VMEM(o.shape, o.dtype) for o in outs]
+        + [dma((len(arrays),)), dma((len(outs),))],
+        compiler_params=pltpu.CompilerParams(vmem_limit_bytes=VMEM_BYTES),
+        name="widen",
+    )(*arrays)
 
 
 def on_device(
@@ -1652,46 +1744,54 @@
     mlp_gain,
 ):
     ns, nz = lax.axis_size("seq"), lax.axis_size("head")
-    seq_index, head_index = lax.axis_index("seq"), lax.axis_index("head")
     lw = q_weight.shape[1]
     heads = lw // HEAD_DIM
-    tl = tokens.shape[0] * nz
-    ff = gate_weight.shape[1]
-    token_index = seq_index * tl + jnp.arange(tl, dtype=jnp.int32)
-    cos, sin = turn_tables(token_index - doc_starts(doc_lengths, token_index))
-    share = ns // heads
-    sources = jnp.stack([source_of(seq_index % share, i, ns, share) for i in range(ns // share)])
-    starts = doc_starts(doc_lengths, sources[:, None] * tl + jnp.arange(tl, dtype=jnp.int32)[None, :])
+    block, ff = gate_weight.shape
     gq, gk = q_gain[None], k_gain[None]
-
-    x, w, q_raw, k_raw, totals, q_rot, k_rot, v_low = run_project(
-        nz, ns, tokens, q_weight, k_weight, v_weight, o_weight, gq, gk, cos, sin
+    frequency = jnp.power(rope_base, -(jnp.arange(HEAD_DIM) % (HEAD_DIM // 2)).astype(F32) * (2.0 / HEAD_DIM))
+
+    x, w, more, q_raw, k_raw, totals, q_rot, k_rot, v_low, cos, sin = run_project(
+        nz, ns, tokens, q_weight, k_weight, v_weight, o_weight, gate_weight, gq, gk, doc_lengths, frequency[None]
     )
-    attended, q_held, k_held, v_held, o_held, lse, gate = run_attend(
-        ns, heads, q_rot, k_rot, v_low, starts, gate_weight
+    attended, q_held, k_held, v_held, o_held, lse, gate_b = run_attend(
+        ns, heads, q_rot, k_rot, v_low, doc_lengths, gate_weight
     )
     output, h1r, branch, hidden, dy2, dg, du, mlp_part, up = run_forward(
-        nz, ns, attended, tokens, cotangent, w, gate, up_weight, down_weight, attn_gain[None], mlp_gain[None]
+        nz, ns, attended, tokens, cotangent, more, gate_b, up_weight, down_weight, attn_gain[None], mlp_gain[None]
     )
     middle, dy1, datt, attn_part, grad_gate, grad_up = run_backward(
-        nz, ns, dg, du, h1r, cotangent, branch, w, gate, up, attn_gain[None]
+        nz, ns, dg, du, h1r, cotangent, branch, more, gate_b, up, attn_gain[None]
     )
-    dq, dk, dv, grad_down = run_attend_back(
-        ns, heads, datt, starts, q_held, k_held, v_held, o_held, lse, dy2, hidden
+    dq, dk, dv, down_a = run_attend_back(
+        ns, heads, datt, doc_lengths, q_held, k_held, v_held, o_held, lse, dy2, hidden
     )
-    last, grad_q, grad_k, grad_v, grad_o, gains = run_input(
-        nz, ns, dq, dk, dv, q_raw, k_raw, totals, gq, gk, cos, sin, x, w, attended, dy1, attn_part, mlp_part
+    last, grad_q, grad_k, grad_v, grad_o, down_b, gains = run_input(
+        nz, ns, dq, dk, dv, q_raw, k_raw, totals, gq, gk, cos, sin, x, w, attended, dy1, attn_part, mlp_part, dy2, hidden
+    )
+    shape = jax.ShapeDtypeStruct
+    small = shape((block, lw), F32)
+    output, grad_gate, grad_up, grad_down, grad_q, grad_k, grad_v, grad_o, input_grad = run_widen(
+        (output, grad_gate, grad_up, down_a, down_b, grad_q, grad_k, grad_v, grad_o, middle, last),
+        (
+            shape(output.shape, BF16),
+            shape((block, ff), F32),
+            shape((block, ff), F32),
+            shape((ff, block), F32),
+            small, small, small,
+            shape((lw, block), F32),
+            shape(middle.shape, F32),
+        ),
     )
     return (
         output,
-        middle + last,
-        grad_q.astype(F32),
-        grad_k.astype(F32),
-        grad_v.astype(F32),
-        grad_o.astype(F32),
-        grad_gate.astype(F32),
-        grad_up.astype(F32),
-        grad_down.astype(F32),
+        input_grad,
+        grad_q,
+        grad_k,
+        grad_v,
+        grad_o,
+        grad_gate,
+        grad_up,
+        grad_down,
         gains[0],
         gains[1],
         gains[2],

time: 550 us -> 519 us (0.944)
  Pallas kernels: 524 us -> 509 us
  other arithmetic: 15.5 us -> 0.52 us
    pallas_call x1, Pallas kernels: 67.1 us -> 51.6 us  [run_attend(): pl.pallas_call(functools.partial(attend_kernel, ns, heads), out_shape=(sh...]
    pallas_call x1, Pallas kernels: 105 us -> 96 us  [run_backward(): pl.pallas_call(functools.partial(backward_kernel, n, ns), out_shape=(shap...]
    pallas_call x1, Pallas kernels: 65.6 us -> 57.5 us  [run_attend_back(): pl.pallas_call(functools.partial(attend_back_kernel, ns, heads), out_shap...]
    convert_element_type x8 -> x0, other arithmetic: 7.99 us -> none  [the longest x1 1.56 us: on_device(): grad_gate.astype(F32)]
    pallas_call x1, Pallas kernels: 56.3 us -> 62.7 us  [run_project(): pl.pallas_call(functools.partial(project_kernel, n, ns, depth), out_shape...]
    pallas_call x0 -> x1, Pallas kernels: none -> 6.07 us  [run_widen(): pl.pallas_call(functools.partial(widen_kernel, len(arrays)), out_shape=tu...]
where the time goes in v6:
time: 519 us; the launch traced here: 512 us
  Pallas kernels  509 us (98%)
    pallas_call x1, Pallas kernels, run_forward(): pl.pallas_call(functools.partial(forward_kernel, n, ns), out_shape=(shape...  168 us
    pallas_call x1, Pallas kernels, run_backward(): pl.pallas_call(functools.partial(backward_kernel, n, ns), out_shape=(shap...  96 us
    pallas_call x1, Pallas kernels, run_input(): pl.pallas_call(functools.partial(input_kernel, n, ns, depth), out_shape=(...  67.2 us
    pallas_call x1, Pallas kernels, run_project(): pl.pallas_call(functools.partial(project_kernel, n, ns, depth), out_shape...  62.7 us
    pallas_call x1, Pallas kernels, run_attend_back(): pl.pallas_call(functools.partial(attend_back_kernel, ns, heads), out_shap...  57.5 us
    pallas_call x1, Pallas kernels, run_attend(): pl.pallas_call(functools.partial(attend_kernel, ns, heads), out_shape=(sh...  51.6 us

profile of v6, /device:TPU:8, one launch (start us, length us, event | category | flops | bytes accessed | tf_op | source)
XLA Modules:
  0.0 511.7 jit_solution(12803523470376795232)
XLA Ops:
  0.6 0.5 fusion.3.turns
  1.2 62.7 %project.1 = (bf16[512,2048]{1,0:T(8,128)(2,1)}, bf16[2048,1536]{1,0:T(8,128)(2,1)}, bf16[2048,1408]{1,0:T(8,128)(2,1)}, f32[512,512]{1,0:T(8,128)}, f32[512,512...) custom-call(bf16[128,2048]{1,0:T(8,128)(2,1)} %tok.3, ...), custom_call_target="tpu_custom_call" | custom-call | flops 3000000000 | bytes 20000000 | tf_op jit(solution)/shard_map/project/pallas_call | solution.py:1457
  63.9 51.6 %attend.1 = (bf16[512,512]{1,0:T(8,128)(2,1)}, bf16[2048,128]{1,0:T(8,128)(2,1)}, bf16[4096,128]{1,0:T(8,128)(2,1)}, bf16[4096,128]{1,0:T(8,128)(2,1)}, f32[2048...) custom-call(bf16[512,512]{1,0:T(8,128)(2,1)} %get-tuple-element.66.q_in, ...), custom_call_target="tpu_custom_call" | custom-call | flops 3000000000 | bytes 8000000 | tf_op jit(solution)/shard_map/attend/pallas_call | solution.py:1002
  115.5 167.6 %feed_forward.1 = (bf16[128,2048]{1,0:T(8,128)(2,1)}, bf16[512,2048]{1,0:T(8,128)(2,1)}, f32[128,2048]{1,0:T(8,128)}, bf16[512,2048]{1,0:T(8,128)(2,1)}, bf16[51...) custom-call(bf16[512,512]{1,0:T(8,128)(2,1)} %get-tuple-element.69.a, ...), custom_call_target="tpu_custom_call" | custom-call | flops 17999998976 | bytes 40000000 | tf_op jit(solution)/shard_map/feed_forward/pallas_call | solution.py:548
  283.1 96.0 %into_attention.1 = (f32[128,2048]{1,0:T(8,128)}, bf16[512,2048]{1,0:T(8,128)(2,1)}, bf16[512,512]{1,0:T(8,128)(2,1)}, f32[1,2048]{1,0:T(1,128)}, bf16[256,2048]{1,0:T(8,128)(2,1)}, /*index=5*/bf16[256,2048]{1,0:T(8,128)(2,1)}) custom-call(bf16[512,2048]{1,0:T(8,128)(2,1)} %get-tuple-element.73.dg, bf16[512,2048]{1,0:T(8,128)(2,1)} %get-tuple-element.74.du, ...), custom_call_target="tpu_custom_call" | custom-call | flops 17999998976 | bytes 30000000 | tf_op jit(solution)/shard_map/into_attention/pallas_call | solution.py:714
  379.1 57.5 %attend_back.1 = (bf16[512,512]{1,0:T(8,128)(2,1)}, bf16[512,512]{1,0:T(8,128)(2,1)}, bf16[512,512]{1,0:T(8,128)(2,1)}, bf16[1536,256]{1,0:T(8,128)(2,1)}) custom-call(bf16[512,512]{1,0:T(8,128)(2,1)} %get-tuple-element.80.do_in, s32[3]{0:T(128)} %docs.5, bf16[2048,128]{1,0:T(8,128)(2,1)} %get-tuple-element.81.q_buf, ...), custom_call_target="tpu_custom_call" | custom-call | flops 8000000000 | bytes 10000000 | tf_op jit(solution)/shard_map/attend_back/pallas_call | solution.py:1228
  436.5 67.2 %into_input.1 = (f32[128,2048]{1,0:T(8,128)}, bf16[256,512]{1,0:T(8,128)(2,1)}, bf16[256,512]{1,0:T(8,128)(2,1)}, bf16[256,512]{1,0:T(8,128)(2,1)}, bf16[512,256...) custom-call(bf16[512,512]{1,0:T(8,128)(2,1)} %get-tuple-element.89.dq, ...), custom_call_target="tpu_custom_call" | custom-call | flops 8000000000 | bytes 30000000 | tf_op jit(solution)/shard_map/into_input/pallas_call | solution.py:1649
  503.7 1.4 fusion.4
  505.2 6.1 %widen.1 = (bf16[128,2048]{1,0:T(8,128)(2,1)}, f32[256,2048]{1,0:T(8,128)}, f32[256,2048]{1,0:T(8,128)}, f32[2048,256]{1,0:T(8,128)}, f32[256,512]{1,0:T(8,128)}...) custom-call(bf16[128,2048]{1,0:T(8,128)(2,1)} %get-tuple-element.72.refs_0_, ...), custom_call_target="tpu_custom_call" | custom-call | tf_op jit(solution)/shard_map/widen/pallas_call | solution.py:1717

commit v7 on v6

--- a/solution.py
+++ b/solution.py
@@ -592,16 +592,16 @@
 
 def backward_kernel(
     n, ns,
-    dg, du, h1r_in, cot, branch, more, gate_b, up, attn_gain,
+    dg_in, du_in, h1r_in, cot, branch, more, gate_b, up, attn_gain,
     middle, dy1, datt, gain_part, grad_gate, grad_up,
-    h1r, wo, wg, wu, land, total,
+    dg, du, h1r, wo, wg, wu, land, total,
     first, held_g, later_g, held_u, later_u,
     wsem, osem, s1s, s1r, g1s, g1r,
     ga, gb, gc, gd, ua, ub, uc, ud,
 ):
     s, z = lax.axis_index("seq"), lax.axis_index("head")
     rows, depth = cot.shape
-    lw, ff = datt.shape[1], dg.shape[1]
+    lw, ff = datt.shape[1], dg_in.shape[1]
     block = depth // ns
     width = depth // STEPS
     early = more.shape[1] - lw
@@ -616,7 +616,10 @@
 
     l_h = pltpu.make_async_copy(h1r_in, h1r, osem.at[0])
     l_o = pltpu.make_async_copy(more.at[:, pl.ds(0, lw)], wo, osem.at[1])
-    l_h.start()
+    l_dg = pltpu.make_async_copy(dg_in, dg, osem.at[2])
+    l_du = pltpu.make_async_copy(du_in, du, osem.at[3])
+    for load in (l_dg, l_h, l_du):
+        load.start()
     for c in range(STEPS):
         for copy in weights_in(c):
             copy.start()
@@ -658,7 +661,9 @@
         during(half // 2 + half, 1, cube_u.add_core)
 
     l_h.wait()
+    l_dg.wait()
     cube_g.send_core()
+    l_du.wait()
     line.run(0, 2 * STEPS, there, task)
     line.start_own()
     line.run(2 * STEPS, line.slots, None, task)
@@ -721,9 +726,11 @@
             shape((block, ff), BF16),
             shape((block, ff), BF16),
         ),
-        in_specs=[VMEM, VMEM, ANY, VMEM, VMEM, ANY, ANY, ANY, VMEM],
+        in_specs=[ANY, ANY, ANY, VMEM, VMEM, ANY, ANY, ANY, VMEM],
         out_specs=(VMEM,) * 6,
         scratch_shapes=[
+            pltpu.VMEM((tl, ff), BF16),
+            pltpu.VMEM((tl, ff), BF16),
             pltpu.VMEM((tl, depth), BF16),
             pltpu.VMEM((depth, lw), BF16),
             pltpu.VMEM((depth, ff), BF16),
@@ -732,7 +739,7 @@
             pltpu.VMEM((rows, depth), F32),
             first, held, later, held, later,
             dma((3, STEPS)),
-            dma((2,)),
+            dma((4,)),
             *sems["scatter"], *sems["gather"],
             *cube_sems, *cube_sems,
         ],
@@ -778,10 +785,10 @@
     return pl.ds(pl.multiple_of(h * HEAD_DIM, HEAD_DIM), HEAD_DIM)
 
 
-def attend_kernel(
+def attend_part(
     ns, heads, q_in, k_in, v_in, docs, gate,
-    att, q_buf, k_buf, v_buf, o_buf, lse, gate_out,
-    o_low, qs, qr, ks, kr, vs, vr, osend, orecv, local, cs, cr,
+    att, q_out, k_out, v_out, o_buf, lse, gate_out,
+    q_buf, k_buf, v_buf, o_low, qs, qr, ks, kr, vs, vr, osend, orecv, local, cs, cr, late,
 ):
     s = lax.axis_index("seq")
     r = ns // heads
@@ -799,7 +806,7 @@
         def _():
             q_buf[rows_at(to_row, tl), :] = q_in[:, head_cols(mine)]
 
-    seq_barrier(s, ns, own_rows)
+    own_rows()
 
     def q_copy(h):
         return pltpu.make_async_remote_copy(
@@ -833,8 +840,8 @@
 
     kv = ((k_in, k_buf, ks, kr), (v_in, v_buf, vs, vr))
     block = gate.shape[0]
-    late = gate_out.shape[1]
-    own = gate.at[:, pl.ds(gate.shape[1] - late, late)]
+    cols = gate_out.shape[1]
+    own = gate.at[:, pl.ds(gate.shape[1] - cols, cols)]
     own_gate = pltpu.make_async_copy(own, gate_out.at[rows_at(s, block)], local.at[0])
     cube = CubeGather(s, ns, gate_out, block, cs, cr, own)
     own_gate.start()
@@ -944,7 +951,14 @@
         def _():
             att[:, head_cols(mine)] = o.astype(BF16)
 
+    late()
     cube.start()
+    keep = [
+        pltpu.make_async_copy(a, b, local.at[1 + i])
+        for i, (a, b) in enumerate(((k_buf, k_out), (v_buf, v_out), (q_buf, q_out)))
+    ]
+    for copy in keep[:2]:
+        copy.start()
     cuts = [0, blocks - 1, blocks, blocks]
     for i in range(3):
         pl.loop(cuts[i], cuts[i + 1])(attend_block)
@@ -953,6 +967,7 @@
     for i in range(2, cube.levels):
         cube.level(i)
 
+    keep[2].start()
     own_gate.wait()
 
     @pl.loop(0, heads)
@@ -990,48 +1005,14 @@
             pass_on(t, False)
 
     cube.finish()
-
-
-def run_attend(ns, heads, q, k, v, docs, gate):
-    tl, lw = q.shape
-    r = ns // heads
-    nq = ns // r * tl
-    nk = ns * tl
-    dma = pltpu.SemaphoreType.DMA
-    shape = jax.ShapeDtypeStruct
-    return pl.pallas_call(
-        functools.partial(attend_kernel, ns, heads),
-        out_shape=(
-            shape((tl, lw), BF16),
-            shape((nq, HEAD_DIM), BF16),
-            shape((nk, HEAD_DIM), BF16),
-            shape((nk, HEAD_DIM), BF16),
-            shape((nq, HEAD_DIM), F32),
-            shape((ns // r, tl), F32),
-            shape((gate.shape[0] * ns, gate.shape[1] - early_part(gate.shape[1])), BF16),
-        ),
-        in_specs=[VMEM] * 3 + [SMEM, VMEM],
-        out_specs=(VMEM,) * 6 + (ANY,),
-        scratch_shapes=[
-            pltpu.VMEM((nq, HEAD_DIM), BF16),
-            dma((heads,)), dma((ns // r,)),
-            dma((2, ns)), dma((ns,)),
-            dma((2, ns)), dma((ns,)),
-            dma((ns // r,)), dma((heads,)),
-            dma((1,)),
-            *CubeGather.sems(ns),
-        ],
-        compiler_params=pltpu.CompilerParams(
-            collective_id=3, has_side_effects=True, vmem_limit_bytes=VMEM_BYTES
-        ),
-        cost_estimate=pl.CostEstimate(flops=3 * 10**9, bytes_accessed=8 * 10**6, transcendentals=5 * 10**6),
-        name="attend",
-    )(q, k, v, docs, gate)
+    for copy in keep:
+        copy.wait()
 
 
 def attend_back_kernel(
-    ns, heads, do_in, docs, q_buf, k_buf, v_buf, o_buf, lse, dy2, hidden,
+    ns, heads, do_in, docs, q_in, k_in, v_in, o_in, lse, dy2_in, hidden_in,
     dq, dk, dv, grad_down,
+    q_buf, k_buf, v_buf, o_buf, dy2, hidden, lsem,
     do_buf, dq_low, dk_acc, dv_acc, low, pair, land,
     first, held, later, ca, cb, cc, cd,
     ds_, dr_, ps, pr, gs, gr, qs, qr,
@@ -1043,6 +1024,15 @@
     mine, sub = s // r, s % r
     parity = s % 2
 
+    loads = [
+        pltpu.make_async_copy(a, b, lsem.at[i])
+        for i, (a, b) in enumerate(
+            ((dy2_in, dy2), (hidden_in, hidden), (q_in, q_buf), (k_in, k_buf), (v_in, v_buf), (o_in, o_buf))
+        )
+    ]
+    for load in loads:
+        load.start()
+
     def clear():
         dk_acc[...] = jnp.zeros_like(dk_acc)
         dv_acc[...] = jnp.zeros_like(dv_acc)
@@ -1070,6 +1060,8 @@
     cube = CubeScatter(
         s, ns, lambda b: mm(dy2[:, rows_at(b, block)], hidden[:, : grad_down.shape[0]], TN), block, first, held, later, (ca, cb, cc, cd)
     )
+    for load in loads:
+        load.wait()
     cube.send_core()
     cube.add_core()
 
@@ -1228,9 +1220,16 @@
     return pl.pallas_call(
         functools.partial(attend_back_kernel, ns, heads),
         out_shape=(shape((tl, lw), BF16),) * 3 + (shape((hidden.shape[1] - lw, dy2.shape[1] // ns), BF16),),
-        in_specs=[VMEM, SMEM] + [VMEM] * 7,
+        in_specs=[VMEM, SMEM] + [ANY] * 4 + [VMEM] + [ANY] * 2,
         out_specs=(VMEM,) * 4,
         scratch_shapes=[
+            pltpu.VMEM((nq, HEAD_DIM), BF16),
+            pltpu.VMEM((nk, HEAD_DIM), BF16),
+            pltpu.VMEM((nk, HEAD_DIM), BF16),
+            pltpu.VMEM((nq, HEAD_DIM), F32),
+            pltpu.VMEM(dy2.shape, BF16),
+            pltpu.VMEM(hidden.shape, BF16),
+            dma((6,)),
             pltpu.VMEM((nq, HEAD_DIM), BF16),
             pltpu.VMEM((nq, HEAD_DIM), BF16),
             pltpu.VMEM((nk, HEAD_DIM), F32),
@@ -1312,11 +1311,11 @@
     return x * cos - pltpu.roll(x, HEAD_DIM // 2, 1) * sin
 
 
-def project_kernel(
+def project_part(
     n, ns, depth_full,
     tok, wq, wk, wv, wo, gate, gq, gk, docs, turns,
-    x_out, w_out, more_out, q_raw, k_raw, totals, q_rot, k_rot, v_low, cos, sin,
-    x, w, own, land, lsem, ags, agr, cgs, cgr, egs, egr, ss, sr,
+    x_out, w_out, more_out, q_out, k_out, totals, cos, sin,
+    q_rot, k_rot, v_low, q_raw, k_raw, x, w, own, land, lsem, ags, agr, cgs, cgr, egs, egr, ss, sr,
 ):
     s, z = lax.axis_index("seq"), lax.axis_index("head")
     rows, depth = tok.shape
@@ -1335,7 +1334,7 @@
         copy.start()
     loads[0].wait()
     cube = CubeGather(s, ns, w, block, cgs, cgr)
-    own_more = pltpu.make_async_copy(own, more_out.at[mine], lsem.at[6])
+    own_more = pltpu.make_async_copy(own, more_out.at[mine], lsem.at[8])
     cube_e = CubeGather(s, ns, more_out, block, egs, egr, own)
     levels = cube.levels
 
@@ -1408,7 +1407,10 @@
             for src, there, _ in sides(k):
                 pl.when(there)(functools.partial(multiply, src))
 
-    outs = [pltpu.make_async_copy(x, x_out, lsem.at[4]), pltpu.make_async_copy(w, w_out, lsem.at[5])]
+    outs = [
+        pltpu.make_async_copy(a, b, lsem.at[4 + i])
+        for i, (a, b) in enumerate(((x, x_out), (w, w_out), (q_raw, q_out), (k_raw, k_out)))
+    ]
     for out in outs:
         out.start()
     totals[...] = row_sums(q_raw[...] * q_raw[...], k_raw[...] * k_raw[...])
@@ -1427,73 +1429,113 @@
             to[:, cols] = turn(raw[:, cols] * scale * gain[:, head_gain(h)], cos[...], sin[...]).astype(BF16)
         if row == 0:
             cube_e.level(0)
-    for i in range(1, levels):
-        cube_e.level(i)
-    small.finish()
-    cube.finish()
-    cube_e.finish()
-    for out in [*outs, own_more]:
-        out.wait()
-
-    @pl.loop(0, n)
-    def _(src):
-        for c in range(AG_CHUNKS):
-
-            @pl.when((src >= z) & (z > 0))
-            def _():
-                copy(src, c, 0).wait_send()
-
-            @pl.when((src <= z) & (z < n - 1))
-            def _():
-                copy(src, c, 1).wait_send()
-
-
-def run_project(n, ns, tok, wq, wk, wv, wo, gate, gq, gk, docs, turns):
+
+    def late():
+        for i in range(1, levels):
+            cube_e.level(i)
+
+    def finish():
+        small.finish()
+        cube.finish()
+        cube_e.finish()
+        for out in [*outs, own_more]:
+            out.wait()
+
+        @pl.loop(0, n)
+        def _(src):
+            for c in range(AG_CHUNKS):
+
+                @pl.when((src >= z) & (z > 0))
+                def _():
+                    copy(src, c, 0).wait_send()
+
+                @pl.when((src <= z) & (z < n - 1))
+                def _():
+                    copy(src, c, 1).wait_send()
+
+    return late, finish
+
+
+def front_kernel(n, ns, heads, depth_full, *refs):
+    ins, refs = refs[:10], refs[10:]
+    made, refs = refs[:8], refs[8:]
+    attended, refs = refs[:7], refs[7:]
+    first, second = refs[:18], refs[18:]
+    late, finish = project_part(n, ns, depth_full, *ins, *made, *first)
+    attend_part(ns, heads, *first[:3], ins[8], ins[5], *attended, *second, late=late)
+    finish()
+
+
+def run_front(n, ns, heads, tok, wq, wk, wv, wo, gate, gq, gk, docs, turns):
     rows, depth = tok.shape
     tl = rows * n
-    lw = wq.shape[1]
+    block, lw = wq.shape
+    r = ns // heads
+    nq = ns // r * tl
+    nk = ns * tl
+    ff = gate.shape[1]
+    early = early_part(ff)
     dma = pltpu.SemaphoreType.DMA
     shape = jax.ShapeDtypeStruct
     return pl.pallas_call(
-        functools.partial(project_kernel, n, ns, depth),
+        functools.partial(front_kernel, n, ns, heads, depth),
         out_shape=(
             shape((tl, depth), BF16),
             shape((depth, 3 * lw), BF16),
-            shape((depth, lw + early_part(gate.shape[1])), BF16),
+            shape((depth, lw + early), BF16),
             shape((tl, lw), F32),
             shape((tl, lw), F32),
             shape((8, tl), F32),
-            shape((tl, lw), BF16),
-            shape((tl, lw), BF16),
-            shape((tl, lw), BF16),
             shape((tl, HEAD_DIM), F32),
             shape((tl, HEAD_DIM), F32),
+            shape((tl, lw), BF16),
+            shape((nq, HEAD_DIM), BF16),
+            shape((nk, HEAD_DIM), BF16),
+            shape((nk, HEAD_DIM), BF16),
+            shape((nq, HEAD_DIM), F32),
+            shape((ns // r, tl), F32),
+            shape((depth, ff - early), BF16),
         ),
         in_specs=[ANY] * 4 + [VMEM] * 4 + [SMEM, VMEM],
-        out_specs=(ANY,) * 3 + (VMEM,) * 8,
+        out_specs=(ANY,) * 5 + (VMEM,) * 4 + (ANY,) * 3 + (VMEM,) * 2 + (ANY,),
         scratch_shapes=[
+            pltpu.VMEM((tl, lw), BF16),
+            pltpu.VMEM((tl, lw), BF16),
+            pltpu.VMEM((tl, lw), BF16),
+            pltpu.VMEM((tl, lw), F32),
+            pltpu.VMEM((tl, lw), F32),
             pltpu.VMEM((tl, depth), BF16),
             pltpu.VMEM((depth, 3 * lw), BF16),
-            pltpu.VMEM((wq.shape[0], lw + early_part(gate.shape[1])), BF16),
+            pltpu.VMEM((block, lw + early), BF16),
             pltpu.VMEM((n, 8, tl), F32),
-            dma((7,)),
+            dma((9,)),
             dma((2, n, AG_CHUNKS)), dma((n, AG_CHUNKS)),
             *CubeGather.sems(ns), *CubeGather.sems(ns),
             dma((n,)), dma((n,)),
+            pltpu.VMEM((nq, HEAD_DIM), BF16),
+            pltpu.VMEM((nk, HEAD_DIM), BF16),
+            pltpu.VMEM((nk, HEAD_DIM), BF16),
+            pltpu.VMEM((nq, HEAD_DIM), BF16),
+            dma((heads,)), dma((ns // r,)),
+            dma((2, ns)), dma((ns,)),
+            dma((2, ns)), dma((ns,)),
+            dma((ns // r,)), dma((heads,)),
+            dma((4,)),
+            *CubeGather.sems(ns),
         ],
         compiler_params=pltpu.CompilerParams(
             collective_id=5, has_side_effects=True, vmem_limit_bytes=VMEM_BYTES
         ),
-        cost_estimate=pl.CostEstimate(flops=3 * 10**9, bytes_accessed=20 * 10**6, transcendentals=0),
-        name="project",
+        cost_estimate=pl.CostEstimate(flops=6 * 10**9, bytes_accessed=30 * 10**6, transcendentals=5 * 10**6),
+        name="front",
     )(tok, wq, wk, wv, wo, gate, gq, gk, docs, turns)
 
 
 def input_kernel(
     n, ns, depth_full,
-    dq, dk, dv, q_raw, k_raw, totals, gq, gk, cos, sin, x, w, att, dy1, attn_part, mlp_part, dy2_in, hidden_in,
+    dq, dk, dv, q_raw, k_raw, totals, gq, gk, cos, sin, x_in, w_in, att, dy1_in, attn_part, mlp_part, dy2_in, hidden_in,
     total, grad_q, grad_k, grad_v, grad_o, grad_down, gains,
-    dy2, hidden, lsem, dqkv, q_back, k_back, inner, land, message, message_z, gain_land,
+    x, w, dy1, dy2, hidden, lsem, dqkv, q_back, k_back, inner, land, message, message_z, gain_land,
     first, held, later, c0s, c0r, c1s, c1r,
     first_o, held_o, later_o, o0s, o0r, o1s, o1r,
     ss, sr, ms, mr, zs, zr, s1s, s1r,
@@ -1514,8 +1556,11 @@
 
     l_d = pltpu.make_async_copy(dy2_in, dy2, lsem.at[0])
     l_h = pltpu.make_async_copy(hidden_in.at[:, pl.ds(hidden_in.shape[1] - lw, lw)], hidden, lsem.at[1])
-    l_d.start()
-    l_h.start()
+    l_y = pltpu.make_async_copy(dy1_in, dy1, lsem.at[2])
+    l_w = pltpu.make_async_copy(w_in, w, lsem.at[3])
+    l_x = pltpu.make_async_copy(x_in, x, lsem.at[4])
+    for load in (l_d, l_h, l_y, l_w, l_x):
+        load.start()
 
     def turn_all():
         message[...] = jnp.zeros_like(message)
@@ -1554,8 +1599,8 @@
     message_z[s] = message[s]
     each_seq(lambda t: message_copy(t, s).start())
     dqkv[:, 2 * lw :] = dv[...]
-    l_d.wait()
-    l_h.wait()
+    for load in (l_d, l_h, l_y):
+        load.wait()
 
     def early_block(b):
         cols = rows_at(b, block)
@@ -1600,6 +1645,8 @@
                     act(2 * (slot - low) + j)
 
     done = 1 + half
+    l_w.wait()
+    l_x.wait()
     line.run(0, done, None, task)
     line.start_own()
     line.run(done, done + 3)
@@ -1651,12 +1698,15 @@
         out_shape=(shape((rows, depth), F32),)
         + (shape((block, lw), BF16),) * 3
         + (shape((lw, block), BF16), shape((lw, block), BF16), shape((8, block), F32)),
-        in_specs=[VMEM] * 16 + [ANY] * 2,
+        in_specs=[VMEM] * 10 + [ANY] * 2 + [VMEM, ANY, VMEM, VMEM] + [ANY] * 2,
         out_specs=(VMEM,) * 7,
         scratch_shapes=[
+            pltpu.VMEM(x.shape, BF16),
+            pltpu.VMEM(w.shape, BF16),
+            pltpu.VMEM((tl, depth), BF16),
             pltpu.VMEM((tl, depth), BF16),
             pltpu.VMEM((tl, lw), BF16),
-            dma((2,)),
+            dma((5,)),
             pltpu.VMEM((tl, 3 * lw), BF16),
             pltpu.VMEM((tl, lw), F32),
             pltpu.VMEM((tl, lw), F32),
@@ -1750,11 +1800,8 @@
     gq, gk = q_gain[None], k_gain[None]
     frequency = jnp.power(rope_base, -(jnp.arange(HEAD_DIM) % (HEAD_DIM // 2)).astype(F32) * (2.0 / HEAD_DIM))
 
-    x, w, more, q_raw, k_raw, totals, q_rot, k_rot, v_low, cos, sin = run_project(
-        nz, ns, tokens, q_weight, k_weight, v_weight, o_weight, gate_weight, gq, gk, doc_lengths, frequency[None]
-    )
-    attended, q_held, k_held, v_held, o_held, lse, gate_b = run_attend(
-        ns, heads, q_rot, k_rot, v_low, doc_lengths, gate_weight
+    x, w, more, q_raw, k_raw, totals, cos, sin, attended, q_held, k_held, v_held, o_held, lse, gate_b = run_front(
+        nz, ns, heads, tokens, q_weight, k_weight, v_weight, o_weight, gate_weight, gq, gk, doc_lengths, frequency[None]
     )
     output, h1r, branch, hidden, dy2, dg, du, mlp_part, up = run_forward(
         nz, ns, attended, tokens, cotangent, more, gate_b, up_weight, down_weight, attn_gain[None], mlp_gain[None]

time: 519 us -> 507 us (0.977)
  Pallas kernels: 509 us -> 497 us
    pallas_call x2 -> x1, Pallas kernels: 114 us -> 107 us  [run_front(): pl.pallas_call(functools.partial(front_kernel, n, ns, heads, depth), out_...]
where the time goes in v7:
time: 507 us; the launch traced here: 500 us
  Pallas kernels  497 us (98%)
    pallas_call x1, Pallas kernels, run_forward(): pl.pallas_call(functools.partial(forward_kernel, n, ns), out_shape=(shape...  169 us
    pallas_call x1, Pallas kernels, run_front(): pl.pallas_call(functools.partial(front_kernel, n, ns, heads, depth), out_...  107 us
    pallas_call x1, Pallas kernels, run_backward(): pl.pallas_call(functools.partial(backward_kernel, n, ns), out_shape=(shap...  95.1 us
    pallas_call x1, Pallas kernels, run_input(): pl.pallas_call(functools.partial(input_kernel, n, ns, depth), out_shape=(...  64.7 us
    pallas_call x1, Pallas kernels, run_attend_back(): pl.pallas_call(functools.partial(attend_back_kernel, ns, heads), out_shap...  55 us

profile of v7, /device:TPU:8, one launch (start us, length us, event | category | flops | bytes accessed | tf_op | source)
XLA Modules:
  0.0 500.1 jit_solution(10970372935911012330)
XLA Ops:
  0.6 0.5 fusion.3.refs_9_
  1.2 107.3 %front.1 = (bf16[512,2048]{1,0:T(8,128)(2,1)}, bf16[2048,1536]{1,0:T(8,128)(2,1)}, bf16[2048,1408]{1,0:T(8,128)(2,1)}, f32[512,512]{1,0:T(8,128)}, f32[512,512]{...) custom-call(bf16[128,2048]{1,0:T(8,128)(2,1)} %tok.1, ...), custom_call_target="tpu_custom_call" | custom-call | flops 6000000000 | bytes 30000000 | tf_op jit(solution)/shard_map/front/pallas_call | solution.py:1480
  108.4 168.8 %feed_forward.1 = (bf16[128,2048]{1,0:T(8,128)(2,1)}, bf16[512,2048]{1,0:T(8,128)(2,1)}, f32[128,2048]{1,0:T(8,128)}, bf16[512,2048]{1,0:T(8,128)(2,1)}, bf16[51...) custom-call(bf16[512,512]{1,0:T(8,128)(2,1)} %get-tuple-element.63.a, ...), custom_call_target="tpu_custom_call" | custom-call | flops 17999998976 | bytes 40000000 | tf_op jit(solution)/shard_map/feed_forward/pallas_call | solution.py:548
  277.2 95.1 %into_attention.1 = (f32[128,2048]{1,0:T(8,128)}, bf16[512,2048]{1,0:T(8,128)(2,1)}, bf16[512,512]{1,0:T(8,128)(2,1)}, f32[1,2048]{1,0:T(1,128)}, bf16[256,2048]{1,0:T(8,128)(2,1)}, /*index=5*/bf16[256,2048]{1,0:T(8,128)(2,1)}) custom-call(bf16[512,2048]{1,0:T(8,128)(2,1)} %get-tuple-element.67.dg_in, bf16[512,2048]{1,0:T(8,128)(2,1)} %get-tuple-element.68.du_in, ...), custom_call_target="tpu_custom_call" | custom-call | flops 17999998976 | bytes 30000000 | tf_op jit(solution)/shard_map/into_attention/pallas_call | solution.py:719
  372.3 55.0 %attend_back.1 = (bf16[512,512]{1,0:T(8,128)(2,1)}, bf16[512,512]{1,0:T(8,128)(2,1)}, bf16[512,512]{1,0:T(8,128)(2,1)}, bf16[1536,256]{1,0:T(8,128)(2,1)}) custom-call(bf16[512,512]{1,0:T(8,128)(2,1)} %get-tuple-element.74.do_in, s32[3]{0:T(128)} %docs.1, bf16[2048,128]{1,0:T(8,128)(2,1)} %get-tuple-element.75.q_in, ...), custom_call_target="tpu_custom_call" | custom-call | flops 8000000000 | bytes 10000000 | tf_op jit(solution)/shard_map/attend_back/pallas_call | solution.py:1220
  427.4 64.7 %into_input.1 = (f32[128,2048]{1,0:T(8,128)}, bf16[256,512]{1,0:T(8,128)(2,1)}, bf16[256,512]{1,0:T(8,128)(2,1)}, bf16[256,512]{1,0:T(8,128)(2,1)}, bf16[512,256...) custom-call(bf16[512,512]{1,0:T(8,128)(2,1)} %get-tuple-element.83.dq, ...), custom_call_target="tpu_custom_call" | custom-call | flops 8000000000 | bytes 30000000 | tf_op jit(solution)/shard_map/into_input/pallas_call | solution.py:1696
  492.1 1.4 fusion.4
  493.5 6.1 %widen.1 = (bf16[128,2048]{1,0:T(8,128)(2,1)}, f32[256,2048]{1,0:T(8,128)}, f32[256,2048]{1,0:T(8,128)}, f32[2048,256]{1,0:T(8,128)}, f32[256,512]{1,0:T(8,128)}...) custom-call(bf16[128,2048]{1,0:T(8,128)(2,1)} %get-tuple-element.66.refs_0_, ...), custom_call_target="tpu_custom_call" | custom-call | tf_op jit(solution)/shard_map/widen/pallas_call | solution.py:1767

commit v8 on v7

--- a/solution.py
+++ b/solution.py
@@ -43,6 +43,10 @@
     return ff * EARLY[0] // EARLY[1] // HEAD_DIM * HEAD_DIM
 
 
+def last_part(ff):
+    return ff // STEPS
+
+
 def rows_at(index, count):
     return pl.ds(pl.multiple_of(index * count, count), count)
 
@@ -217,7 +221,7 @@
     }
 
 
-BLOCK = 16
+BLOCK = 64
 
 
 def row_scale(block):
@@ -392,7 +396,7 @@
 
 def forward_kernel(
     n, ns,
-    att, tok, cot, more, gate_b, up, down, attn_gain, mlp_gain,
+    att, tok, cot, more, gate_b, gate_own, up, down, attn_gain, mlp_gain,
     out, h1r_out, branch_out, hidden_out, dy2_out, dg_out, du_out, gain_part, up_out,
     h1r, hidden, dy2, dg, du,
     wo, wd, wg, wu, land, branch, h1, second, g_pre, u_pre,
@@ -405,17 +409,20 @@
     width = depth // STEPS
     mine = rows_at(s, block)
     l_o = pltpu.make_async_copy(more.at[:, pl.ds(0, lw)], wo, wsem.at[0])
-    l_u = pltpu.make_async_copy(up, wu.at[mine], wsem.at[1])
+    last = last_part(ff)
+    l_u = pltpu.make_async_copy(up, wu.at[mine, pl.ds(last, ff)], wsem.at[1])
+    l_c = pltpu.make_async_copy(gate_own.at[:, pl.ds(ff - last, last)], wu.at[mine, pl.ds(0, last)], wsem.at[4])
     early = more.shape[1] - lw
     l_g = pltpu.make_async_copy(more.at[:, pl.ds(lw, early)], wg.at[:, pl.ds(0, early)], wsem.at[2])
-    l_h = pltpu.make_async_copy(gate_b, wg.at[:, pl.ds(early, ff - early)], wsem.at[3])
-    for copy in (l_o, l_u, l_g, l_h):
+    l_h = pltpu.make_async_copy(gate_b, wg.at[:, pl.ds(early, ff - early - last)], wsem.at[3])
+    for copy in (l_o, l_u, l_c, l_g, l_h):
         copy.start()
     cube_barrier(s, z, ns, n)
     cube_u = CubeGather(s, ns, wu, block, us, ur)
     cube_d = CubeGather(s, ns, wd, block, ds, dr)
     levels = cube_u.levels
     l_u.wait()
+    l_c.wait()
     cube_u.start()
     l_o.wait()
 
@@ -426,12 +433,13 @@
     line.run(0, STEPS)
     line.start_own()
     wd[mine, :] = jnp.transpose(down[...].astype(F32)).astype(BF16)
+    line.run(STEPS, 2 * STEPS)
     cube_u.level(0)
-    line.run(STEPS, 2 * STEPS)
+    line.run(2 * STEPS, 3 * STEPS)
     for i in range(1, levels - 1):
         cube_u.level(i)
     cube_d.start()
-    line.run(2 * STEPS, line.slots)
+    line.run(3 * STEPS, line.slots)
     line.own()
     line.finish()
     o_branch = pltpu.make_async_copy(branch, branch_out, osem.at[0])
@@ -455,15 +463,17 @@
     def up_block(src):
         at = rows_at(src, rows)
 
-        @pl.loop(0, STEPS)
-        def _(c):
+        def columns(c, gate):
             cols = rows_at(c, fw)
             x = h1r[at, :]
-            g = mm(x, wg[:, cols])
-            u = mm(x, wu[:, cols])
+            g = mm(x, gate)
+            u = mm(x, wu[:, pl.ds(pl.multiple_of(last + c * fw, HEAD_DIM), fw)])
             g_pre[at, cols] = g
             u_pre[at, cols] = u
             hidden[at, cols] = (g * sigmoid(g) * u).astype(BF16)
+
+        pl.loop(0, STEPS - 1)(lambda c: columns(c, wg[:, rows_at(c, fw)]))
+        columns(STEPS - 1, wu[:, :last])
 
     def weights_there():
         l_g.wait()
@@ -538,7 +548,7 @@
     cube_d.finish()
 
 
-def run_forward(n, ns, att, tok, cot, more, gate_b, up, down, attn_gain, mlp_gain):
+def run_forward(n, ns, att, tok, cot, more, gate_b, gate_own, up, down, attn_gain, mlp_gain):
     rows, depth = tok.shape
     tl, lw = att.shape
     ff = up.shape[1]
@@ -556,9 +566,9 @@
             shape((tl, ff), BF16),
             shape((tl, ff), BF16),
             shape((1, depth), F32),
-            shape((depth, ff), BF16),
+            shape((depth, ff + last_part(ff)), BF16),
         ),
-        in_specs=[VMEM, VMEM, VMEM, ANY, ANY, ANY, VMEM, VMEM, VMEM],
+        in_specs=[VMEM, VMEM, VMEM, ANY, ANY, ANY, ANY, VMEM, VMEM, VMEM],
         out_specs=(VMEM, ANY, ANY, ANY, ANY, ANY, ANY, VMEM, ANY),
         scratch_shapes=[
             pltpu.VMEM((tl, depth), BF16),
@@ -568,15 +578,15 @@
             pltpu.VMEM((tl, ff), BF16),
             pltpu.VMEM((depth, lw), BF16),
             pltpu.VMEM((depth, ff), BF16),
-            pltpu.VMEM((depth, ff), BF16),
-            pltpu.VMEM((depth, ff), BF16),
+            pltpu.VMEM((depth, ff - last_part(ff)), BF16),
+            pltpu.VMEM((depth, ff + last_part(ff)), BF16),
             pltpu.VMEM((2, n, STEPS, rows, depth // STEPS), BF16),
             pltpu.VMEM((rows, depth), F32),
             pltpu.VMEM((rows, depth), F32),
             pltpu.VMEM((rows, depth), F32),
             pltpu.VMEM((tl, ff), F32),
             pltpu.VMEM((tl, ff), F32),
-            dma((4,)),
+            dma((5,)),
             dma((5,)),
             dma((2, n)),
             *sems["gather"], *sems["scatter"], *sems["gather"], *sems["scatter"],
@@ -587,7 +597,7 @@
         ),
         cost_estimate=pl.CostEstimate(flops=18 * 10**9, bytes_accessed=40 * 10**6, transcendentals=2 * 10**6),
         name="feed_forward",
-    )(att, tok, cot, more, gate_b, up, down, attn_gain, mlp_gain)
+    )(att, tok, cot, more, gate_b, gate_own, up, down, attn_gain, mlp_gain)
 
 
 def backward_kernel(
@@ -605,13 +615,15 @@
     block = depth // ns
     width = depth // STEPS
     early = more.shape[1] - lw
+    last = last_part(ff)
 
     def weights_in(c):
         at = rows_at(c, width)
         return [
             pltpu.make_async_copy(more.at[at, pl.ds(lw, early)], wg.at[at, pl.ds(0, early)], wsem.at[0, c]),
-            pltpu.make_async_copy(gate_b.at[at], wg.at[at, pl.ds(early, ff - early)], wsem.at[1, c]),
-            pltpu.make_async_copy(up.at[at], wu.at[at], wsem.at[2, c]),
+            pltpu.make_async_copy(gate_b.at[at], wg.at[at, pl.ds(early, ff - early - last)], wsem.at[1, c]),
+            pltpu.make_async_copy(up.at[at, pl.ds(0, last)], wg.at[at, pl.ds(ff - last, last)], wsem.at[3, c]),
+            pltpu.make_async_copy(up.at[at, pl.ds(last, ff)], wu.at[at], wsem.at[2, c]),
         ]
 
     l_h = pltpu.make_async_copy(h1r_in, h1r, osem.at[0])
@@ -710,7 +722,7 @@
 def run_backward(n, ns, dg, du, h1r, cot, branch, more, gate_b, up, attn_gain):
     rows, depth = cot.shape
     tl, ff = dg.shape
-    lw = more.shape[1] + gate_b.shape[1] - ff
+    lw = more.shape[1] + gate_b.shape[1] + last_part(ff) - ff
     block = depth // ns
     dma = pltpu.SemaphoreType.DMA
     sems = line_sems(n)
@@ -738,7 +750,7 @@
             pltpu.VMEM((2, n, STEPS, rows, depth // STEPS), BF16),
             pltpu.VMEM((rows, depth), F32),
             first, held, later, held, later,
-            dma((3, STEPS)),
+            dma((4, STEPS)),
             dma((4,)),
             *sems["scatter"], *sems["gather"],
             *cube_sems, *cube_sems,
@@ -841,7 +853,7 @@
     kv = ((k_in, k_buf, ks, kr), (v_in, v_buf, vs, vr))
     block = gate.shape[0]
     cols = gate_out.shape[1]
-    own = gate.at[:, pl.ds(gate.shape[1] - cols, cols)]
+    own = gate.at[:, pl.ds(early_part(gate.shape[1]), cols)]
     own_gate = pltpu.make_async_copy(own, gate_out.at[rows_at(s, block)], local.at[0])
     cube = CubeGather(s, ns, gate_out, block, cs, cr, own)
     own_gate.start()
@@ -1494,7 +1506,7 @@
             shape((nk, HEAD_DIM), BF16),
             shape((nq, HEAD_DIM), F32),
             shape((ns // r, tl), F32),
-            shape((depth, ff - early), BF16),
+            shape((depth, ff - early - last_part(ff)), BF16),
         ),
         in_specs=[ANY] * 4 + [VMEM] * 4 + [SMEM, VMEM],
         out_specs=(ANY,) * 5 + (VMEM,) * 4 + (ANY,) * 3 + (VMEM,) * 2 + (ANY,),
@@ -1804,7 +1816,7 @@
         nz, ns, heads, tokens, q_weight, k_weight, v_weight, o_weight, gate_weight, gq, gk, doc_lengths, frequency[None]
     )
     output, h1r, branch, hidden, dy2, dg, du, mlp_part, up = run_forward(
-        nz, ns, attended, tokens, cotangent, more, gate_b, up_weight, down_weight, attn_gain[None], mlp_gain[None]
+        nz, ns, attended, tokens, cotangent, more, gate_b, gate_weight, up_weight, down_weight, attn_gain[None], mlp_gain[None]
     )
     middle, dy1, datt, attn_part, grad_gate, grad_up = run_backward(
         nz, ns, dg, du, h1r, cotangent, branch, more, gate_b, up, attn_gain[None]

time: 507 us -> 496 us (0.978)
  Pallas kernels: 497 us -> 485 us
    pallas_call x1, Pallas kernels: 107 us -> 98.1 us  [run_front(): pl.pallas_call(functools.partial(front_kernel, n, ns, heads, depth), out_...]
    pallas_call x1, Pallas kernels: 169 us -> 162 us  [run_forward(): pl.pallas_call(functools.partial(forward_kernel, n, ns), out_shape=(shape...]
where the time goes in v8:
time: 496 us; the launch traced here: 488 us
  Pallas kernels  485 us (98%)
    pallas_call x1, Pallas kernels, run_forward(): pl.pallas_call(functools.partial(forward_kernel, n, ns), out_shape=(shape...  162 us
    pallas_call x1, Pallas kernels, run_front(): pl.pallas_call(functools.partial(front_kernel, n, ns, heads, depth), out_...  98.1 us
    pallas_call x1, Pallas kernels, run_backward(): pl.pallas_call(functools.partial(backward_kernel, n, ns), out_shape=(shap...  97.2 us
    pallas_call x1, Pallas kernels, run_input(): pl.pallas_call(functools.partial(input_kernel, n, ns, depth), out_shape=(...  66.6 us
    pallas_call x1, Pallas kernels, run_attend_back(): pl.pallas_call(functools.partial(attend_back_kernel, ns, heads), out_shap...  55 us

profile of v8, /device:TPU:8, one launch (start us, length us, event | category | flops | bytes accessed | tf_op | source)
XLA Modules:
  0.0 488.1 jit_solution(9417652270166073917)
XLA Ops:
  0.6 0.5 fusion.3.refs_9_
  1.2 98.1 %front.1 = (bf16[512,2048]{1,0:T(8,128)(2,1)}, bf16[2048,1536]{1,0:T(8,128)(2,1)}, bf16[2048,1408]{1,0:T(8,128)(2,1)}, f32[512,512]{1,0:T(8,128)}, f32[512,512]{...) custom-call(bf16[128,2048]{1,0:T(8,128)(2,1)} %tok.1, ...), custom_call_target="tpu_custom_call" | custom-call | flops 6000000000 | bytes 30000000 | tf_op jit(solution)/shard_map/front/pallas_call | solution.py:1492
  99.2 162.1 %feed_forward.1 = (bf16[128,2048]{1,0:T(8,128)(2,1)}, bf16[512,2048]{1,0:T(8,128)(2,1)}, f32[128,2048]{1,0:T(8,128)}, bf16[512,2048]{1,0:T(8,128)(2,1)}, bf16[51...) custom-call(bf16[512,512]{1,0:T(8,128)(2,1)} %get-tuple-element.63.a, ...), custom_call_target="tpu_custom_call" | custom-call | flops 17999998976 | bytes 40000000 | tf_op jit(solution)/shard_map/feed_forward/pallas_call | solution.py:558
  261.4 97.2 %into_attention.1 = (f32[128,2048]{1,0:T(8,128)}, bf16[512,2048]{1,0:T(8,128)(2,1)}, bf16[512,512]{1,0:T(8,128)(2,1)}, f32[1,2048]{1,0:T(1,128)}, bf16[256,2048]{1,0:T(8,128)(2,1)}, /*index=5*/bf16[256,2048]{1,0:T(8,128)(2,1)}) custom-call(bf16[512,2048]{1,0:T(8,128)(2,1)} %get-tuple-element.67.dg_in, bf16[512,2048]{1,0:T(8,128)(2,1)} %get-tuple-element.68.du_in, ...), custom_call_target="tpu_custom_call" | custom-call | flops 17999998976 | bytes 30000000 | tf_op jit(solution)/shard_map/into_attention/pallas_call | solution.py:731
  358.6 55.0 %attend_back.1 = (bf16[512,512]{1,0:T(8,128)(2,1)}, bf16[512,512]{1,0:T(8,128)(2,1)}, bf16[512,512]{1,0:T(8,128)(2,1)}, bf16[1536,256]{1,0:T(8,128)(2,1)}) custom-call(bf16[512,512]{1,0:T(8,128)(2,1)} %get-tuple-element.74.do_in, s32[3]{0:T(128)} %docs.1, bf16[2048,128]{1,0:T(8,128)(2,1)} %get-tuple-element.75.q_in, ...), custom_call_target="tpu_custom_call" | custom-call | flops 8000000000 | bytes 10000000 | tf_op jit(solution)/shard_map/attend_back/pallas_call | solution.py:1232
  413.6 66.6 %into_input.1 = (f32[128,2048]{1,0:T(8,128)}, bf16[256,512]{1,0:T(8,128)(2,1)}, bf16[256,512]{1,0:T(8,128)(2,1)}, bf16[256,512]{1,0:T(8,128)(2,1)}, bf16[512,256...) custom-call(bf16[512,512]{1,0:T(8,128)(2,1)} %get-tuple-element.83.dq, ...), custom_call_target="tpu_custom_call" | custom-call | flops 8000000000 | bytes 30000000 | tf_op jit(solution)/shard_map/into_input/pallas_call | solution.py:1708
  480.2 1.4 fusion.4
  481.6 6.1 %widen.1 = (bf16[128,2048]{1,0:T(8,128)(2,1)}, f32[256,2048]{1,0:T(8,128)}, f32[256,2048]{1,0:T(8,128)}, f32[2048,256]{1,0:T(8,128)}, f32[256,512]{1,0:T(8,128)}...) custom-call(bf16[128,2048]{1,0:T(8,128)(2,1)} %get-tuple-element.66.refs_0_, ...), custom_call_target="tpu_custom_call" | custom-call | tf_op jit(solution)/shard_map/widen/pallas_call | solution.py:1779

commit v9 on v8

--- a/solution.py
+++ b/solution.py
@@ -130,7 +130,8 @@
 
 
 class LineScatter:
-    def __init__(self, z, n, partial, land, send_sem, recv_sem, total):
+    def __init__(self, z, n, partial, land, send_sem, recv_sem, total, own_late=False):
+        self.own_late = own_late
         self.z, self.n, self.partial, self.land, self.total = z, n, partial, land, total
         self.send_sem, self.recv_sem = send_sem, recv_sem
 
@@ -178,15 +179,20 @@
 
                     self.copy(d, c, up).start()
 
+            if self.own_late:
+                @pl.when(slot >= self.slots - STEPS)
+                def _():
+                    self.own_chunk(slot - (self.slots - STEPS))
+
             if after is not None:
                 after(slot)
 
+    def own_chunk(self, c):
+        width = self.total.shape[1] // STEPS
+        self.total[:, rows_at(c, width)] = self.partial(self.z, c)
+
     def start_own(self):
-        width = self.total.shape[1] // STEPS
-
-        @pl.loop(0, STEPS)
-        def _(c):
-            self.total[:, rows_at(c, width)] = self.partial(self.z, c)
+        pl.loop(0, STEPS)(self.own_chunk)
 
     def own(self):
         z, n, total = self.z, self.n, self.total
@@ -648,7 +654,7 @@
         at, cols = rows_at(d, rows), rows_at(c, width)
         return mm(dg[at, :], wg[cols, :], NT) + mm(du[at, :], wu[cols, :], NT)
 
-    line = LineScatter(z, n, in_part, land, s1s, s1r, total)
+    line = LineScatter(z, n, in_part, land, s1s, s1r, total, True)
     half = ns // 2
 
     def there(slot):
@@ -677,7 +683,6 @@
     cube_g.send_core()
     l_du.wait()
     line.run(0, 2 * STEPS, there, task)
-    line.start_own()
     line.run(2 * STEPS, line.slots, None, task)
 
     @pl.loop(line.slots, max(line.slots, half // 2 + 2 * half))
@@ -1021,10 +1026,10 @@
         copy.wait()
 
 
-def attend_back_kernel(
-    ns, heads, do_in, docs, q_in, k_in, v_in, o_in, lse, dy2_in, hidden_in,
-    dq, dk, dv, grad_down,
-    q_buf, k_buf, v_buf, o_buf, dy2, hidden, lsem,
+def attend_back_part(
+    n, ns, heads, free, do_in, docs, q_in, k_in, v_in, o_in, lse, dy2_in, hidden_in,
+    grad_down,
+    q_buf, k_buf, v_buf, o_buf, dy2, hidden, lsem, dq, dk, dv,
     do_buf, dq_low, dk_acc, dv_acc, low, pair, land,
     first, held, later, ca, cb, cc, cd,
     ds_, dr_, ps, pr, gs, gr, qs, qr,
@@ -1049,7 +1054,7 @@
         dk_acc[...] = jnp.zeros_like(dk_acc)
         dv_acc[...] = jnp.zeros_like(dv_acc)
 
-    seq_barrier(s, ns, clear)
+    cross_barrier(s, lax.axis_index("head"), ns, n, clear)
     to_sub, to_row = share_of(s, ns, r)
 
     def copy(src, dst, send, recv, t):
@@ -1175,6 +1180,8 @@
             def _():
                 land[w, slot, :, head_cols(mine)] = low[w, at, :]
 
+    free()
+
     @pl.loop(0, heads)
     def _(h):
         for w in range(2):
@@ -1198,69 +1205,32 @@
             do_copy(h).wait_send()
             copy(dq_low.at[rows_at(0, tl)], dq.at[:, head_cols(h)], qs.at[0], qr.at[h], s ^ 1).wait_recv()
 
-    @pl.loop(0, blocks)
-    def _(i):
-        src = source_of(sub, i, ns, r)
-
-        @pl.when(src != s)
-        def _():
-            dq_copy(i, src).wait_send()
-
-    @pl.loop(0, half)
-    def _(i):
-        for w in range(2):
-            pair_copy(w, i).wait_send()
-
-            @pl.when(2 * i + parity != s)
+    def late():
+        for i in range(1, cube.stages):
+            cube.step(i)
+        grad_down[...] = jnp.transpose(held[0].astype(F32)).astype(BF16)
+
+    def finish():
+        @pl.loop(0, blocks)
+        def _(i):
+            src = source_of(sub, i, ns, r)
+
+            @pl.when(src != s)
             def _():
-                back_copy(w, i).wait_send()
-
-    for i in range(1, cube.stages):
-        cube.step(i)
-    grad_down[...] = jnp.transpose(held[0].astype(F32)).astype(BF16)
-    cube.core_sent()
-    cube.finish()
-
-
-def run_attend_back(ns, heads, do, docs, q, k, v, o, lse, dy2, hidden):
-    tl, lw = do.shape
-    r = ns // heads
-    nq = ns // r * tl
-    nk = ns * tl
-    dma = pltpu.SemaphoreType.DMA
-    shape = jax.ShapeDtypeStruct
-    return pl.pallas_call(
-        functools.partial(attend_back_kernel, ns, heads),
-        out_shape=(shape((tl, lw), BF16),) * 3 + (shape((hidden.shape[1] - lw, dy2.shape[1] // ns), BF16),),
-        in_specs=[VMEM, SMEM] + [ANY] * 4 + [VMEM] + [ANY] * 2,
-        out_specs=(VMEM,) * 4,
-        scratch_shapes=[
-            pltpu.VMEM((nq, HEAD_DIM), BF16),
-            pltpu.VMEM((nk, HEAD_DIM), BF16),
-            pltpu.VMEM((nk, HEAD_DIM), BF16),
-            pltpu.VMEM((nq, HEAD_DIM), F32),
-            pltpu.VMEM(dy2.shape, BF16),
-            pltpu.VMEM(hidden.shape, BF16),
-            dma((6,)),
-            pltpu.VMEM((nq, HEAD_DIM), BF16),
-            pltpu.VMEM((nq, HEAD_DIM), BF16),
-            pltpu.VMEM((nk, HEAD_DIM), F32),
-            pltpu.VMEM((nk, HEAD_DIM), F32),
-            pltpu.VMEM((2, nk, HEAD_DIM), BF16),
-            pltpu.VMEM((2, nk // 2, HEAD_DIM), BF16),
-            pltpu.VMEM((2, r // 2, tl, lw), BF16),
-            *CubeScatter.scratch(ns, dy2.shape[1] // ns, hidden.shape[1] - lw),
-            dma((heads,)), dma((ns // r,)),
-            dma((2, ns // 2)), dma((2, ns // 2)),
-            dma((2, ns // 2)), dma((2, heads, r // 2)),
-            dma((ns // r,)), dma((heads,)),
-        ],
-        compiler_params=pltpu.CompilerParams(
-            collective_id=4, has_side_effects=True, vmem_limit_bytes=VMEM_BYTES
-        ),
-        cost_estimate=pl.CostEstimate(flops=8 * 10**9, bytes_accessed=10 * 10**6, transcendentals=5 * 10**6),
-        name="attend_back",
-    )(do, docs, q, k, v, o, lse, dy2, hidden)
+                dq_copy(i, src).wait_send()
+
+        @pl.loop(0, half)
+        def _(i):
+            for w in range(2):
+                pair_copy(w, i).wait_send()
+
+                @pl.when(2 * i + parity != s)
+                def _():
+                    back_copy(w, i).wait_send()
+
+        cube.finish()
+
+    return cube.core_sent, late, finish
 
 
 def cross_barrier(s, z, ns, n, between=None):
@@ -1543,13 +1513,14 @@
     )(tok, wq, wk, wv, wo, gate, gq, gk, docs, turns)
 
 
-def input_kernel(
-    n, ns, depth_full,
-    dq, dk, dv, q_raw, k_raw, totals, gq, gk, cos, sin, x_in, w_in, att, dy1_in, attn_part, mlp_part, dy2_in, hidden_in,
+def input_part(
+    n, ns, depth_full, sent, late,
+    dq, dk, dv, q_raw, k_raw, totals, gq, gk, cos, sin, x_in, w_in, att, dy1_in, attn_part, mlp_part,
     total, grad_q, grad_k, grad_v, grad_o, grad_down, gains,
-    x, w, dy1, dy2, hidden, lsem, dqkv, q_back, k_back, inner, land, message, message_z, gain_land,
-    first, held, later, c0s, c0r, c1s, c1r,
-    first_o, held_o, later_o, o0s, o0r, o1s, o1r,
+    dy2, hidden, first, q_back, k_back,
+    w, dy1, lsem, dqkv, inner, land, message, message_z, gain_land,
+    held, later, c0s, c0r, c1s, c1r,
+    held_o, later_o, o0s, o0r, o1s, o1r,
     ss, sr, ms, mr, zs, zr, s1s, s1r,
 ):
     s, z = lax.axis_index("seq"), lax.axis_index("head")
@@ -1566,13 +1537,10 @@
     todo = ((dq, q_raw, gq, q_back), (dk, k_raw, gk, k_back))
     products = []
 
-    l_d = pltpu.make_async_copy(dy2_in, dy2, lsem.at[0])
-    l_h = pltpu.make_async_copy(hidden_in.at[:, pl.ds(hidden_in.shape[1] - lw, lw)], hidden, lsem.at[1])
-    l_y = pltpu.make_async_copy(dy1_in, dy1, lsem.at[2])
-    l_w = pltpu.make_async_copy(w_in, w, lsem.at[3])
-    l_x = pltpu.make_async_copy(x_in, x, lsem.at[4])
-    for load in (l_d, l_h, l_y, l_w, l_x):
-        load.start()
+    x = dy2
+    l_y = pltpu.make_async_copy(dy1_in, dy1, lsem.at[0])
+    l_w = pltpu.make_async_copy(w_in, w, lsem.at[1])
+    l_x = pltpu.make_async_copy(x_in, x, lsem.at[2])
 
     def turn_all():
         message[...] = jnp.zeros_like(message)
@@ -1580,11 +1548,11 @@
             product = jnp.zeros((tl, HEAD_DIM), F32)
             for h in range(heads):
                 cols = slice(h * HEAD_DIM, (h + 1) * HEAD_DIM)
-                hat = raw[:, cols] * scales[i]
+                hat = raw[h * tl : (h + 1) * tl, :] * scales[i]
                 turned = turn_back(grad[:, cols].astype(F32), cos[...], sin[...])
                 message[0, pl.ds(i, 1), cols] = jnp.sum(turned * hat, axis=0, keepdims=True)
                 turned = turned * gain[:, head_gain(h)]
-                back[:, cols] = turned
+                back[h * tl : (h + 1) * tl, :] = turned
                 product = product + turned * hat
             products.append(product)
         inner[z] = row_sums(*products)
@@ -1594,7 +1562,7 @@
             for i, part in enumerate((attn_part, mlp_part)):
                 message[t, pl.ds(i, 1), pl.ds(lw, block)] = part[:, t * block : (t + 1) * block]
 
-    cross_barrier(s, z, ns, n, turn_all)
+    turn_all()
     small = SmallExchange("head", z, n, inner, ss, sr)
     small.start()
 
@@ -1611,18 +1579,21 @@
     message_z[s] = message[s]
     each_seq(lambda t: message_copy(t, s).start())
     dqkv[:, 2 * lw :] = dv[...]
-    for load in (l_d, l_h, l_y):
-        load.wait()
+    l_y.wait()
+    ff = hidden.shape[1]
 
     def early_block(b):
         cols = rows_at(b, block)
-        return jnp.concatenate([mm(dy1[:, cols], att[...], TN), mm(dy2[:, cols], hidden[...], TN)], axis=1)
+        return jnp.concatenate([mm(dy1[:, cols], att[...], TN), mm(dy2[:, cols], hidden[:, ff - lw :], TN)], axis=1)
 
     cube_o = CubeScatter(
-        s, ns, early_block, block, first_o, held_o, later_o, (o0s, o0r, o1s, o1r)
+        s, ns, early_block, block, first.at[:, :, pl.ds(0, 2 * lw)], held_o, later_o, (o0s, o0r, o1s, o1r)
     )
+    sent()
     cube_o.send_core()
     cube_o.add_core()
+    l_x.start()
+    late()
     small.receive()
     sums = inner[0]
     for k in range(1, n):
@@ -1632,7 +1603,7 @@
         for h in range(heads):
             cols = slice(h * HEAD_DIM, (h + 1) * HEAD_DIM)
             to = slice(i * lw + h * HEAD_DIM, i * lw + (h + 1) * HEAD_DIM)
-            dqkv[:, to] = (scales[i] * (back[:, cols] - raw[:, cols] * scales[i] * mean)).astype(BF16)
+            dqkv[:, to] = (scales[i] * (back[h * tl : (h + 1) * tl, :] - raw[h * tl : (h + 1) * tl, :] * scales[i] * mean)).astype(BF16)
 
     width = depth // STEPS
 
@@ -1644,7 +1615,7 @@
         return mm(dqkv[rows_at(d, rows), :], w[rows_at(c, width), :], NT)
 
     cube = CubeScatter(s, ns, weight_block, block, first, held, later, (c0s, c0r, c1s, c1r))
-    line = LineScatter(z, n, in_part, land, s1s, s1r, total)
+    line = LineScatter(z, n, in_part, land, s1s, s1r, total, True)
     half = ns // 2
 
     def task(slot):
@@ -1659,8 +1630,8 @@
     done = 1 + half
     l_w.wait()
     l_x.wait()
+    cube_o.core_sent()
     line.run(0, done, None, task)
-    line.start_own()
     line.run(done, done + 3)
     for i in range(cube.stages - 1):
         cube_o.step(i)
@@ -1691,55 +1662,108 @@
     for k in range(1, n):
         both = both + gain_land[k, pl.ds(0, 2), pl.ds(lw, block)]
     gains[2:4, :] = both
-    for one in (cube, cube_o):
-        one.core_sent()
-        one.finish()
+    cube.core_sent()
+    cube.finish()
+    cube_o.finish()
     line.finish()
     small.finish()
     rounds.finish()
 
 
-def run_input(n, ns, dq, dk, dv, q_raw, k_raw, totals, gq, gk, cos, sin, x, w, att, dy1, attn_part, mlp_part, dy2, hidden):
-    tl, lw = dq.shape
+def back_kernel(n, ns, heads, depth_full, *refs):
+    ins, more, refs = refs[:9], refs[9:22], refs[22:]
+    down, outs, refs = refs[0], refs[1:8], refs[8:]
+    held, rest, raw_sem = refs[:32], refs[32:-1], refs[-1]
+    dy2, hidden, dq, dk, dv, dk_acc, first = held[4], held[5], *held[7:10], held[12], held[17]
+    half, tl = dk_acc.shape[0] // 2, dq.shape[0]
+    back, raws = ([acc.at[pl.ds(i * half, tl * heads)] for i in range(2)] for acc in (dk_acc, held[13]))
+    raw_loads = [
+        pltpu.make_async_copy(m.at[:, pl.ds(h * HEAD_DIM, HEAD_DIM)], to.at[pl.ds(h * tl, tl)], raw_sem.at[i, h])
+        for i, (m, to) in enumerate(zip(more[:2], raws))
+        for h in range(heads)
+    ]
+
+    def free():
+        for load in raw_loads:
+            load.start()
+
+    starts = [
+        pltpu.make_async_copy(more[10], rest[1], rest[2].at[0]), pltpu.make_async_copy(more[8], rest[0], rest[2].at[1])
+    ]
+    for load in starts:
+        load.start()
+    sent, late, finish = attend_back_part(n, ns, heads, free, *ins, down, *held)
+    for load in raw_loads:
+        load.wait()
+    input_part(n, ns, depth_full, sent, late, dq, dk, dv, *raws, *more[2:], *outs, dy2, hidden, first, *back, *rest)
+    finish()
+
+
+def run_back(n, ns, heads, do, docs, q, k, v, o, lse, dy2, hidden, *more):
+    q_raw, k_raw, totals, gq, gk, cos, sin, x, w, att, dy1, attn_part, mlp_part = more
+    tl, lw = do.shape
     rows, depth = tl // n, x.shape[1]
     block = depth // ns
+    ff = hidden.shape[1]
+    r = ns // heads
+    nq = ns // r * tl
+    nk = ns * tl
     dma = pltpu.SemaphoreType.DMA
     shape = jax.ShapeDtypeStruct
+    first, held, later, *cube_sems = CubeScatter.scratch(ns, block, 3 * lw)
     return pl.pallas_call(
-        functools.partial(input_kernel, n, ns, depth),
-        out_shape=(shape((rows, depth), F32),)
+        functools.partial(back_kernel, n, ns, heads, depth),
+        out_shape=(shape((ff - lw, block), BF16), shape((rows, depth), F32))
         + (shape((block, lw), BF16),) * 3
         + (shape((lw, block), BF16), shape((lw, block), BF16), shape((8, block), F32)),
-        in_specs=[VMEM] * 10 + [ANY] * 2 + [VMEM, ANY, VMEM, VMEM] + [ANY] * 2,
-        out_specs=(VMEM,) * 7,
+        in_specs=[VMEM, SMEM] + [ANY] * 4 + [VMEM] + [ANY] * 4 + [VMEM] * 5 + [ANY] * 2 + [VMEM, ANY, VMEM, VMEM],
+        out_specs=(VMEM,) * 8,
         scratch_shapes=[
-            pltpu.VMEM(x.shape, BF16),
+            pltpu.VMEM((nq, HEAD_DIM), BF16),
+            pltpu.VMEM((nk, HEAD_DIM), BF16),
+            pltpu.VMEM((nk, HEAD_DIM), BF16),
+            pltpu.VMEM((nq, HEAD_DIM), F32),
+            pltpu.VMEM(dy2.shape, BF16),
+            pltpu.VMEM(hidden.shape, BF16),
+            dma((6,)),
+            pltpu.VMEM((tl, lw), BF16),
+            pltpu.VMEM((tl, lw), BF16),
+            pltpu.VMEM((tl, lw), BF16),
+            pltpu.VMEM((nq, HEAD_DIM), BF16),
+            pltpu.VMEM((nq, HEAD_DIM), BF16),
+            pltpu.VMEM((nk, HEAD_DIM), F32),
+            pltpu.VMEM((nk, HEAD_DIM), F32),
+            pltpu.VMEM((2, nk, HEAD_DIM), BF16),
+            pltpu.VMEM((2, nk // 2, HEAD_DIM), BF16),
+            pltpu.VMEM((2, r // 2, tl, lw), BF16),
+            *CubeScatter.scratch(ns, block, ff - lw),
+            dma((heads,)), dma((ns // r,)),
+            dma((2, ns // 2)), dma((2, ns // 2)),
+            dma((2, ns // 2)), dma((2, heads, r // 2)),
+            dma((ns // r,)), dma((heads,)),
             pltpu.VMEM(w.shape, BF16),
             pltpu.VMEM((tl, depth), BF16),
-            pltpu.VMEM((tl, depth), BF16),
-            pltpu.VMEM((tl, lw), BF16),
-            dma((5,)),
+            dma((3,)),
             pltpu.VMEM((tl, 3 * lw), BF16),
-            pltpu.VMEM((tl, lw), F32),
-            pltpu.VMEM((tl, lw), F32),
             pltpu.VMEM((n, 8, tl), F32),
             pltpu.VMEM((2, n, STEPS, rows, depth // STEPS), BF16),
             pltpu.VMEM((ns, 8, lw + block), F32),
             pltpu.VMEM((ns, 8, lw + block), F32),
             pltpu.VMEM((n, 8, lw + block), F32),
-            *CubeScatter.scratch(ns, block, 3 * lw),
-            *CubeScatter.scratch(ns, block, 2 * lw),
+            held, later, *cube_sems,
+            *CubeScatter.scratch(ns, block, 2 * lw)[1:],
             dma((n,)), dma((n,)),
             dma((ns,)), dma((ns,)),
             dma((n,)), dma((n,)),
             *line_sems(n)["scatter"],
+            dma((2, heads)),
         ],
         compiler_params=pltpu.CompilerParams(
             collective_id=6, has_side_effects=True, vmem_limit_bytes=VMEM_BYTES
         ),
-        cost_estimate=pl.CostEstimate(flops=8 * 10**9, bytes_accessed=30 * 10**6, transcendentals=0),
-        name="into_input",
-    )(dq, dk, dv, q_raw, k_raw, totals, gq, gk, cos, sin, x, w, att, dy1, attn_part, mlp_part, dy2, hidden)
+        cost_estimate=pl.CostEstimate(flops=16 * 10**9, bytes_accessed=40 * 10**6, transcendentals=5 * 10**6),
+        name="back",
+    )(do, docs, q, k, v, o, lse, dy2, hidden, *more)
 
 
 def widen_kernel(count, *refs):
@@ -1821,11 +1845,9 @@
     middle, dy1, datt, attn_part, grad_gate, grad_up = run_backward(
         nz, ns, dg, du, h1r, cotangent, branch, more, gate_b, up, attn_gain[None]
     )
-    dq, dk, dv, down_a = run_attend_back(
-        ns, heads, datt, doc_lengths, q_held, k_held, v_held, o_held, lse, dy2, hidden
-    )
-    last, grad_q, grad_k, grad_v, grad_o, down_b, gains = run_input(
-        nz, ns, dq, dk, dv, q_raw, k_raw, totals, gq, gk, cos, sin, x, w, attended, dy1, attn_part, mlp_part, dy2, hidden
+    down_a, last, grad_q, grad_k, grad_v, grad_o, down_b, gains = run_back(
+        nz, ns, heads, datt, doc_lengths, q_held, k_held, v_held, o_held, lse, dy2, hidden,
+        q_raw, k_raw, totals, gq, gk, cos, sin, x, w, attended, dy1, attn_part, mlp_part,
     )
     shape = jax.ShapeDtypeStruct
     small = shape((block, lw), F32)

time: 496 us -> 490 us (0.988)
  Pallas kernels: 485 us -> 478 us
    pallas_call x2 -> x1, Pallas kernels: 122 us -> 115 us  [run_back(): pl.pallas_call(functools.partial(back_kernel, n, ns, heads, depth), out_s...]
where the time goes in v9:
time: 490 us; the launch traced here: 481 us
  Pallas kernels  478 us (98%)
    pallas_call x1, Pallas kernels, run_forward(): pl.pallas_call(functools.partial(forward_kernel, n, ns), out_shape=(shape...  162 us
    pallas_call x1, Pallas kernels, run_back(): pl.pallas_call(functools.partial(back_kernel, n, ns, heads, depth), out_s...  115 us
    pallas_call x1, Pallas kernels, run_front(): pl.pallas_call(functools.partial(front_kernel, n, ns, heads, depth), out_...  98.1 us
    pallas_call x1, Pallas kernels, run_backward(): pl.pallas_call(functools.partial(backward_kernel, n, ns), out_shape=(shap...  96.2 us

profile of v9, /device:TPU:8, one launch (start us, length us, event | category | flops | bytes accessed | tf_op | source)
XLA Modules:
  0.0 480.7 jit_solution(14378985964377544218)
XLA Ops:
  0.6 0.5 fusion.3.refs_9_
  1.2 98.1 %front.1 = (bf16[512,2048]{1,0:T(8,128)(2,1)}, bf16[2048,1536]{1,0:T(8,128)(2,1)}, bf16[2048,1408]{1,0:T(8,128)(2,1)}, f32[512,512]{1,0:T(8,128)}, f32[512,512]{...) custom-call(bf16[128,2048]{1,0:T(8,128)(2,1)} %tok.1, ...), custom_call_target="tpu_custom_call" | custom-call | flops 6000000000 | bytes 30000000 | tf_op jit(solution)/shard_map/front/pallas_call | solution.py:1462
  99.3 162.1 %feed_forward.1 = (bf16[128,2048]{1,0:T(8,128)(2,1)}, bf16[512,2048]{1,0:T(8,128)(2,1)}, f32[128,2048]{1,0:T(8,128)}, bf16[512,2048]{1,0:T(8,128)(2,1)}, bf16[51...) custom-call(bf16[512,512]{1,0:T(8,128)(2,1)} %get-tuple-element.60.a, ...), custom_call_target="tpu_custom_call" | custom-call | flops 17999998976 | bytes 40000000 | tf_op jit(solution)/shard_map/feed_forward/pallas_call | solution.py:564
  261.4 96.2 %into_attention.1 = (f32[128,2048]{1,0:T(8,128)}, bf16[512,2048]{1,0:T(8,128)(2,1)}, bf16[512,512]{1,0:T(8,128)(2,1)}, f32[1,2048]{1,0:T(1,128)}, bf16[256,2048]{1,0:T(8,128)(2,1)}, /*index=5*/bf16[256,2048]{1,0:T(8,128)(2,1)}) custom-call(bf16[512,2048]{1,0:T(8,128)(2,1)} %get-tuple-element.64.dg_in, bf16[512,2048]{1,0:T(8,128)(2,1)} %get-tuple-element.65.du_in, ...), custom_call_target="tpu_custom_call" | custom-call | flops 17999998976 | bytes 30000000 | tf_op jit(solution)/shard_map/into_attention/pallas_call | solution.py:736
  357.6 115.2 %back.1 = (bf16[1536,256]{1,0:T(8,128)(2,1)}, f32[128,2048]{1,0:T(8,128)}, bf16[256,512]{1,0:T(8,128)(2,1)}, bf16[256,512]{1,0:T(8,128)(2,1)}, bf16[256,512]{1,0...) custom-call(bf16[512,512]{1,0:T(8,128)(2,1)} %get-tuple-element.71.refs_0_, ...), custom_call_target="tpu_custom_call" | custom-call | flops 16000000000 | bytes 40000000 | tf_op jit(solution)/shard_map/back/pallas_call | solution.py:1714
  472.8 1.4 fusion.4
  474.2 6.1 %widen.1 = (bf16[128,2048]{1,0:T(8,128)(2,1)}, f32[256,2048]{1,0:T(8,128)}, f32[256,2048]{1,0:T(8,128)}, f32[2048,256]{1,0:T(8,128)}, f32[256,512]{1,0:T(8,128)}...) custom-call(bf16[128,2048]{1,0:T(8,128)(2,1)} %get-tuple-element.63.refs_0_, ...), custom_call_target="tpu_custom_call" | custom-call | tf_op jit(solution)/shard_map/widen/pallas_call | solution.py:1803

commit v10 on v9

--- a/solution.py
+++ b/solution.py
@@ -16,7 +16,7 @@
 BF16 = jnp.bfloat16
 STEPS = 4
 LAG = 1
-EARLY = (7, 16)
+EARLY = (10, 16)
 AG_CHUNKS = 2
 VMEM_BYTES = 62 * 1024 * 1024
 ANY = pl.BlockSpec(memory_space=pl.ANY)

time: 490 us -> 494 us (level)
  Pallas kernels: 478 us -> 483 us
    pallas_call x1, Pallas kernels: 98.1 us -> 104 us  [run_front(): pl.pallas_call(functools.partial(front_kernel, n, ns, heads, depth), out_...]
where the time goes in v10:
time: 494 us; the launch traced here: 486 us
  Pallas kernels  483 us (98%)
    pallas_call x1, Pallas kernels, run_forward(): pl.pallas_call(functools.partial(forward_kernel, n, ns), out_shape=(shape...  163 us
    pallas_call x1, Pallas kernels, run_back(): pl.pallas_call(functools.partial(back_kernel, n, ns, heads, depth), out_s...  116 us
    pallas_call x1, Pallas kernels, run_front(): pl.pallas_call(functools.partial(front_kernel, n, ns, heads, depth), out_...  104 us
    pallas_call x1, Pallas kernels, run_backward(): pl.pallas_call(functools.partial(backward_kernel, n, ns), out_shape=(shap...  93.6 us

profile of v10, /device:TPU:8, one launch (start us, length us, event | category | flops | bytes accessed | tf_op | source)
XLA Modules:
  0.0 485.9 jit_solution(2182186772543960731)
XLA Ops:
  0.6 0.5 fusion.3.refs_9_
  1.2 104.1 %front.1 = (bf16[512,2048]{1,0:T(8,128)(2,1)}, bf16[2048,1536]{1,0:T(8,128)(2,1)}, bf16[2048,1792]{1,0:T(8,128)(2,1)}, f32[512,512]{1,0:T(8,128)}, f32[512,512]{...) custom-call(bf16[128,2048]{1,0:T(8,128)(2,1)} %tok.1, ...), custom_call_target="tpu_custom_call" | custom-call | flops 6000000000 | bytes 30000000 | tf_op jit(solution)/shard_map/front/pallas_call | solution.py:1462
  105.3 163.1 %feed_forward.1 = (bf16[128,2048]{1,0:T(8,128)(2,1)}, bf16[512,2048]{1,0:T(8,128)(2,1)}, f32[128,2048]{1,0:T(8,128)}, bf16[512,2048]{1,0:T(8,128)(2,1)}, bf16[51...) custom-call(bf16[512,512]{1,0:T(8,128)(2,1)} %get-tuple-element.60.a, ...), custom_call_target="tpu_custom_call" | custom-call | flops 17999998976 | bytes 40000000 | tf_op jit(solution)/shard_map/feed_forward/pallas_call | solution.py:564
  268.4 93.6 %into_attention.1 = (f32[128,2048]{1,0:T(8,128)}, bf16[512,2048]{1,0:T(8,128)(2,1)}, bf16[512,512]{1,0:T(8,128)(2,1)}, f32[1,2048]{1,0:T(1,128)}, bf16[256,2048]{1,0:T(8,128)(2,1)}, /*index=5*/bf16[256,2048]{1,0:T(8,128)(2,1)}) custom-call(bf16[512,2048]{1,0:T(8,128)(2,1)} %get-tuple-element.64.dg_in, bf16[512,2048]{1,0:T(8,128)(2,1)} %get-tuple-element.65.du_in, ...), custom_call_target="tpu_custom_call" | custom-call | flops 17999998976 | bytes 30000000 | tf_op jit(solution)/shard_map/into_attention/pallas_call | solution.py:736
  362.0 116.0 %back.1 = (bf16[1536,256]{1,0:T(8,128)(2,1)}, f32[128,2048]{1,0:T(8,128)}, bf16[256,512]{1,0:T(8,128)(2,1)}, bf16[256,512]{1,0:T(8,128)(2,1)}, bf16[256,512]{1,0...) custom-call(bf16[512,512]{1,0:T(8,128)(2,1)} %get-tuple-element.71.refs_0_, ...), custom_call_target="tpu_custom_call" | custom-call | flops 16000000000 | bytes 40000000 | tf_op jit(solution)/shard_map/back/pallas_call | solution.py:1714
  478.0 1.4 fusion.4
  479.4 6.1 %widen.1 = (bf16[128,2048]{1,0:T(8,128)(2,1)}, f32[256,2048]{1,0:T(8,128)}, f32[256,2048]{1,0:T(8,128)}, f32[2048,256]{1,0:T(8,128)}, f32[256,512]{1,0:T(8,128)}...) custom-call(bf16[128,2048]{1,0:T(8,128)(2,1)} %get-tuple-element.63.refs_0_, ...), custom_call_target="tpu_custom_call" | custom-call | tf_op jit(solution)/shard_map/widen/pallas_call | solution.py:1803
